TPU v7x, 256 devices: a whole 4x4x8 slice. The times are simulated.
256 devices in a mesh: dp: 16 (over z, y_hi), seq: 16 (over x, y_lo, core).
Axes of the slice: x: 4, y: 4 (y_hi: 2, y_lo: 2; y = y_hi * 2 + y_lo), z: 8, core: 2. Of those that a mesh axis runs over, the one named last changes fastest.
Arguments:
- tokens: bfloat16 [16, 4096, 768], P('dp', 'seq'), may hold values from -6 to 6
- cotangent: bfloat16 [16, 4096, 768], P('dp', 'seq'), may hold values from -6 to 6
- w_conv: bfloat16 [3, 768, 512], P(None, ('dp', 'seq')), may hold values from -0.125 to 0.125
- w_point: bfloat16 [512, 768], P(('dp', 'seq')), may hold values from -0.25 to 0.25
Outputs:
- output: bfloat16 [16, 4096, 768], P('dp', 'seq')
- grad_tokens: bfloat16 [16, 4096, 768], P('dp', 'seq')
- grad_conv: float32 [768, 3, 512], P(('dp', 'seq'))
- grad_point: float32 [512, 768], P(('dp', 'seq'))
All inputs are finite; a program needn't handle non-finite values.
Results may differ from a plain program's by a relative error of at most 0.0052.
Values may be sent and summed in bfloat16 or wider, within the bound.
No kernel may reach another device: no remote copies, remote signals or barrier semaphores. Data moves between devices by JAX's collectives and lax.ppermute only.
A program may use at most 64 MiB of HBM per device.

v0:
```python
import jax
import jax.numpy as jnp
from jax import lax
from jax.sharding import PartitionSpec as P


def from_behind(value, axis, steps):
    count = lax.axis_size(axis)
    first, last = (max(0, -steps), min(count, count - steps))
    return lax.ppermute(value, axis, [(source, source + steps) for source in range(first, last)])


def gelu_tanh(values):
    return jax.nn.gelu(values, approximate=True)


def rows_product(left, right):
    return jnp.dot(left, right, preferred_element_type=jnp.float32)


def contract_rows(left, right):
    return lax.dot_general(
        left, right, (((0,), (0,)), ((), ())), preferred_element_type=jnp.float32
    )


def times_transpose(left, right):
    return lax.dot_general(
        left, right, (((1,), (1,)), ((), ())), preferred_element_type=jnp.float32
    )


def shards(tokens, cotangent, w_conv, w_point):
    offset_devices = lax.axis_size("seq") // 4
    conv_full, point_full = (
        lax.all_gather(w_conv, ("dp", "seq"), axis=1, tiled=True),
        lax.all_gather(w_point, ("dp", "seq"), axis=0, tiled=True),
    )
    tokens_wide = tokens[0].astype(jnp.float32)
    grad_out = cotangent[0]
    activated = gelu_tanh(tokens_wide).astype(jnp.bfloat16)
    before = from_behind(activated, "seq", offset_devices)
    after = from_behind(activated, "seq", -offset_devices)
    conv_out = (
        rows_product(activated, conv_full[1])
        + rows_product(before, conv_full[0])
        + rows_product(after, conv_full[2])
    )
    inner_act = gelu_tanh(conv_out).astype(jnp.bfloat16)
    output = (tokens_wide + rows_product(inner_act, point_full)).astype(jnp.bfloat16)
    grad_point = contract_rows(inner_act, grad_out)
    grad_pre = times_transpose(grad_out, point_full)
    grad_inner = jax.vjp(gelu_tanh, conv_out)[1](grad_pre)[0].astype(jnp.bfloat16)
    grad_conv = jnp.stack(
        [
            contract_rows(before, grad_inner),
            contract_rows(activated, grad_inner),
            contract_rows(after, grad_inner),
        ],
        axis=1,
    )
    grad_later = from_behind(grad_inner, "seq", -offset_devices)
    grad_earlier = from_behind(grad_inner, "seq", offset_devices)
    grad_act = (
        times_transpose(grad_inner, conv_full[1])
        + times_transpose(grad_later, conv_full[0])
        + times_transpose(grad_earlier, conv_full[2])
    )
    grad_tokens = (
        grad_out.astype(jnp.float32) + jax.vjp(gelu_tanh, tokens_wide)[1](grad_act)[0]
    ).astype(jnp.bfloat16)
    conv_share, point_share = (
        lax.psum_scatter(grad_conv, ("dp", "seq"), scatter_dimension=0, tiled=True),
        lax.psum_scatter(grad_point, ("dp", "seq"), scatter_dimension=0, tiled=True),
    )
    return (output[None], grad_tokens[None], conv_share, point_share)


def solution(mesh):
    return jax.shard_map(
        shards,
        mesh=mesh,
        in_specs=(
            P("dp", "seq", None),
            P("dp", "seq", None),
            P(None, ("dp", "seq"), None),
            P(("dp", "seq"), None),
        ),
        out_specs=(
            P("dp", "seq", None),
            P("dp", "seq", None),
            P(("dp", "seq"), None, None),
            P(("dp", "seq"), None),
        ),
        check_vma=False,
    )
```

profile of v0, /device:TPU:1, one launch (start us, length us, event | category | flops | bytes accessed | tf_op | source)
XLA Modules:
  0.0 725.7 jit_solution(1338136062553876485)
XLA Ops:
  7.2 1.3 copy.11
  8.6 2.0 fusion.16
  10.6 4.0 collective-permute-start
  14.6 1.3 collective-permute-start.1
  15.9 354.1 %all-gather = bf16[256,2,768]{2,1,0:T(2,128)(2,1)S(1)} all-gather(bf16[1,2,768]{2,1,0:T(2,128)(2,1)} %bitcast.99), channel_id=1, replica_groups=mesh['dp'=16,'seq'=16] {'dp','seq'}, dimensions={0}, use_global_device_ids=true | all-gather | bytes 789504 | tf_op jit(solution)/shard_map/all_gather | solution.py:37
  370.0 1.2 reshape.13
  371.2 55.2 %all-gather.3.cloned.1.call-done = bf16[3,768,512]{2,0,1:T(4,128)(2,1)} async-done(((bf16[3,3,512]{2,0,1:T(4,128)(2,1)}), bf16[3,768,512]{2,0,1:T(4,128)(2,1)}) %all-gather.3.cloned.1.call-update) | async-done | bytes 2359312 | tf_op jit(solution)/shard_map/all_gather | solution.py:36
  426.4 8.0 %fusion.52 = (bf16[1,768,512]{2,0,1:T(2,128)(2,1)S(1)}, bf16[1,768,512]{2,0,1:T(2,128)(2,1)S(1)}, bf16[1,768,512]{2,0,1:T(2,128)(2,1)S(1)}) fusion(bf16[3,768,512]{2,0,1:T(4,128)(2,1)} %all-gather.3.cloned.1.call-done), kind=kLoop, calls=%fused_computation.69 | loop fusion | bytes 4718592 | tf_op jit(solution)/shard_map/slice | solution.py:47
  434.4 0.5 fusion.34
  435.5 1.4 convolution_add_fusion.2
  436.9 1.7 fusion.36
  438.6 0.6 fusion.32
  439.3 0.6 convolution_bitcast_fusion.1
  439.8 1.4 convolution_bitcast_fusion
  441.7 2.7 pad_maximum_fusion
  444.4 1.3 collective-permute-start.2
  445.7 4.0 collective-permute-start.3
  449.7 2.6 fusion.7
  453.2 1.1 copy-done.1
  454.7 1.5 fusion.25
  456.2 259.8 %all-reduce.5.cloned.1.call-done = (f32[768,3,512]{2,0,1:T(8,128)}, f32[512,768]{1,0:T(8,128)}) async-done(((f32[768,3,512]{2,0,1:T(8,128)}, f32[512,768]{1,0:T(8,128)}), (f32[768,3,512]{2,0,1:T(8,128)}, f32[512,768]{1,0:T(8,128)})) %all-reduce.5.cloned.1.call-update) | async-done | bytes 6291472
  716.0 0.9 constant_dynamic-slice_fusion.1
  717.0 0.6 copy.15
  717.6 1.3 constant_dynamic-slice_fusion
  (31 shorter events, 2.4 us)
Async XLA Ops:
  7.2 419.2 %all-gather.3.cloned.1.call-start = ((), (), s32[]{:S(2)}) async-start(), calls=%async_computation | async-start | bytes 3158016 | tf_op jit(solution)/shard_map/all_gather | solution.py:36
  8.5 707.5 %all-reduce.5.cloned.1.call-start = ((), (), s32[]{:S(2)}) async-start(), calls=%async_computation.1 | async-start | bytes 12582912
  10.6 424.3 %collective-permute-start = (bf16[256,768]{1,0:T(8,128)(2,1)}, bf16[256,768]{1,0:T(8,128)(2,1)S(1)}, u32[]{:S(2)}, u32[]{:S(2)}) collective-permute-start(bf16[256,768]{1,0:T(8,128)(2,1)} %fusion.16), channel_id=1, source_target_pairs={{0,4},{1,5},{2,6},{3,7},{4,8},{5,9},{6,10},{7,11},{8,12},{9,13},{1... | collective-permute-start | bytes 1179656 | tf_op jit(solution)/shard_map/ppermute | solution.py:10
  14.6 420.7 %collective-permute-start.1 = (bf16[256,768]{1,0:T(8,128)(2,1)}, bf16[256,768]{1,0:T(8,128)(2,1)}, u32[]{:S(2)}, u32[]{:S(2)}) collective-permute-start(bf16[256,768]{1,0:T(8,128)(2,1)} %fusion.16), channel_id=1, source_target_pairs={{4,0},{5,1},{6,2},{7,3},{8,4},{9,5},{10,6},{11,7},{12,8},{13,9},{1... | collective-permute-start | bytes 1179656 | tf_op jit(solution)/shard_map/ppermute | solution.py:10
  426.4 8.0 %copy-start.8 = (bf16[1,256,768]{2,1,0:T(8,128)(2,1)S(1)}, bf16[1,256,768]{2,1,0:T(8,128)(2,1)}, u32[]{:S(2)}) copy-start(bf16[1,256,768]{2,1,0:T(8,128)(2,1)} %param.4) | copy-start | bytes 1179652
  434.4 1.1 copy-start
  434.9 2.0 copy-start.3
  435.3 1.6 copy-start.6
  436.9 2.4 copy-start.2
  436.9 1.7 copy-start.5
  439.8 1.4 copy-start.4
  444.4 8.4 %collective-permute-start.2 = (bf16[256,512]{1,0:T(8,128)(2,1)S(1)}, bf16[256,512]{1,0:T(8,128)(2,1)S(1)}, u32[]{:S(2)}, u32[]{:S(2)}) collective-permute-start(bf16[256,512]{1,0:T(8,128)(2,1)S(1)} %fusion.32), channel_id=1, source_target_pairs={{4,0},{5,1},{6,2},{7,3},{8,4},{9,5},{10,6},{11,7},{12,8},{13,9},{1... | collective-permute-start | bytes 786440 | tf_op jit(solution)/shard_map/ppermute | solution.py:10
  445.7 7.5 %collective-permute-start.3 = (bf16[256,512]{1,0:T(8,128)(2,1)S(1)}, bf16[256,512]{1,0:T(8,128)(2,1)S(1)}, u32[]{:S(2)}, u32[]{:S(2)}) collective-permute-start(bf16[256,512]{1,0:T(8,128)(2,1)S(1)} %fusion.32), channel_id=1, source_target_pairs={{0,4},{1,5},{2,6},{3,7},{4,8},{5,9},{6,10},{7,11},{8,12},{9,13},{1... | collective-permute-start | bytes 786440 | tf_op jit(solution)/shard_map/ppermute | solution.py:10
  452.7 1.5 copy-start.1
  452.7 1.7 copy-start.7
  452.7 1.9 copy-start.9
Sparse Core Ops, SparseCore 0:
  10.5 415.8 all-gather.2
  444.5 271.4 all-reduce.4
where the time goes:
time: 727 us; the launch traced here: 726 us
  blocking collectives  354 us (49%)
  waiting for transfers between devices  315 us (43%)
  local copies, waits for them, and re-layouts  15 us (2%)
  between operations  14.3 us (2%)
  matrix products  11.9 us (2%)
  starting transfers between devices  10.6 us (1%)
    all_gather x1, blocking collectives, shards(): lax.all_gather(w_point, ('dp', 'seq'), axis=0, tiled=True)  354 us
    unnamed x3, waiting for transfers between devices  260 us
    all_gather x1, waiting for transfers between devices, shards(): lax.all_gather(w_conv, ('dp', 'seq'), axis=1, tiled=True)  55.2 us
  transfers between devices with their start and end apart: 6, of which 2 were waited for; matrix products, arithmetic and copies ran while one was open for 2% of the time, Pallas kernels for 0%

commit v1 on v0

v1 whole, which is shorter than its diff:
```python
import numpy as np
import jax
import jax.numpy as jnp
from jax import lax
from jax.sharding import Mesh, PartitionSpec as P

NZ, NYH, NX, NYL, NC = 8, 2, 4, 2, 2
AXES = ("z", "yh", "x", "yl", "core")
PLANE = ("yh", "x", "yl")
LINE = ("z", "core")
BF16 = jnp.bfloat16
F32 = jnp.float32


def one_hot_rows(source):
    source = np.asarray(source).reshape(-1)
    matrix = np.zeros((source.size, source.size), np.float32)
    matrix[np.arange(source.size), source] = 1.0
    return matrix


def spread_order():
    rows = np.zeros((NX, 192), np.int64)
    for x in range(NX):
        for t in range(3):
            for zc in range(16):
                for r in range(3):
                    rows[x, t * 48 + zc * 3 + r] = zc * 48 + x * 9 + t * 3 + r
        for j in range(6):
            for z2 in range(2):
                for core in range(2):
                    for r in range(2):
                        zc = (2 * x + z2) * 2 + core
                        rows[x, 144 + j * 8 + z2 * 4 + core * 2 + r] = zc * 48 + 36 + r * 6 + j
    return one_hot_rows(rows)


def channel_order():
    rows = np.zeros((NZ, NYH, NX, NYL, NC, 3), np.int64)
    for z, yh, x, yl, core, r in np.ndindex(*rows.shape):
        rows[z, yh, x, yl, core, r] = ((yh * 4 + x) * 2 + yl) * 48 + (z * 2 + core) * 3 + r
    return one_hot_rows(rows)


def inner_order():
    rows = np.zeros((6, 2, NYH, NX, NYL, NC, 2), np.int64)
    for j, z2, yh, x, yl, core, r in np.ndindex(*rows.shape):
        rows[j, z2, yh, x, yl, core, r] = ((yh * 4 + x) * 2 + yl) * 48 + j * 8 + z2 * 4 + core * 2 + r
    return one_hot_rows(rows)


def step_along_x(value, step):
    return lax.ppermute(value, "x", [(i, (i + step) % NX) for i in range(NX)])


def gelu_tanh(values):
    return jax.nn.gelu(values, approximate=True)


def dot(left, right, left_dim, right_dim):
    return lax.dot_general(
        left, right, (((left_dim,), (right_dim,)), ((), ())), preferred_element_type=F32
    )


def shards(tokens, cotangent, w_conv, w_point):
    me = lax.axis_index("x")
    spread = jnp.asarray(spread_order(), BF16)
    channels = jnp.asarray(channel_order(), BF16)
    inner = jnp.asarray(inner_order(), BF16)

    own = jnp.concatenate(
        [
            w_conv.reshape(3, 3, NX, 128).transpose(2, 0, 1, 3).reshape(36, 128),
            w_point.reshape(12, 128),
        ],
        axis=0,
    )
    line = lax.all_to_all(jnp.broadcast_to(own, (16, 48, 128)), LINE, 0, 0)
    blocks = dot(spread, line.reshape(768, 128), 1, 0).astype(BF16).reshape(NX, 192, 128)

    tokens_wide = tokens[0].astype(F32)
    pair = jnp.stack([gelu_tanh(tokens_wide).astype(BF16), cotangent[0]])
    from_left = step_along_x(pair, 1)
    from_right = step_along_x(pair, -1)
    far_top = step_along_x(from_left[:, :128], 1)
    far_bottom = step_along_x(from_right[:, 128:], -1)
    far = jnp.concatenate([far_top, far_bottom], axis=1)
    both = jnp.concatenate([pair, from_right, far, from_left], axis=1)
    act, grad_out = both[0], both[1]

    plane = lax.all_to_all(
        jnp.broadcast_to(blocks[None, :, None], (NYH, NX, NYL, 192, 128)).reshape(16, 192, 128),
        PLANE, 0, 0,
    )
    conv_rows = jnp.concatenate(
        [plane[:, t * 48:(t + 1) * 48].reshape(768, 128) for t in range(3)], axis=1
    )
    conv_w = dot(channels, conv_rows, 1, 0).astype(BF16)
    point_w = dot(inner, plane[:, 144:].reshape(768, 128), 1, 0).astype(BF16)
    point_w = point_w.reshape(6, 128, 128).transpose(1, 0, 2).reshape(128, 768)

    taps = dot(act, conv_w, 1, 0).reshape(4, 256, 384)
    place = [(me + r) % NX for r in range(NX)]
    has_before = [p != 0 for p in place]
    has_after = [p != NX - 1 for p in place]
    conv_out = jnp.concatenate(
        [
            taps[r, :, 128:256]
            + jnp.where(has_before[r], taps[(r - 1) % NX, :, :128], 0.0)
            + jnp.where(has_after[r], taps[(r + 1) % NX, :, 256:], 0.0)
            for r in range(NX)
        ],
        axis=0,
    )
    grad_pre = dot(grad_out, point_w, 1, 1)
    inner_wide, pull = jax.vjp(gelu_tanh, conv_out)
    inner_act = inner_wide.astype(BF16)
    grad_inner = pull(grad_pre)[0].astype(BF16).reshape(4, 256, 128)
    zero = jnp.zeros((), BF16)
    spread_grad = jnp.concatenate(
        [
            jnp.concatenate(
                [
                    jnp.where(has_after[r], grad_inner[(r + 1) % NX], zero),
                    grad_inner[r],
                    jnp.where(has_before[r], grad_inner[(r - 1) % NX], zero),
                ],
                axis=1,
            )
            for r in range(NX)
        ],
        axis=0,
    )
    conv_g = dot(act, spread_grad, 0, 0).astype(BF16)
    point_g = dot(inner_act, grad_out, 0, 0).astype(BF16)
    conv_g = dot(channels, conv_g, 0, 0).astype(BF16).reshape(16, 48, 384)
    point_g = dot(inner, point_g.reshape(128, 6, 128).transpose(1, 0, 2).reshape(768, 128), 0, 0)
    grads = jnp.concatenate(
        [conv_g[:, :, :128], conv_g[:, :, 128:256], conv_g[:, :, 256:],
         point_g.astype(BF16).reshape(16, 48, 128)],
        axis=1,
    )
    plane_g = lax.all_to_all(grads, PLANE, 0, 0)

    out_part = dot(inner_act, point_w, 1, 0).reshape(4, 256, 768)
    act_part = dot(spread_grad, conv_w, 1, 1).reshape(4, 256, 768)
    parts = jnp.stack([out_part, act_part], axis=1)
    top = step_along_x(parts[2, :, :128].astype(BF16), 1).astype(F32)
    bottom = step_along_x(parts[2, :, 128:].astype(BF16), -1).astype(F32)
    to_right = jnp.concatenate([parts[1, :, :128] + top, parts[1, :, 128:]], axis=1)
    to_left = jnp.concatenate([parts[3, :, :128], parts[3, :, 128:] + bottom], axis=1)
    got_left = step_along_x(to_right.astype(BF16), 1).astype(F32)
    got_right = step_along_x(to_left.astype(BF16), -1).astype(F32)
    total = parts[0] + got_left + got_right
    output = (tokens_wide + total[0]).astype(BF16)
    grad_tokens = (
        cotangent[0].astype(F32) + jax.vjp(gelu_tanh, tokens_wide)[1](total[1])[0]
    ).astype(BF16)

    plane_sum = plane_g.astype(F32).reshape(NYH, NX, NYL, 192, 128).sum(axis=(0, 2))
    line_g = dot(spread, plane_sum.astype(BF16).reshape(768, 128), 0, 0).astype(BF16)
    line_g = lax.all_to_all(line_g.reshape(16, 48, 128), LINE, 0, 0)
    share = line_g.astype(F32).sum(axis=0)
    conv_share = share[:36].reshape(NX, 3, 3, 128).transpose(2, 1, 0, 3).reshape(3, 3, 512)
    point_share = share[36:].reshape(2, 768)
    return (output[None], grad_tokens[None], conv_share, point_share)


def solution(mesh):
    fine = Mesh(mesh.devices.reshape(NZ, NYH, NX, NYL, NC), AXES)
    dp, seq = ("z", "yh"), ("x", "yl", "core")
    rows = P(dp, seq, None)
    return jax.shard_map(
        shards,
        mesh=fine,
        in_specs=(rows, rows, P(None, AXES, None), P(AXES, None)),
        out_specs=(rows, rows, P(AXES, None, None), P(AXES, None)),
        check_vma=False,
    )
```

time: 727 us -> 132 us (0.18)
  blocking collectives: 354 us -> 21.8 us
  waiting for transfers between devices: 315 us -> 17.8 us
  starting transfers between devices: 10.6 us -> 30.6 us
  between operations: 14.3 us -> 0.98 us
  other arithmetic: 4.72 us -> 15.4 us
  local copies, waits for them, and re-layouts: 15 us -> 24.6 us
  matrix products: 11.9 us -> 19.8 us
    all_gather x1 -> x0, blocking collectives: 354 us -> none  [shards(): lax.all_gather(w_point, ('dp', 'seq'), axis=0, tiled=True)]
    unnamed x3 -> x0, waiting for transfers between devices: 260 us -> none
    all_gather x1 -> x0, waiting for transfers between devices: 55.2 us -> none  [shards(): lax.all_gather(w_conv, ('dp', 'seq'), axis=1, tiled=True)]
    all_to_all x0 -> x1, blocking collectives: none -> 21.8 us  [shards(): line_g = lax.all_to_all(line_g.reshape(16, 48, 128), LINE, 0, 0)]
    all_to_all x0 -> x3, starting transfers between devices: none -> 21.2 us  [the longest x1 9.98 us: shards(): line = lax.all_to_all(jnp.broadcast_to(own, (16, 48, 128)), LINE, 0, 0)]
    all_to_all x0 -> x3, waiting for transfers between devices: none -> 16.4 us  [the longest x1 5.77 us: shards(): lax.all_to_all(jnp.broadcast_to(blocks[None, :, None], (NYH, NX, NYL, 192...]
    dot_general x12 -> x11, matrix products: 11.9 us -> 19.8 us  [dot(): lax.dot_general(left, right, (((left_dim,), (right_dim,)), ((), ())), pre...]
  transfers between devices with their start and end apart: 6 -> 11, of which waited for: 2 -> 4; matrix products, arithmetic and copies ran while one was open for 2% -> 26% of each run, Pallas kernels for 0% -> 0%
where the time goes in v1:
time: 132 us; the launch traced here: 131 us
  starting transfers between devices  30.6 us (23%)
  local copies, waits for them, and re-layouts  24.6 us (19%)
  blocking collectives  21.8 us (17%)
  matrix products  19.8 us (15%)
  waiting for transfers between devices  17.8 us (13%)
  other arithmetic  15.4 us (12%)
    all_to_all x1, blocking collectives, shards(): line_g = lax.all_to_all(line_g.reshape(16, 48, 128), LINE, 0, 0)  21.8 us
    dot_general x11, matrix products, dot(): lax.dot_general(left, right, (((left_dim,), (right_dim,)), ((), ())), pre...  19.8 us
    all_to_all x1, starting transfers between devices, shards(): line = lax.all_to_all(jnp.broadcast_to(own, (16, 48, 128)), LINE, 0, 0)  9.98 us
    ppermute x8, starting transfers between devices, step_along_x(): return lax.ppermute(value, 'x', [(i, (i + step) % NX) for i in range(NX)])  9.37 us
    all_to_all x1, starting transfers between devices, shards(): lax.all_to_all(jnp.broadcast_to(blocks[None, :, None], (NYH, NX, NYL, 192...  6.8 us
    all_to_all x1, waiting for transfers between devices, shards(): lax.all_to_all(jnp.broadcast_to(blocks[None, :, None], (NYH, NX, NYL, 192...  5.77 us
    all_to_all x1, waiting for transfers between devices, shards(): line = lax.all_to_all(jnp.broadcast_to(own, (16, 48, 128)), LINE, 0, 0)  5.67 us
    unnamed x25, local copies, waits for them, and re-layouts  4.99 us
  transfers between devices with their start and end apart: 11, of which 4 were waited for; matrix products, arithmetic and copies ran while one was open for 26% of the time, Pallas kernels for 0%

profile of v1, /device:TPU:1, one launch (start us, length us, event | category | flops | bytes accessed | tf_op | source)
XLA Modules:
  0.0 131.0 jit_solution(7609985411217584199)
XLA Ops:
  2.9 10.0 %all-to-all-start = ((bf16[16,48,128]{2,1,0:T(8,128)(2,1)}), bf16[16,48,128]{2,1,0:T(8,128)(2,1)}, u32[]{:S(2)}, u32[]{:S(2)}) async-start(bf16[16,48,128]{2,1,0:T(8,128)(2,1)} %broadcast_in_dim.34), calls=%async_computation | async-start | bytes 393216 | tf_op jit(solution)/shard_map/all_to_all | solution.py:79
  15.1 2.5 %collective-permute-start = (bf16[2,256,768]{2,1,0:T(8,128)(2,1)}, bf16[2,256,768]{2,1,0:T(8,128)(2,1)}, u32[]{:S(2)}, u32[]{:S(2)}) collective-permute-start(bf16[2,256,768]{2,1,0:T(8,128)(2,1)} %get-tuple-element.13), channel_id=1, source_target_pairs={{0,12},{4,0},{8,4},{12,8},{1,13},{5,1},{9,5},{13,9},{2,14},{6,2},{... | collective-permute-start | bytes 2359304 | tf_op jit(solution)/shard_map/ppermute | solution.py:53
  17.6 5.7 %all-to-all-done = bf16[16,48,128]{2,1,0:T(8,128)(2,1)} async-done(((bf16[16,48,128]{2,1,0:T(8,128)(2,1)}), bf16[16,48,128]{2,1,0:T(8,128)(2,1)}, u32[]{:S(2)}, u32[]{:S(2)}) %all-to-all-start) | async-done | bytes 196640 | tf_op jit(solution)/shard_map/all_to_all | solution.py:79
  23.3 1.9 %fusion.11 = bf16[768,128]{0,1:T(8,128)(2,1)S(1)} fusion(bf16[768,128]{1,0:T(8,128)(2,1)} %bitcast.2, bf16[768,768]{1,0:T(8,128)(2,1)} %constant.64.clone), kind=kOutput, calls=%fused_computation.27 | convolution fusion | flops 151093248 | bytes 1572864 | tf_op jit(solution)/shard_map/dot_general | solution.py:61
  26.4 6.8 %all-to-all-start.1 = ((bf16[16,192,128]{2,1,0:T(8,128)(2,1)}), bf16[16,192,128]{2,1,0:T(8,128)(2,1)}, u32[]{:S(2)}, u32[]{:S(2)}) async-start(bf16[16,192,128]{2,1,0:T(8,128)(2,1)} %bitcast.110), calls=%async_computation.1 | async-start | bytes 1572864 | tf_op jit(solution)/shard_map/all_to_all | solution.py:92
  34.7 1.8 %slice.169 = bf16[2,128,768]{2,1,0:T(8,128)(2,1)} slice(bf16[2,256,768]{2,1,0:T(8,128)(2,1)} %collective-permute-done), slice={[0:2], [128:256], [0:768]} | slice | bytes 786432 | tf_op jit(solution)/shard_map/slice | solution.py:87
  36.5 3.4 %collective-permute-start.3 = (bf16[2,128,768]{2,1,0:T(8,128)(2,1)}, bf16[2,128,768]{2,1,0:T(8,128)(2,1)}, u32[]{:S(2)}, u32[]{:S(2)}) collective-permute-start(bf16[2,128,768]{2,1,0:T(8,128)(2,1)} %slice.169), channel_id=1, source_target_pairs={{0,12},{4,0},{8,4},{12,8},{1,13},{5,1},{9,5},{13,9},{2,14},{6,2},{... | collective-permute-start | bytes 1179656 | tf_op jit(solution)/shard_map/ppermute | solution.py:53
  39.9 1.8 %slice.168 = bf16[2,128,768]{2,1,0:T(8,128)(2,1)} slice(bf16[2,256,768]{2,1,0:T(8,128)(2,1)} %collective-permute-done.1), slice={[0:2], [0:128], [0:768]} | slice | bytes 786432 | tf_op jit(solution)/shard_map/slice | solution.py:86
  42.9 5.8 %all-to-all-done.1 = bf16[16,192,128]{2,1,0:T(8,128)(2,1)} async-done(((bf16[16,192,128]{2,1,0:T(8,128)(2,1)}), bf16[16,192,128]{2,1,0:T(8,128)(2,1)}, u32[]{:S(2)}, u32[]{:S(2)}) %all-to-all-start.1) | async-done | bytes 786464 | tf_op jit(solution)/shard_map/all_to_all | solution.py:92
  48.6 2.1 %fusion.65 = (bf16[16,48,128]{2,1,0:T(8,128)(2,1)S(1)}, bf16[16,48,128]{2,1,0:T(8,128)(2,1)}, bf16[16,48,128]{2,1,0:T(8,128)(2,1)}, bf16[16,48,128]{2,1,0:T(8,128)(2,1)}) fusion(bf16[16,192,128]{2,1,0:T(8,128)(2,1)} %all-to-all-done.1), kind=kLoop, calls=%fused_computation.117 | loop fusion | bytes 1572864 | tf_op jit(solution)/shard_map/slice | solution.py:100
  52.3 2.2 %convolution_convert_fusion.1 = bf16[384,768]{1,0:T(8,128)(2,1)S(1)} fusion(bf16[768,768]{1,0:T(8,128)(2,1)} %constant.65.clone, bf16[768,128]{1,0:T(8,128)(2,1)} %bitcast.121, bf16[768,128]{1,0:T(8,128)(2,1)} %bitcast.122, bf16[768,128]{1,0:T(8,128)(2,1)} %bitcast.123), kind=kOutput, calls=%fused_computation.20 | convolution fusion | flops 455049216 | bytes 2359296 | tf_op jit(solution)/shard_map/dot_general | solution.py:61
  61.6 4.1 %fusion.9 = bf16[768,384]{0,1:T(8,128)(2,1)} fusion(bf16[768,768]{1,0:T(8,128)(2,1)} %constant.65.clone, bf16[2,1024,768]{2,1,0:T(8,128)(2,1)S(1)} %constant_dynamic-update-slice_fusion, bf16[256,128]{1,0:T(8,128)(2,1)} %get-tuple-element.29, bf16[256,128]{1,0:T(8,128)(2,1)} %get-tuple-element.31, bf16[256,128]{1,0:T(8,128)(2,1)} %get-tuple-element.25, ...), kind=kOutput, calls=%fused_computation.21 | convolution fusion | flops 1066991616 | bytes 4128768 | tf_op jit(solution)/shard_map/dot_general | solution.py:61
  65.7 4.0 %fusion.64 = f32[1024,768]{1,0:T(8,128)} fusion(bf16[384,768]{1,0:T(8,128)(2,1)} %copy-done.10, bf16[256,128]{1,0:T(8,128)(2,1)} %get-tuple-element.29, bf16[256,128]{1,0:T(8,128)(2,1)} %get-tuple-element.31, bf16[256,128]{1,0:T(8,128)(2,1)} %get-tuple-element.25, bf16[256,128]{1,0:T(8,128)(2,1)} %get-tuple-element.23, ...), kind=kOutput, calls=%fused_computation.116 | convolution fusion | flops 613416960 | bytes 4521984 | tf_op jit(solution)/shard_map/dot_general | solution.py:61
  70.8 1.8 %reshape.154 = bf16[768,128]{1,0:T(8,128)(2,1)} reshape(bf16[128,768]{1,0:T(8,128)(2,1)} %fusion.10) | data formatting | bytes 393216 | tf_op jit(solution)/shard_map/dot_general | solution.py:61
  72.6 1.6 %convolution_bitcast_fusion = f32[4,1,256,768]{3,2,0,1:T(8,128)S(1)} fusion(bf16[4,256,128]{2,1,0:T(8,128)(2,1)S(1)} %bitcast.112, bf16[128,768,1]{0,1,2:T(8,128)(2,1)} %bitcast.113), kind=kOutput, calls=%fused_computation.3 | convolution fusion | flops 201326592 | bytes 3604480 | tf_op jit(solution)/shard_map/dot_general | solution.py:61
  77.3 1.7 %copy.43 = bf16[768,128]{1,0:T(8,128)(2,1)} copy(bf16[768,128]{0,1:T(8,128)(2,1)} %fusion.13) | data formatting | bytes 393216 | tf_op jit(solution)/shard_map/convert_element_type | solution.py:141
  79.1 2.1 %copy.42 = bf16[768,384]{1,0:T(8,128)(2,1)} copy(bf16[768,384]{0,1:T(8,128)(2,1)} %fusion.9) | data formatting | bytes 1179648 | tf_op jit(solution)/shard_map/convert_element_type | solution.py:137
  83.2 1.9 %pad_maximum_fusion.4 = bf16[16,192,128]{2,1,0:T(8,128)(2,1)} fusion(bf16[16,48,128]{2,1,0:T(8,128)(2,1)} %bitcast.117, bf16[16,48,128]{2,1,0:T(8,128)(2,1)S(1)} %get-tuple-element.20, bf16[16,48,128]{2,1,0:T(8,128)(2,1)S(1)} %get-tuple-element.21, bf16[16,48,128]{2,1,0:T(8,128)(2,1)S(1)} %get-tuple-element.19), kind=kLoop, calls=%fused_computation.54 | loop fusion | flops 3145728 | bytes 1572864 | tf_op jit(solution)/shard_map/concatenate | solution.py:139
  85.1 4.5 %all-to-all-start.2 = ((bf16[16,192,128]{2,1,0:T(8,128)(2,1)}), bf16[16,192,128]{2,1,0:T(8,128)(2,1)}, u32[]{:S(2)}, u32[]{:S(2)}) async-start(bf16[16,192,128]{2,1,0:T(8,128)(2,1)} %pad_maximum_fusion.4), calls=%async_computation.2 | async-start | bytes 1572864 | tf_op jit(solution)/shard_map/all_to_all | solution.py:144
  91.9 2.5 %collective-permute-start.7 = (bf16[2,256,768]{2,1,0:T(8,128)(2,1)}, bf16[2,256,768]{2,1,0:T(8,128)(2,1)}, u32[]{:S(2)}, u32[]{:S(2)}) collective-permute-start(bf16[2,256,768]{2,1,0:T(8,128)(2,1)} %pad_maximum_fusion.3), channel_id=1, source_target_pairs={{0,12},{4,0},{8,4},{12,8},{1,13},{5,1},{9,5},{13,9},{2,14},{6,2},{... | collective-permute-start | bytes 2359304 | tf_op jit(solution)/shard_map/ppermute | solution.py:53
  96.4 4.9 %all-to-all-done.2 = bf16[16,192,128]{2,1,0:T(8,128)(2,1)} async-done(((bf16[16,192,128]{2,1,0:T(8,128)(2,1)}), bf16[16,192,128]{2,1,0:T(8,128)(2,1)}, u32[]{:S(2)}, u32[]{:S(2)}) %all-to-all-start.2) | async-done | bytes 786464 | tf_op jit(solution)/shard_map/all_to_all | solution.py:144
  102.7 1.6 %fusion.14 = bf16[768,128]{0,1:T(8,128)(2,1)S(1)} fusion(bf16[768,128]{1,0:T(8,128)(2,1)S(1)} %bitcast.116, bf16[768,768]{1,0:T(8,128)(2,1)} %constant.64.clone), kind=kOutput, calls=%fused_computation.30 | convolution fusion | flops 151093248 | bytes 1572864 | tf_op jit(solution)/shard_map/dot_general | solution.py:61
  104.5 21.8 %all_to_all.20 = bf16[16,48,128]{2,1,0:T(8,128)(2,1)S(1)} all-to-all(bf16[16,48,128]{2,1,0:T(8,128)(2,1)S(1)} %bitcast.119), channel_id=1, replica_groups=mesh['z'=8,'yh'=2,'x'=4,'yl'=2,'core'=2] {'z','core'}, dimensions={0} | all-to-all | bytes 393216 | tf_op jit(solution)/shard_map/all_to_all | solution.py:163
  127.6 1.9 %fusion.1 = f32[2,256,768]{2,1,0:T(8,128)S(1)} fusion(bf16[2,256,768]{2,1,0:T(8,128)(2,1)} %collective-permute-done.7, bf16[2,256,768]{2,1,0:T(8,128)(2,1)} %collective-permute-done.5, f32[4,1,256,768]{3,2,0,1:T(8,128)} %bitcast.106, f32[4,1,256,768]{3,2,0,1:T(8,128)S(1)} %convolution_bitcast_fusion), kind=kLoop, calls=%fused_computation.12 | loop fusion | flops 3145728 | bytes 9437184 | tf_op jit(solution)/shard_map/add | solution.py:155
  (78 shorter events, 31.6 us)
Async XLA Ops:
  0.6 13.5 %copy-start.2 = (bf16[1,256,768]{2,1,0:T(8,128)(2,1)S(1)}, bf16[1,256,768]{2,1,0:T(8,128)(2,1)}, u32[]{:S(2)}) copy-start(bf16[1,256,768]{2,1,0:T(8,128)(2,1)} %param.8) | copy-start | bytes 1179652
  2.9 20.4 %all-to-all-start = ((bf16[16,48,128]{2,1,0:T(8,128)(2,1)}), bf16[16,48,128]{2,1,0:T(8,128)(2,1)}, u32[]{:S(2)}, u32[]{:S(2)}) async-start(bf16[16,48,128]{2,1,0:T(8,128)(2,1)} %broadcast_in_dim.34), calls=%async_computation | async-start | bytes 393216 | tf_op jit(solution)/shard_map/all_to_all | solution.py:79
  15.1 19.6 %collective-permute-start = (bf16[2,256,768]{2,1,0:T(8,128)(2,1)}, bf16[2,256,768]{2,1,0:T(8,128)(2,1)}, u32[]{:S(2)}, u32[]{:S(2)}) collective-permute-start(bf16[2,256,768]{2,1,0:T(8,128)(2,1)} %get-tuple-element.13), channel_id=1, source_target_pairs={{0,12},{4,0},{8,4},{12,8},{1,13},{5,1},{9,5},{13,9},{2,14},{6,2},{... | collective-permute-start | bytes 2359304 | tf_op jit(solution)/shard_map/ppermute | solution.py:53
  17.6 22.3 %collective-permute-start.1 = (bf16[2,256,768]{2,1,0:T(8,128)(2,1)}, bf16[2,256,768]{2,1,0:T(8,128)(2,1)}, u32[]{:S(2)}, u32[]{:S(2)}) collective-permute-start(bf16[2,256,768]{2,1,0:T(8,128)(2,1)} %get-tuple-element.13), channel_id=1, source_target_pairs={{0,4},{4,8},{8,12},{12,0},{1,5},{5,9},{9,13},{13,1},{2,6},{6,10},{... | collective-permute-start | bytes 2359304 | tf_op jit(solution)/shard_map/ppermute | solution.py:53
  26.4 22.2 %all-to-all-start.1 = ((bf16[16,192,128]{2,1,0:T(8,128)(2,1)}), bf16[16,192,128]{2,1,0:T(8,128)(2,1)}, u32[]{:S(2)}, u32[]{:S(2)}) async-start(bf16[16,192,128]{2,1,0:T(8,128)(2,1)} %bitcast.110), calls=%async_computation.1 | async-start | bytes 1572864 | tf_op jit(solution)/shard_map/all_to_all | solution.py:92
  36.5 19.3 %collective-permute-start.3 = (bf16[2,128,768]{2,1,0:T(8,128)(2,1)}, bf16[2,128,768]{2,1,0:T(8,128)(2,1)}, u32[]{:S(2)}, u32[]{:S(2)}) collective-permute-start(bf16[2,128,768]{2,1,0:T(8,128)(2,1)} %slice.169), channel_id=1, source_target_pairs={{0,12},{4,0},{8,4},{12,8},{1,13},{5,1},{9,5},{13,9},{2,14},{6,2},{... | collective-permute-start | bytes 1179656 | tf_op jit(solution)/shard_map/ppermute | solution.py:53
  41.7 12.9 %collective-permute-start.2 = (bf16[2,128,768]{2,1,0:T(8,128)(2,1)}, bf16[2,128,768]{2,1,0:T(8,128)(2,1)}, u32[]{:S(2)}, u32[]{:S(2)}) collective-permute-start(bf16[2,128,768]{2,1,0:T(8,128)(2,1)} %slice.168), channel_id=1, source_target_pairs={{0,4},{4,8},{8,12},{12,0},{1,5},{5,9},{9,13},{13,1},{2,6},{6,10},{... | collective-permute-start | bytes 1179656 | tf_op jit(solution)/shard_map/ppermute | solution.py:53
  48.6 2.1 %copy-start.7 = (bf16[768,768]{1,0:T(8,128)(2,1)S(1)}, bf16[768,768]{1,0:T(8,128)(2,1)}, u32[]{:S(2)}) copy-start(bf16[768,768]{1,0:T(8,128)(2,1)} %constant.66.clone) | copy-start | bytes 3538948
  54.5 3.6 %copy-start.10 = (bf16[384,768]{1,0:T(8,128)(2,1)}, bf16[384,768]{1,0:T(8,128)(2,1)S(1)}, u32[]{:S(2)}) copy-start(bf16[384,768]{1,0:T(8,128)(2,1)S(1)} %convolution_convert_fusion.1) | copy-start | bytes 1769476
  59.2 0.9 copy-start.8
  72.6 2.0 %copy-start = (f32[1024,768]{1,0:T(8,128)S(1)}, f32[1024,768]{1,0:T(8,128)}, u32[]{:S(2)}) copy-start(f32[1024,768]{1,0:T(8,128)} %fusion.64) | copy-start | bytes 9437188
  74.6 1.7 %copy-start.6 = (bf16[768,768]{1,0:T(8,128)(2,1)S(1)}, bf16[768,768]{1,0:T(8,128)(2,1)}, u32[]{:S(2)}) copy-start(bf16[768,768]{1,0:T(8,128)(2,1)} %constant.73) | copy-start | bytes 3538948
  74.6 1.7 %copy-start.9 = (bf16[768,128]{1,0:T(8,128)(2,1)S(1)}, bf16[768,128]{1,0:T(8,128)(2,1)}, u32[]{:S(2)}) copy-start(bf16[768,128]{1,0:T(8,128)(2,1)} %reshape.154) | copy-start | bytes 589828
  75.7 13.9 %collective-permute-start.6 = (bf16[2,128,768]{2,1,0:T(8,128)(2,1)}, bf16[2,128,768]{2,1,0:T(8,128)(2,1)}, u32[]{:S(2)}, u32[]{:S(2)}) collective-permute-start(bf16[2,128,768]{2,1,0:T(8,128)(2,1)} %get-tuple-element.5), channel_id=1, source_target_pairs={{0,12},{4,0},{8,4},{12,8},{1,13},{5,1},{9,5},{13,9},{2,14},{6,2},{... | collective-permute-start | bytes 1179656 | tf_op jit(solution)/shard_map/ppermute | solution.py:53
  81.2 13.3 %collective-permute-start.4 = (bf16[2,128,768]{2,1,0:T(8,128)(2,1)}, bf16[2,128,768]{2,1,0:T(8,128)(2,1)}, u32[]{:S(2)}, u32[]{:S(2)}) collective-permute-start(bf16[2,128,768]{2,1,0:T(8,128)(2,1)} %get-tuple-element.4), channel_id=1, source_target_pairs={{0,4},{4,8},{8,12},{12,0},{1,5},{5,9},{9,13},{13,1},{2,6},{6,10},{... | collective-permute-start | bytes 1179656 | tf_op jit(solution)/shard_map/ppermute | solution.py:53
  85.1 16.3 %all-to-all-start.2 = ((bf16[16,192,128]{2,1,0:T(8,128)(2,1)}), bf16[16,192,128]{2,1,0:T(8,128)(2,1)}, u32[]{:S(2)}, u32[]{:S(2)}) async-start(bf16[16,192,128]{2,1,0:T(8,128)(2,1)} %pad_maximum_fusion.4), calls=%async_computation.2 | async-start | bytes 1572864 | tf_op jit(solution)/shard_map/all_to_all | solution.py:144
  89.6 1.4 %copy-start.5 = (bf16[2,128,768]{2,1,0:T(8,128)(2,1)S(1)}, bf16[2,128,768]{2,1,0:T(8,128)(2,1)}, u32[]{:S(2)}) copy-start(bf16[2,128,768]{2,1,0:T(8,128)(2,1)} %get-tuple-element.6) | copy-start | bytes 1179652
  89.6 4.9 %copy-start.1 = (f32[1024,768]{1,0:T(8,128)S(1)}, f32[1024,768]{1,0:T(8,128)}, u32[]{:S(2)}) copy-start(f32[1024,768]{1,0:T(8,128)} %fusion.64) | copy-start | bytes 9437188
  91.9 35.7 %collective-permute-start.7 = (bf16[2,256,768]{2,1,0:T(8,128)(2,1)}, bf16[2,256,768]{2,1,0:T(8,128)(2,1)}, u32[]{:S(2)}, u32[]{:S(2)}) collective-permute-start(bf16[2,256,768]{2,1,0:T(8,128)(2,1)} %pad_maximum_fusion.3), channel_id=1, source_target_pairs={{0,12},{4,0},{8,4},{12,8},{1,13},{5,1},{9,5},{13,9},{2,14},{6,2},{... | collective-permute-start | bytes 2359304 | tf_op jit(solution)/shard_map/ppermute | solution.py:53
  96.4 31.1 %collective-permute-start.5 = (bf16[2,256,768]{2,1,0:T(8,128)(2,1)}, bf16[2,256,768]{2,1,0:T(8,128)(2,1)}, u32[]{:S(2)}, u32[]{:S(2)}) collective-permute-start(bf16[2,256,768]{2,1,0:T(8,128)(2,1)} %pad_maximum_fusion.2), channel_id=1, source_target_pairs={{0,4},{4,8},{8,12},{12,0},{1,5},{5,9},{9,13},{13,1},{2,6},{6,10},{... | collective-permute-start | bytes 2359304 | tf_op jit(solution)/shard_map/ppermute | solution.py:53
  127.6 1.9 %copy-start.3 = (bf16[1,256,768]{2,1,0:T(8,128)(2,1)S(1)}, bf16[1,256,768]{2,1,0:T(8,128)(2,1)}, u32[]{:S(2)}) copy-start(bf16[1,256,768]{2,1,0:T(8,128)(2,1)} %param.8) | copy-start | bytes 1179652
  127.6 1.9 %copy-start.4 = (bf16[1,256,768]{2,1,0:T(8,128)(2,1)S(1)}, bf16[1,256,768]{2,1,0:T(8,128)(2,1)}, u32[]{:S(2)}) copy-start(bf16[1,256,768]{2,1,0:T(8,128)(2,1)} %param.7) | copy-start | bytes 1179652

commit v2 on v1

v2 whole, which is shorter than its diff:
```python
import numpy as np
import jax
import jax.numpy as jnp
from jax import lax
from jax.experimental import pallas as pl
from jax.experimental.pallas import tpu as pltpu
from jax.sharding import Mesh, PartitionSpec as P

NZ, NYH, NX, NYL, NC = 8, 2, 4, 2, 2
AXES = ("z", "yh", "x", "yl", "core")
PLANE = ("yh", "x", "yl")
LINE = ("z", "core")
ROWS, D, TAKE = 256, 768, 128
BF16 = jnp.bfloat16
F32 = jnp.float32
SCALE = 0.7978845608028654
CUBIC = 0.044715


def one_hot_rows(source):
    source = np.asarray(source).reshape(-1)
    matrix = np.zeros((source.size, source.size), np.float32)
    matrix[np.arange(source.size), source] = 1.0
    return matrix


def spread_order():
    rows = np.zeros((NX, 192), np.int64)
    for x in range(NX):
        for t in range(3):
            for zc in range(16):
                for r in range(3):
                    rows[x, t * 48 + zc * 3 + r] = zc * 48 + x * 9 + t * 3 + r
        for j in range(6):
            for z2 in range(2):
                for core in range(2):
                    for r in range(2):
                        zc = (2 * x + z2) * 2 + core
                        rows[x, 144 + j * 8 + z2 * 4 + core * 2 + r] = zc * 48 + 36 + r * 6 + j
    return one_hot_rows(rows)


def channel_order():
    rows = np.zeros((NZ, NYH, NX, NYL, NC, 3), np.int64)
    for z, yh, x, yl, core, r in np.ndindex(*rows.shape):
        rows[z, yh, x, yl, core, r] = ((yh * 4 + x) * 2 + yl) * 48 + (z * 2 + core) * 3 + r
    return one_hot_rows(rows)


def inner_order():
    rows = np.zeros((6, 2, NYH, NX, NYL, NC, 2), np.int64)
    for j, z2, yh, x, yl, core, r in np.ndindex(*rows.shape):
        rows[j, z2, yh, x, yl, core, r] = ((yh * 4 + x) * 2 + yl) * 48 + j * 8 + z2 * 4 + core * 2 + r
    return one_hot_rows(rows)


def step_along_x(value, step):
    return lax.ppermute(value, "x", [(i, (i + step) % NX) for i in range(NX)])


def tanh_of(values):
    return jnp.tanh(SCALE * (values + CUBIC * (values * values * values)))


def gelu_tanh(values):
    return values * (0.5 * (1.0 + tanh_of(values)))


def gelu_slope(values):
    t = tanh_of(values)
    return 0.5 * (1.0 + t) + (0.5 * values) * ((1.0 - t * t) * (SCALE * (1.0 + 3.0 * CUBIC * (values * values))))


def dot(left, right, left_dim, right_dim):
    return lax.dot_general(
        left, right, (((left_dim,), (right_dim,)), ((), ())), preferred_element_type=F32
    )


def kernel_call(body, out_shapes, scratch=(), flops=0, moved=0, limit=16):
    many = isinstance(out_shapes, (list, tuple))
    vmem = pl.BlockSpec(memory_space=pltpu.VMEM)

    def call(*operands):
        return pl.pallas_call(
            body,
            out_shape=out_shapes,
            in_specs=[vmem] * len(operands),
            out_specs=[vmem] * len(out_shapes) if many else vmem,
            scratch_shapes=list(scratch),
            compiler_params=pltpu.CompilerParams(vmem_limit_bytes=limit * 2**20),
            cost_estimate=pl.CostEstimate(flops=flops, bytes_accessed=moved, transcendentals=0),
        )(*operands)

    return call


def shape(*dims, dtype=BF16):
    return jax.ShapeDtypeStruct(dims, dtype)


def spread_kernel(line, order, out):
    for x in range(NX):
        block = dot(order[x * 192:(x + 1) * 192, :], line[...], 1, 0).astype(BF16)
        for yh in range(NYH):
            for yl in range(NYL):
                out[(yh * NX + x) * NYL + yl] = block


def middle_kernel(
    act0, act1, act2, act3, ct0, ct1, ct2, ct3, plane, to_d, to_h, from_d, from_h,
    grads, inner_act, spread_grad, conv_w, point_w,
    rows_s, point_s, taps_s, grad_s, sum_s,
):
    acts, cts = (act0, act1, act2, act3), (ct0, ct1, ct2, ct3)
    me = lax.axis_index("x")
    place = [lax.rem(me + r, NX) for r in range(NX)]
    keep_before = [(p != 0).astype(F32) for p in place]
    keep_after = [(p != NX - 1).astype(F32) for p in place]

    for p in range(16):
        at = slice(p * 48, (p + 1) * 48)
        for t in range(3):
            rows_s[at, t * TAKE:(t + 1) * TAKE] = plane[p, t * 48:(t + 1) * 48, :]
        point_s[at, :] = plane[p, 144:192, :]
    for k in range(3):
        at = slice(k * 256, (k + 1) * 256)
        conv_w[at, :] = dot(to_d[at, :], rows_s[...], 1, 0).astype(BF16)
    for j in range(6):
        at = slice(j * TAKE, (j + 1) * TAKE)
        point_w[:, at] = dot(to_h[at, :], point_s[...], 1, 0).astype(BF16)

    for r in range(NX):
        taps_s[r] = dot(acts[r][...], conv_w[...], 1, 0)
    for r in range(NX):
        grad_pre = dot(cts[r][...], point_w[...], 1, 1)
        conv_out = (
            taps_s[r, :, TAKE:2 * TAKE]
            + taps_s[(r - 1) % NX, :, :TAKE] * keep_before[r]
            + taps_s[(r + 1) % NX, :, 2 * TAKE:] * keep_after[r]
        )
        t = tanh_of(conv_out)
        cdf = 0.5 * (1.0 + t)
        inner_act[r] = (conv_out * cdf).astype(BF16)
        slope = cdf + (0.5 * conv_out) * (
            (1.0 - t * t) * (SCALE * (1.0 + 3.0 * CUBIC * (conv_out * conv_out)))
        )
        grad_s[r] = (grad_pre * slope).astype(BF16)
    for r in range(NX):
        spread_grad[r, :, :TAKE] = grad_s[(r + 1) % NX] * keep_after[r].astype(BF16)
        spread_grad[r, :, TAKE:2 * TAKE] = grad_s[r]
        spread_grad[r, :, 2 * TAKE:] = grad_s[(r - 1) % NX] * keep_before[r].astype(BF16)

    for t in range(3):
        at = slice(t * TAKE, (t + 1) * TAKE)
        total = dot(spread_grad[0, :, at], acts[0][...], 0, 0)
        for r in range(1, NX):
            total = total + dot(spread_grad[r, :, at], acts[r][...], 0, 0)
        sum_s[at, :] = total.astype(BF16)
    for p in range(4):
        back = dot(from_d[p * 192:(p + 1) * 192, :], sum_s[...], 1, 1).astype(BF16)
        for k in range(4):
            for t in range(3):
                grads[4 * p + k, t * 48:(t + 1) * 48, :] = back[
                    k * 48:(k + 1) * 48, t * TAKE:(t + 1) * TAKE
                ]
    total = dot(inner_act[0], cts[0][...], 0, 0)
    for r in range(1, NX):
        total = total + dot(inner_act[r], cts[r][...], 0, 0)
    for j in range(6):
        at = slice(j * TAKE, (j + 1) * TAKE)
        point_s[at, :] = total[:, at].astype(BF16)
    for p in range(4):
        back = dot(from_h[p * 192:(p + 1) * 192, :], point_s[...], 1, 0).astype(BF16)
        for k in range(4):
            grads[4 * p + k, 144:192, :] = back[k * 48:(k + 1) * 48, :]


def parts_kernel(inner_act, spread_grad, conv_w, point_w, *outs):
    for r in (2, 1, 3, 0):
        outs[r][...] = dot(inner_act[r], point_w[...], 1, 0).astype(BF16)
        outs[NX + r][...] = dot(spread_grad[r], conv_w[...], 1, 1).astype(BF16)


def line_kernel(plane, order, out, sum_s):
    for x in range(NX):
        total = plane[x * NYL].astype(F32)
        for yh in range(NYH):
            for yl in range(NYL):
                if yh or yl:
                    total = total + plane[(yh * NX + x) * NYL + yl].astype(F32)
        sum_s[x * 192:(x + 1) * 192, :] = total.astype(BF16)
    for k in range(4):
        at = slice(k * 192, (k + 1) * 192)
        out[at, :] = dot(order[at, :], sum_s[...], 1, 0).astype(BF16)


def shards(tokens, cotangent, w_conv, w_point):
    spread, channels, inner = spread_order(), channel_order(), inner_order()

    def constant(matrix):
        return jnp.asarray(matrix, BF16)

    own = jnp.concatenate(
        [
            w_conv.reshape(3, 3, NX, TAKE).transpose(2, 0, 1, 3).reshape(36, TAKE),
            w_point.reshape(12, TAKE),
        ],
        axis=0,
    )
    line = lax.all_to_all(jnp.broadcast_to(own, (16, 48, TAKE)), LINE, 0, 0)
    blocks = kernel_call(
        spread_kernel, shape(16, 192, TAKE), flops=2 * D * D * TAKE, moved=3 * 2**20
    )(line.reshape(D, TAKE), constant(spread))
    plane = lax.all_to_all(blocks, PLANE, 0, 0)

    tokens_wide = tokens[0].astype(F32)
    act = [gelu_tanh(tokens_wide).astype(BF16), None, None, None]
    ct = [cotangent[0], None, None, None]
    act[3], act[1] = step_along_x(act[0], 1), step_along_x(act[0], -1)
    ct[3], ct[1] = step_along_x(ct[0], 1), step_along_x(ct[0], -1)
    act[2] = step_along_x(act[3], 1)
    ct[2] = step_along_x(ct[1], -1)

    grads, inner_act, spread_grad, conv_w, point_w = kernel_call(
        middle_kernel,
        [
            shape(16, 192, TAKE),
            shape(NX, ROWS, TAKE),
            shape(NX, ROWS, 3 * TAKE),
            shape(D, 3 * TAKE),
            shape(TAKE, D),
        ],
        scratch=[
            pltpu.VMEM((D, 3 * TAKE), BF16),
            pltpu.VMEM((D, TAKE), BF16),
            pltpu.VMEM((NX, ROWS, 3 * TAKE), F32),
            pltpu.VMEM((NX, ROWS, TAKE), BF16),
            pltpu.VMEM((3 * TAKE, D), BF16),
        ],
        flops=4 * 10**9,
        moved=12 * 2**20,
        limit=32,
    )(
        *act, *ct, plane,
        constant(channels), constant(inner), constant(channels.T), constant(inner.T),
    )
    plane_g = lax.all_to_all(grads, PLANE, 0, 0)

    parts = kernel_call(
        parts_kernel, [shape(ROWS, D)] * 8, flops=10**9, moved=6 * 2**20
    )(inner_act, spread_grad, conv_w, point_w)
    out_part, act_part = parts[:4], parts[4:]
    out_far = step_along_x(out_part[2], 1)
    act_far = step_along_x(act_part[2], -1)
    out_left = step_along_x(out_part[3], -1)
    act_right = step_along_x(act_part[1], 1)
    out_right = step_along_x((out_part[1].astype(F32) + out_far.astype(F32)).astype(BF16), 1)
    act_left = step_along_x((act_part[3].astype(F32) + act_far.astype(F32)).astype(BF16), -1)
    output = (
        tokens_wide + out_part[0].astype(F32) + out_left.astype(F32) + out_right.astype(F32)
    ).astype(BF16)
    grad_act = act_part[0].astype(F32) + act_left.astype(F32) + act_right.astype(F32)
    grad_tokens = (ct[0].astype(F32) + grad_act * gelu_slope(tokens_wide)).astype(BF16)

    line_g = kernel_call(
        line_kernel, shape(D, TAKE), scratch=[pltpu.VMEM((D, TAKE), BF16)],
        flops=2 * D * D * TAKE, moved=3 * 2**20,
    )(plane_g, constant(spread.T))
    line_g = lax.all_to_all(line_g.reshape(16, 48, TAKE), LINE, 0, 0)
    share = line_g.astype(F32).sum(axis=0)
    conv_share = share[:36].reshape(NX, 3, 3, TAKE).transpose(2, 1, 0, 3).reshape(3, 3, 512)
    point_share = share[36:].reshape(2, D)
    return (output[None], grad_tokens[None], conv_share, point_share)


def solution(mesh):
    fine = Mesh(mesh.devices.reshape(NZ, NYH, NX, NYL, NC), AXES)
    dp, seq = ("z", "yh"), ("x", "yl", "core")
    rows = P(dp, seq, None)
    return jax.shard_map(
        shards,
        mesh=fine,
        in_specs=(rows, rows, P(None, AXES, None), P(AXES, None)),
        out_specs=(rows, rows, P(AXES, None, None), P(AXES, None)),
        check_vma=False,
    )
```

time: 132 us -> 120 us (0.909)
  waiting for transfers between devices: 17.8 us -> 42.2 us
  blocking collectives: 21.8 us -> 0 us
  matrix products: 19.8 us -> 0 us
  starting transfers between devices: 30.6 us -> 43.5 us
  local copies, waits for them, and re-layouts: 24.6 us -> 13.6 us
  Pallas kernels: 0 us -> 10.4 us
  other arithmetic: 15.4 us -> 8.13 us
    ppermute x8 -> x12, waiting for transfers between devices: 1.46 us -> 32.7 us  [step_along_x(): return lax.ppermute(value, 'x', [(i, (i + step) % NX) for i in range(NX)])]
    all_to_all x1 -> x0, blocking collectives: 21.8 us -> none  [shards(): line_g = lax.all_to_all(line_g.reshape(16, 48, 128), LINE, 0, 0)]
    dot_general x11 -> x0, matrix products: 19.8 us -> none  [dot(): lax.dot_general(left, right, (((left_dim,), (right_dim,)), ((), ())), pre...]
    pallas_call x0 -> x4, Pallas kernels: none -> 10.4 us  [call(): pl.pallas_call(body, out_shape=out_shapes, in_specs=[vmem] * len(operands...]
    slice x8 -> x2, local copies, waits for them, and re-layouts: 6.94 us -> 0.01 us  [the longest x1 0.01 us: shards(): point_share = share[36:].reshape(2, D)]
    ppermute x8 -> x12, starting transfers between devices: 9.37 us -> 16 us  [step_along_x(): return lax.ppermute(value, 'x', [(i, (i + step) % NX) for i in range(NX)])]
    all_to_all x2 -> x3, starting transfers between devices: 16.8 us -> 23.4 us  [the longest x1 9.98 us: shards(): line = lax.all_to_all(jnp.broadcast_to(own, (16, 48, TAKE)), LINE, 0, 0)]
    unnamed x25 -> x30, local copies, waits for them, and re-layouts: 4.99 us -> 10.1 us
  transfers between devices with their start and end apart: 11 -> 16, of which waited for: 4 -> 8; matrix products, arithmetic and copies ran while one was open for 26% -> 7% of each run, Pallas kernels for 0% -> 2%
where the time goes in v2:
time: 120 us; the launch traced here: 119 us
  starting transfers between devices  43.5 us (36%)
  waiting for transfers between devices  42.2 us (35%)
  local copies, waits for them, and re-layouts  13.6 us (11%)
  Pallas kernels  10.4 us (9%)
  other arithmetic  8.13 us (7%)
    ppermute x12, waiting for transfers between devices, step_along_x(): return lax.ppermute(value, 'x', [(i, (i + step) % NX) for i in range(NX)])  32.7 us
    ppermute x12, starting transfers between devices, step_along_x(): return lax.ppermute(value, 'x', [(i, (i + step) % NX) for i in range(NX)])  16 us
    pallas_call x4, Pallas kernels, call(): pl.pallas_call(body, out_shape=out_shapes, in_specs=[vmem] * len(operands...  10.4 us
    unnamed x30, local copies, waits for them, and re-layouts  10.1 us
    all_to_all x1, starting transfers between devices, shards(): line = lax.all_to_all(jnp.broadcast_to(own, (16, 48, TAKE)), LINE, 0, 0)  9.98 us
    all_to_all x1, starting transfers between devices, shards(): plane = lax.all_to_all(blocks, PLANE, 0, 0)  6.89 us
    all_to_all x1, starting transfers between devices, shards(): line_g = lax.all_to_all(line_g.reshape(16, 48, TAKE), LINE, 0, 0)  6.56 us
    all_to_all x1, waiting for transfers between devices, shards(): line = lax.all_to_all(jnp.broadcast_to(own, (16, 48, TAKE)), LINE, 0, 0)  6.28 us
  transfers between devices with their start and end apart: 16, of which 8 were waited for; matrix products, arithmetic and copies ran while one was open for 7% of the time, Pallas kernels for 2%

profile of v2, /device:TPU:1, one launch (start us, length us, event | category | flops | bytes accessed | tf_op | source)
XLA Modules:
  0.0 118.6 jit_solution(16516888865333054959)
XLA Ops:
  2.9 10.0 %all-to-all-start = ((bf16[16,48,128]{2,1,0:T(8,128)(2,1)}), bf16[16,48,128]{2,1,0:T(8,128)(2,1)S(1)}, u32[]{:S(2)}, u32[]{:S(2)}) async-start(bf16[16,48,128]{2,1,0:T(8,128)(2,1)} %broadcast_in_dim.9), calls=%async_computation | async-start | bytes 393216 | tf_op jit(solution)/shard_map/all_to_all | solution.py:211
  14.2 1.3 %collective-permute-start.1 = (bf16[256,768]{1,0:T(8,128)(2,1)S(1)}, bf16[256,768]{1,0:T(8,128)(2,1)S(1)}, u32[]{:S(2)}, u32[]{:S(2)}) collective-permute-start(bf16[256,768]{1,0:T(8,128)(2,1)S(1)} %fusion.12.act0), channel_id=1, source_target_pairs={{0,4},{4,8},{8,12},{12,0},{1,5},{5,9},{9,13},{13,1},{2,6},{6,10},{... | collective-permute-start | bytes 1179656 | tf_op jit(solution)/shard_map/ppermute | solution.py:58
  15.5 1.5 %collective-permute-start.3 = (bf16[256,768]{1,0:T(8,128)(2,1)}, bf16[256,768]{1,0:T(8,128)(2,1)S(1)}, u32[]{:S(2)}, u32[]{:S(2)}) collective-permute-start(bf16[256,768]{1,0:T(8,128)(2,1)} %bitcast.20), channel_id=1, source_target_pairs={{0,12},{4,0},{8,4},{12,8},{1,13},{5,1},{9,5},{13,9},{2,14},{6,2},{... | collective-permute-start | bytes 1179656 | tf_op jit(solution)/shard_map/ppermute | solution.py:58
  17.0 6.3 %all-to-all-done = bf16[16,48,128]{2,1,0:T(8,128)(2,1)S(1)} async-done(((bf16[16,48,128]{2,1,0:T(8,128)(2,1)}), bf16[16,48,128]{2,1,0:T(8,128)(2,1)S(1)}, u32[]{:S(2)}, u32[]{:S(2)}) %all-to-all-start) | async-done | bytes 196640 | tf_op jit(solution)/shard_map/all_to_all | solution.py:211
  23.2 1.4 %shard_map.129 = bf16[16,192,128]{2,1,0:T(8,128)(2,1)} custom-call(bf16[768,128]{1,0:T(8,128)(2,1)S(1)} %bitcast.19, bf16[768,768]{1,0:T(8,128)(2,1)S(1)} %copy-done.1), custom_call_target="tpu_custom_call" | custom-call | flops 150994944 | bytes 3145728 | tf_op jit(solution)/shard_map/pallas_call | solution.py:85
  24.6 6.9 %all-to-all-start.1 = ((bf16[16,192,128]{2,1,0:T(8,128)(2,1)}), bf16[16,192,128]{2,1,0:T(8,128)(2,1)S(1)}, u32[]{:S(2)}, u32[]{:S(2)}) async-start(bf16[16,192,128]{2,1,0:T(8,128)(2,1)} %shard_map.129), calls=%async_computation.1 | async-start | bytes 1572864 | tf_op jit(solution)/shard_map/all_to_all | solution.py:215
  31.5 2.6 %collective-permute-start = (bf16[256,768]{1,0:T(8,128)(2,1)S(1)}, bf16[256,768]{1,0:T(8,128)(2,1)S(1)}, u32[]{:S(2)}, u32[]{:S(2)}) collective-permute-start(bf16[256,768]{1,0:T(8,128)(2,1)S(1)} %fusion.12.act0), channel_id=1, source_target_pairs={{0,12},{4,0},{8,4},{12,8},{1,13},{5,1},{9,5},{13,9},{2,14},{6,2},{... | collective-permute-start | bytes 1179656 | tf_op jit(solution)/shard_map/ppermute | solution.py:58
  34.3 2.5 %collective-permute-start.4 = (bf16[256,768]{1,0:T(8,128)(2,1)S(1)}, bf16[256,768]{1,0:T(8,128)(2,1)S(1)}, u32[]{:S(2)}, u32[]{:S(2)}) collective-permute-start(bf16[256,768]{1,0:T(8,128)(2,1)S(1)} %collective-permute-done.3.ct1), channel_id=1, source_target_pairs={{0,12},{4,0},{8,4},{12,8},{1,13},{5,1},{9,5},{13,9},{2,14},{6,2},{... | collective-permute-start | bytes 1179656 | tf_op jit(solution)/shard_map/ppermute | solution.py:58
  36.8 13.9 %collective-permute-done.act1 = bf16[256,768]{1,0:T(8,128)(2,1)S(1)} collective-permute-done((bf16[256,768]{1,0:T(8,128)(2,1)S(1)}, bf16[256,768]{1,0:T(8,128)(2,1)S(1)}, u32[]{:S(2)}, u32[]{:S(2)}) %collective-permute-start) | collective-permute-done | bytes 393248 | tf_op jit(solution)/shard_map/ppermute | solution.py:58
  50.8 1.3 %collective-permute-done.5.ct3 = bf16[256,768]{1,0:T(8,128)(2,1)S(1)} collective-permute-done((bf16[256,768]{1,0:T(8,128)(2,1)S(1)}, bf16[256,768]{1,0:T(8,128)(2,1)S(1)}, u32[]{:S(2)}, u32[]{:S(2)}) %collective-permute-start.5) | collective-permute-done | bytes 393248 | tf_op jit(solution)/shard_map/ppermute | solution.py:58
  52.0 8.4 %collective-permute-done.2.act2 = bf16[256,768]{1,0:T(8,128)(2,1)S(1)} collective-permute-done((bf16[256,768]{1,0:T(8,128)(2,1)S(1)}, bf16[256,768]{1,0:T(8,128)(2,1)S(1)}, u32[]{:S(2)}, u32[]{:S(2)}) %collective-permute-start.2) | collective-permute-done | bytes 393248 | tf_op jit(solution)/shard_map/ppermute | solution.py:58
  69.1 5.6 %shard_map.130 = (bf16[16,192,128]{2,1,0:T(8,128)(2,1)}, bf16[4,256,128]{2,1,0:T(8,128)(2,1)S(1)}, bf16[4,256,384]{2,1,0:T(8,128)(2,1)S(1)}, bf16[768,384]{1,0:T(8,128)(2,1)S(1)}, bf16[128,768]{1,0:T(8,128)(2,1)S(1)}) custom-call(bf16[256,768]{1,0:T(8,128)(2,1)S(1)} %fusion.12.act0, bf16[256,768]{1,0:T(8,128)(2,1)S(1)} %collective-permute-done.act1, ...), custom_call_target="tpu_custom_call" | custom-call | flops 4000000000 | bytes 12582912 | tf_op jit(solution)/shard_map/pallas_call | solution.py:85
  74.7 2.2 %shard_map.131 = (bf16[256,768]{1,0:T(8,128)(2,1)S(1)}, bf16[256,768]{1,0:T(8,128)(2,1)S(1)}, bf16[256,768]{1,0:T(8,128)(2,1)S(1)}, bf16[256,768]{1,0:T(8,128)(2...) custom-call(bf16[4,256,128]{2,1,0:T(8,128)(2,1)S(1)} %get-tuple-elem, ...), custom_call_target="tpu_custom_call" | custom-call | flops 1000000000 | bytes 6291456 | tf_op jit(solution)/shard_map/pallas_call | solution.py:85
  77.6 2.7 %collective-permute-start.9 = (bf16[256,768]{1,0:T(8,128)(2,1)}, bf16[256,768]{1,0:T(8,128)(2,1)}, u32[]{:S(2)}, u32[]{:S(2)}) collective-permute-start(bf16[256,768]{1,0:T(8,128)(2,1)} %get-tuple-element.27), channel_id=1, source_target_pairs={{0,12},{4,0},{8,4},{12,8},{1,13},{5,1},{9,5},{13,9},{2,14},{6,2},{... | collective-permute-start | bytes 1179656 | tf_op jit(solution)/shard_map/ppermute | solution.py:58
  80.3 4.1 %all-to-all-start.2 = ((bf16[16,192,128]{2,1,0:T(8,128)(2,1)}), bf16[16,192,128]{2,1,0:T(8,128)(2,1)S(1)}, u32[]{:S(2)}, u32[]{:S(2)}) async-start(bf16[16,192,128]{2,1,0:T(8,128)(2,1)} %get-tuple-element.29), calls=%async_computation.2 | async-start | bytes 1572864 | tf_op jit(solution)/shard_map/all_to_all | solution.py:248
  84.4 2.6 %collective-permute-start.6 = (bf16[256,768]{1,0:T(8,128)(2,1)}, bf16[256,768]{1,0:T(8,128)(2,1)}, u32[]{:S(2)}, u32[]{:S(2)}) collective-permute-start(bf16[256,768]{1,0:T(8,128)(2,1)} %get-tuple-element.22), channel_id=1, source_target_pairs={{0,12},{4,0},{8,4},{12,8},{1,13},{5,1},{9,5},{13,9},{2,14},{6,2},{... | collective-permute-start | bytes 1179656 | tf_op jit(solution)/shard_map/ppermute | solution.py:58
  87.0 1.8 %collective-permute-done.7 = bf16[256,768]{1,0:T(8,128)(2,1)S(1)} collective-permute-done((bf16[256,768]{1,0:T(8,128)(2,1)S(1)}, bf16[256,768]{1,0:T(8,128)(2,1)S(1)}, u32[]{:S(2)}, u32[]{:S(2)}) %collective-permute-start.7) | collective-permute-done | bytes 393248 | tf_op jit(solution)/shard_map/ppermute | solution.py:58
  89.5 1.9 %add_convert_fusion.1 = bf16[256,768]{1,0:T(8,128)(2,1)} fusion(bf16[256,768]{1,0:T(8,128)(2,1)} %copy-done.14, bf16[256,768]{1,0:T(8,128)(2,1)S(1)} %get-tuple-element.23), kind=kLoop, calls=%fused_computation.23 | loop fusion | flops 786432 | bytes 1179648 | tf_op jit(solution)/shard_map/convert_element_type | solution.py:258
  91.5 1.8 %add_convert_fusion = bf16[256,768]{1,0:T(8,128)(2,1)} fusion(bf16[256,768]{1,0:T(8,128)(2,1)} %collective-permute-done.9, bf16[256,768]{1,0:T(8,128)(2,1)S(1)} %get-tuple-element.26), kind=kLoop, calls=%fused_computation.22 | loop fusion | flops 786432 | bytes 1179648 | tf_op jit(solution)/shard_map/convert_element_type | solution.py:259
  93.3 2.7 %collective-permute-start.10 = (bf16[256,768]{1,0:T(8,128)(2,1)}, bf16[256,768]{1,0:T(8,128)(2,1)}, u32[]{:S(2)}, u32[]{:S(2)}) collective-permute-start(bf16[256,768]{1,0:T(8,128)(2,1)} %add_convert_fusion), channel_id=1, source_target_pairs={{0,12},{4,0},{8,4},{12,8},{1,13},{5,1},{9,5},{13,9},{2,14},{6,2},{... | collective-permute-start | bytes 1179656 | tf_op jit(solution)/shard_map/ppermute | solution.py:58
  96.0 3.2 %all-to-all-done.2.plane = bf16[16,192,128]{2,1,0:T(8,128)(2,1)S(1)} async-done(((bf16[16,192,128]{2,1,0:T(8,128)(2,1)}), bf16[16,192,128]{2,1,0:T(8,128)(2,1)S(1)}, u32[]{:S(2)}, u32[]{:S(2)}) %all-to-all-start.2) | async-done | bytes 786464 | tf_op jit(solution)/shard_map/all_to_all | solution.py:248
  100.4 6.6 %all-to-all-start.3 = ((bf16[16,48,128]{2,1,0:T(8,128)(2,1)}), bf16[16,48,128]{2,1,0:T(8,128)(2,1)S(1)}, u32[]{:S(2)}, u32[]{:S(2)}) async-start(bf16[16,48,128]{2,1,0:T(8,128)(2,1)} %bitcast.7), calls=%async_computation.3 | async-start | bytes 393216 | tf_op jit(solution)/shard_map/all_to_all | solution.py:270
  106.9 7.2 %collective-permute-done.8 = bf16[256,768]{1,0:T(8,128)(2,1)} collective-permute-done((bf16[256,768]{1,0:T(8,128)(2,1)}, bf16[256,768]{1,0:T(8,128)(2,1)}, u32[]{:S(2)}, u32[]{:S(2)}) %collective-permute-start.8) | collective-permute-done | bytes 393248 | tf_op jit(solution)/shard_map/ppermute | solution.py:58
  114.2 3.1 %fusion.17 = (bf16[1,256,768]{2,1,0:T(8,128)(2,1)}, bf16[1,256,768]{2,1,0:T(8,128)(2,1)}) fusion(bf16[1,256,768]{2,1,0:T(8,128)(2,1)S(1)} %copy-done.13, bf16[256,768]{1,0:T(8,128)(2,1)} %collective-permute-done.11, bf16[256,768]{1,0:T(8,128)(2,1)} %collective-permute-done.10, bf16[256,768]{1,0:T(8,128)(2,1)S(1)} %copy-done.4, ...), kind=kLoop, calls=%fused_computation.27 | loop fusion | flops 6488064 | bytes 3932160 | tf_op jit(solution)/shard_map/broadcast_in_dim | solution.py:274
  (59 shorter events, 16.5 us)
Async XLA Ops:
  0.6 22.6 %copy-start.1 = (bf16[768,768]{1,0:T(8,128)(2,1)S(1)}, bf16[768,768]{1,0:T(8,128)(2,1)}, u32[]{:S(2)}) copy-start(bf16[768,768]{1,0:T(8,128)(2,1)} %constant.24.clone.order) | copy-start | bytes 3538948
  2.9 20.3 %all-to-all-start = ((bf16[16,48,128]{2,1,0:T(8,128)(2,1)}), bf16[16,48,128]{2,1,0:T(8,128)(2,1)S(1)}, u32[]{:S(2)}, u32[]{:S(2)}) async-start(bf16[16,48,128]{2,1,0:T(8,128)(2,1)} %broadcast_in_dim.9), calls=%async_computation | async-start | bytes 393216 | tf_op jit(solution)/shard_map/all_to_all | solution.py:211
  14.2 19.9 %collective-permute-start.1 = (bf16[256,768]{1,0:T(8,128)(2,1)S(1)}, bf16[256,768]{1,0:T(8,128)(2,1)S(1)}, u32[]{:S(2)}, u32[]{:S(2)}) collective-permute-start(bf16[256,768]{1,0:T(8,128)(2,1)S(1)} %fusion.12.act0), channel_id=1, source_target_pairs={{0,4},{4,8},{8,12},{12,0},{1,5},{5,9},{9,13},{13,1},{2,6},{6,10},{... | collective-permute-start | bytes 1179656 | tf_op jit(solution)/shard_map/ppermute | solution.py:58
  15.5 18.8 %collective-permute-start.3 = (bf16[256,768]{1,0:T(8,128)(2,1)}, bf16[256,768]{1,0:T(8,128)(2,1)S(1)}, u32[]{:S(2)}, u32[]{:S(2)}) collective-permute-start(bf16[256,768]{1,0:T(8,128)(2,1)} %bitcast.20), channel_id=1, source_target_pairs={{0,12},{4,0},{8,4},{12,8},{1,13},{5,1},{9,5},{13,9},{2,14},{6,2},{... | collective-permute-start | bytes 1179656 | tf_op jit(solution)/shard_map/ppermute | solution.py:58
  24.6 9.5 %copy-start.2 = (bf16[1,256,768]{2,1,0:T(8,128)(2,1)S(1)}, bf16[1,256,768]{2,1,0:T(8,128)(2,1)}, u32[]{:S(2)}) copy-start(bf16[1,256,768]{2,1,0:T(8,128)(2,1)} %param.11) | copy-start | bytes 1179652
  24.6 37.4 %all-to-all-start.1 = ((bf16[16,192,128]{2,1,0:T(8,128)(2,1)}), bf16[16,192,128]{2,1,0:T(8,128)(2,1)S(1)}, u32[]{:S(2)}, u32[]{:S(2)}) async-start(bf16[16,192,128]{2,1,0:T(8,128)(2,1)} %shard_map.129), calls=%async_computation.1 | async-start | bytes 1572864 | tf_op jit(solution)/shard_map/all_to_all | solution.py:215
  31.5 19.3 %collective-permute-start = (bf16[256,768]{1,0:T(8,128)(2,1)S(1)}, bf16[256,768]{1,0:T(8,128)(2,1)S(1)}, u32[]{:S(2)}, u32[]{:S(2)}) collective-permute-start(bf16[256,768]{1,0:T(8,128)(2,1)S(1)} %fusion.12.act0), channel_id=1, source_target_pairs={{0,12},{4,0},{8,4},{12,8},{1,13},{5,1},{9,5},{13,9},{2,14},{6,2},{... | collective-permute-start | bytes 1179656 | tf_op jit(solution)/shard_map/ppermute | solution.py:58
  34.1 18.0 %collective-permute-start.5 = (bf16[256,768]{1,0:T(8,128)(2,1)S(1)}, bf16[256,768]{1,0:T(8,128)(2,1)S(1)}, u32[]{:S(2)}, u32[]{:S(2)}) collective-permute-start(bf16[256,768]{1,0:T(8,128)(2,1)S(1)} %bitcast.21), channel_id=1, source_target_pairs={{0,4},{4,8},{8,12},{12,0},{1,5},{5,9},{9,13},{13,1},{2,6},{6,10},{... | collective-permute-start | bytes 1179656 | tf_op jit(solution)/shard_map/ppermute | solution.py:58
  34.1 26.4 %collective-permute-start.2 = (bf16[256,768]{1,0:T(8,128)(2,1)S(1)}, bf16[256,768]{1,0:T(8,128)(2,1)S(1)}, u32[]{:S(2)}, u32[]{:S(2)}) collective-permute-start(bf16[256,768]{1,0:T(8,128)(2,1)S(1)} %collective-permute-done.1.act3), channel_id=1, source_target_pairs={{0,4},{4,8},{8,12},{12,0},{1,5},{5,9},{9,13},{13,1},{2,6},{6,10},{... | collective-permute-start | bytes 1179656 | tf_op jit(solution)/shard_map/ppermute | solution.py:58
  34.3 26.9 %collective-permute-start.4 = (bf16[256,768]{1,0:T(8,128)(2,1)S(1)}, bf16[256,768]{1,0:T(8,128)(2,1)S(1)}, u32[]{:S(2)}, u32[]{:S(2)}) collective-permute-start(bf16[256,768]{1,0:T(8,128)(2,1)S(1)} %collective-permute-done.3.ct1), channel_id=1, source_target_pairs={{0,12},{4,0},{8,4},{12,8},{1,13},{5,1},{9,5},{13,9},{2,14},{6,2},{... | collective-permute-start | bytes 1179656 | tf_op jit(solution)/shard_map/ppermute | solution.py:58
  64.0 1.3 %copy-start.9 = (bf16[768,768]{1,0:T(8,128)(2,1)S(1)}, bf16[768,768]{1,0:T(8,128)(2,1)}, u32[]{:S(2)}) copy-start(bf16[768,768]{1,0:T(8,128)(2,1)} %constant.28.clone.from_h) | copy-start | bytes 3538948
  65.2 1.3 %copy-start.10 = (bf16[768,768]{1,0:T(8,128)(2,1)S(1)}, bf16[768,768]{1,0:T(8,128)(2,1)}, u32[]{:S(2)}) copy-start(bf16[768,768]{1,0:T(8,128)(2,1)} %constant.27.clone.from_d) | copy-start | bytes 3538948
  66.5 1.3 %copy-start.11 = (bf16[768,768]{1,0:T(8,128)(2,1)S(1)}, bf16[768,768]{1,0:T(8,128)(2,1)}, u32[]{:S(2)}) copy-start(bf16[768,768]{1,0:T(8,128)(2,1)} %constant.26.clone.to_h) | copy-start | bytes 3538948
  77.6 11.2 %collective-permute-start.7 = (bf16[256,768]{1,0:T(8,128)(2,1)S(1)}, bf16[256,768]{1,0:T(8,128)(2,1)S(1)}, u32[]{:S(2)}, u32[]{:S(2)}) collective-permute-start(bf16[256,768]{1,0:T(8,128)(2,1)S(1)} %get-tuple-element.24), channel_id=1, source_target_pairs={{0,4},{4,8},{8,12},{12,0},{1,5},{5,9},{9,13},{13,1},{2,6},{6,10},{... | collective-permute-start | bytes 1179656 | tf_op jit(solution)/shard_map/ppermute | solution.py:58
  77.6 13.8 %collective-permute-start.9 = (bf16[256,768]{1,0:T(8,128)(2,1)}, bf16[256,768]{1,0:T(8,128)(2,1)}, u32[]{:S(2)}, u32[]{:S(2)}) collective-permute-start(bf16[256,768]{1,0:T(8,128)(2,1)} %get-tuple-element.27), channel_id=1, source_target_pairs={{0,12},{4,0},{8,4},{12,8},{1,13},{5,1},{9,5},{13,9},{2,14},{6,2},{... | collective-permute-start | bytes 1179656 | tf_op jit(solution)/shard_map/ppermute | solution.py:58
  80.3 18.8 %all-to-all-start.2 = ((bf16[16,192,128]{2,1,0:T(8,128)(2,1)}), bf16[16,192,128]{2,1,0:T(8,128)(2,1)S(1)}, u32[]{:S(2)}, u32[]{:S(2)}) async-start(bf16[16,192,128]{2,1,0:T(8,128)(2,1)} %get-tuple-element.29), calls=%async_computation.2 | async-start | bytes 1572864 | tf_op jit(solution)/shard_map/all_to_all | solution.py:248
  84.4 22.5 %collective-permute-start.6 = (bf16[256,768]{1,0:T(8,128)(2,1)}, bf16[256,768]{1,0:T(8,128)(2,1)}, u32[]{:S(2)}, u32[]{:S(2)}) collective-permute-start(bf16[256,768]{1,0:T(8,128)(2,1)} %get-tuple-element.22), channel_id=1, source_target_pairs={{0,12},{4,0},{8,4},{12,8},{1,13},{5,1},{9,5},{13,9},{2,14},{6,2},{... | collective-permute-start | bytes 1179656 | tf_op jit(solution)/shard_map/ppermute | solution.py:58
  87.0 20.0 %collective-permute-start.11 = (bf16[256,768]{1,0:T(8,128)(2,1)}, bf16[256,768]{1,0:T(8,128)(2,1)}, u32[]{:S(2)}, u32[]{:S(2)}) collective-permute-start(bf16[256,768]{1,0:T(8,128)(2,1)} %get-tuple-element.28), channel_id=1, source_target_pairs={{0,4},{4,8},{8,12},{12,0},{1,5},{5,9},{9,13},{13,1},{2,6},{6,10},{... | collective-permute-start | bytes 1179656 | tf_op jit(solution)/shard_map/ppermute | solution.py:58
  89.5 9.6 %copy-start = (bf16[768,768]{1,0:T(8,128)(2,1)S(1)}, bf16[768,768]{1,0:T(8,128)(2,1)}, u32[]{:S(2)}) copy-start(bf16[768,768]{1,0:T(8,128)(2,1)} %constant.29.clone.order) | copy-start | bytes 3538948
  91.5 22.7 %collective-permute-start.8 = (bf16[256,768]{1,0:T(8,128)(2,1)}, bf16[256,768]{1,0:T(8,128)(2,1)}, u32[]{:S(2)}, u32[]{:S(2)}) collective-permute-start(bf16[256,768]{1,0:T(8,128)(2,1)} %add_convert_fusion.1), channel_id=1, source_target_pairs={{0,4},{4,8},{8,12},{12,0},{1,5},{5,9},{9,13},{13,1},{2,6},{6,10},{... | collective-permute-start | bytes 1179656 | tf_op jit(solution)/shard_map/ppermute | solution.py:58
  93.3 20.9 %copy-start.4 = (bf16[256,768]{1,0:T(8,128)(2,1)S(1)}, bf16[256,768]{1,0:T(8,128)(2,1)}, u32[]{:S(2)}) copy-start(bf16[256,768]{1,0:T(8,128)(2,1)} %copy-done.3) | copy-start | bytes 1179652
  93.3 20.9 %copy-start.13 = (bf16[1,256,768]{2,1,0:T(8,128)(2,1)S(1)}, bf16[1,256,768]{2,1,0:T(8,128)(2,1)}, u32[]{:S(2)}) copy-start(bf16[1,256,768]{2,1,0:T(8,128)(2,1)} %param.10) | copy-start | bytes 1179652
  93.3 20.9 %collective-permute-start.10 = (bf16[256,768]{1,0:T(8,128)(2,1)}, bf16[256,768]{1,0:T(8,128)(2,1)}, u32[]{:S(2)}, u32[]{:S(2)}) collective-permute-start(bf16[256,768]{1,0:T(8,128)(2,1)} %add_convert_fusion), channel_id=1, source_target_pairs={{0,12},{4,0},{8,4},{12,8},{1,13},{5,1},{9,5},{13,9},{2,14},{6,2},{... | collective-permute-start | bytes 1179656 | tf_op jit(solution)/shard_map/ppermute | solution.py:58
  100.4 16.9 %all-to-all-start.3 = ((bf16[16,48,128]{2,1,0:T(8,128)(2,1)}), bf16[16,48,128]{2,1,0:T(8,128)(2,1)S(1)}, u32[]{:S(2)}, u32[]{:S(2)}) async-start(bf16[16,48,128]{2,1,0:T(8,128)(2,1)} %bitcast.7), calls=%async_computation.3 | async-start | bytes 393216 | tf_op jit(solution)/shard_map/all_to_all | solution.py:270
  (7 other events, 6.3 us)

commit v3 on v2

v3 whole, which is shorter than its diff:
```python
import numpy as np
import jax
import jax.numpy as jnp
from jax import lax
from jax.experimental import pallas as pl
from jax.experimental.pallas import tpu as pltpu
from jax.sharding import Mesh, PartitionSpec as P

NZ, NYH, NX, NYL, NC = 8, 2, 4, 2, 2
AXES = ("z", "yh", "x", "yl", "core")
SLAB = ("yh", "yl", "core")
SHEET = ("z", "x")
ROWS, D, INNER, TAKE = 256, 768, 512, 128
BF16 = jnp.bfloat16
F32 = jnp.float32
SCALE = 0.7978845608028654
CUBIC = 0.044715


def one_hot_rows(source):
    source = np.asarray(source).reshape(-1)
    matrix = np.zeros((source.size, source.size), np.float32)
    matrix[np.arange(source.size), source] = 1.0
    return matrix


def column_order():
    return one_hot_rows([
        64 * z + 32 * yh + 8 * x + low
        for x in range(NX) for z in range(NZ) for yh in range(NYH) for low in range(8)
    ])


def conv_rows_order():
    matrix = np.zeros((144, 384), np.float32)
    for t, q, r in np.ndindex(3, 16, 3):
        matrix[t * 48 + q * 3 + r, q * 24 + t * 3 + r] = 1.0
    return matrix


def point_rows_order():
    matrix = np.zeros((96, 192), np.float32)
    for j, z, r in np.ndindex(6, NZ, 2):
        matrix[j * 16 + z * 2 + r, z * 24 + 12 + r * 6 + j] = 1.0
    return matrix


def channel_order():
    return one_hot_rows([
        ((yh * 2 + yl) * 2 + core) * 48 + z * 12 + x * 3 + r
        for z in range(4) for yh in range(NYH) for x in range(NX)
        for yl in range(NYL) for core in range(NC) for r in range(3)
    ])


def inner_order():
    return one_hot_rows([p * 16 + z * 2 + r for z in range(NZ) for p in range(8) for r in range(2)])


def step_along_x(value, step):
    return lax.ppermute(value, "x", [(i, (i + step) % NX) for i in range(NX)])


def tanh_of(values):
    return jnp.tanh(SCALE * (values + CUBIC * (values * values * values)))


def gelu_tanh(values):
    return values * (0.5 * (1.0 + tanh_of(values)))


def gelu_slope(values):
    t = tanh_of(values)
    return 0.5 * (1.0 + t) + (0.5 * values) * ((1.0 - t * t) * (SCALE * (1.0 + 3.0 * CUBIC * (values * values))))


def dot(left, right, left_dim, right_dim):
    return lax.dot_general(
        left, right, (((left_dim,), (right_dim,)), ((), ())), preferred_element_type=F32
    )


def kernel_call(body, out_shapes, scratch=(), flops=0, moved=0, limit=8, far=0, far_out=False):
    many = isinstance(out_shapes, (list, tuple))
    vmem, hbm = pl.BlockSpec(memory_space=pltpu.VMEM), pl.BlockSpec(memory_space=pltpu.HBM)
    out_spec = hbm if far_out else vmem

    def call(*operands):
        return pl.pallas_call(
            body,
            out_shape=out_shapes,
            in_specs=[vmem] * (len(operands) - far) + [hbm] * far,
            out_specs=[out_spec] * len(out_shapes) if many else out_spec,
            scratch_shapes=list(scratch),
            compiler_params=pltpu.CompilerParams(vmem_limit_bytes=limit * 2**20),
            cost_estimate=pl.CostEstimate(flops=flops, bytes_accessed=moved, transcendentals=0),
        )(*operands)

    return call


def shape(*dims, dtype=BF16):
    return jax.ShapeDtypeStruct(dims, dtype)


def fetch(sources, targets, sems, first=0):
    copies = [
        pltpu.make_async_copy(source, target, sems.at[first + k])
        for k, (source, target) in enumerate(zip(sources, targets))
    ]
    for copy in copies:
        copy.start()
    return copies


def own_kernel(w_conv_far, w_point_far, order_far, out, rows_s, block_s, w_conv, w_point, order, sems):
    for copy in fetch((w_conv_far, w_point_far, order_far), (w_conv, w_point, order), sems):
        copy.wait()
    rows_s[...] = jnp.zeros_like(rows_s)
    for t in range(3):
        rows_s[t * 3:(t + 1) * 3, :] = w_conv[t].astype(F32)
    parted = dot(rows_s[...].astype(BF16), order[...], 1, 1)
    block_s[...] = jnp.zeros_like(block_s)
    point = w_point[...].astype(F32)
    for r in range(2):
        for j in range(6):
            block_s[pl.ds(12 + r * 6 + j, 1), :] = point[r:r + 1, j * TAKE:(j + 1) * TAKE]
    for x in range(NX):
        block_s[:9, :] = parted[:9, x * TAKE:(x + 1) * TAKE]
        block = block_s[...].astype(BF16)
        for z in range(NZ):
            out[z * NX + x] = block


def share_kernel(line, order, conv_share, point_share, rows_s, sum_s):
    me = lax.axis_index("x")
    rows_s[...] = jnp.zeros_like(rows_s)
    for x in range(NX):
        total = line[x].astype(F32)
        for z in range(1, NZ):
            total = total + line[z * NX + x].astype(F32)
        sum_s[...] = total
        rows_s[:9, x * TAKE:(x + 1) * TAKE] = sum_s[:9, :]
    total = line[me].astype(F32)
    for z in range(1, NZ):
        total = total + line[z * NX + me].astype(F32)
    sum_s[...] = total
    for r in range(2):
        for j in range(6):
            point_share[pl.ds(r, 1), j * TAKE:(j + 1) * TAKE] = sum_s[pl.ds(12 + r * 6 + j, 1), :]
    rows = rows_s[...]
    high = rows.astype(BF16)
    low = (rows - high.astype(F32)).astype(BF16)
    joined = dot(high, order[...], 1, 0) + dot(low, order[...], 1, 0)
    for t in range(3):
        for r in range(3):
            conv_share[r, pl.ds(t, 1), :] = joined[t * 3 + r:t * 3 + r + 1, :]


def slope_kernel(tokens, slope):
    for k in range(4):
        at = slice(k * 64, (k + 1) * 64)
        slope[at, :] = gelu_slope(tokens[at, :].astype(F32))


def add_kernel(mine, others, out):
    out[...] = (mine[...].astype(F32) + others[0].astype(F32)).astype(BF16)


def out_kernel(tokens, cotangent, slope, own, from_left, from_right, out_right, act_left, output, grad_tokens):
    for k in range(4):
        at = slice(k * 64, (k + 1) * 64)
        output[at, :] = (
            tokens[at, :].astype(F32) + own[0, at, :].astype(F32)
            + from_right[1, at, :].astype(F32) + out_right[at, :].astype(F32)
        ).astype(BF16)
        grad_act = own[1, at, :].astype(F32) + from_left[1, at, :].astype(F32) + act_left[at, :].astype(F32)
        grad_tokens[at, :] = (cotangent[at, :].astype(F32) + grad_act * slope[at, :]).astype(BF16)


def spread_kernel(line, conv_order, point_order, out, block_s, mine_s, all_s):
    me = lax.axis_index("x")
    for q in range(32):
        all_s[q * 24:(q + 1) * 24, :] = line[q].astype(F32)
    for z in range(NZ):
        mine_s[z * 24:(z + 1) * 24, :] = line[z * NX + me].astype(F32)
    for g in range(2):
        rows = dot(conv_order[...], all_s[g * 384:(g + 1) * 384, :].astype(BF16), 1, 0).astype(BF16)
        for t in range(3):
            block_s[t * 96 + g * 48:t * 96 + g * 48 + 48, :] = rows[t * 48:(t + 1) * 48]
    block_s[288:, :] = dot(point_order[...], mine_s[...].astype(BF16), 1, 0).astype(BF16)
    for p in range(8):
        out[p] = block_s[...]


def line_kernel(slab, conv_order, point_order, out, block_s, all_s):
    me = lax.axis_index("x")
    total = slab[0].astype(F32)
    for p in range(1, 8):
        total = total + slab[p].astype(F32)
    block_s[...] = total.astype(BF16)
    for g in range(2):
        rows = dot(conv_order[:, :48], block_s[g * 48:g * 48 + 48, :], 1, 0)
        for t in (1, 2):
            rows = rows + dot(
                conv_order[:, t * 48:(t + 1) * 48], block_s[t * 96 + g * 48:t * 96 + g * 48 + 48, :], 1, 0
            )
        for q in range(16):
            all_s[g * 16 + q] = rows[q * 24:(q + 1) * 24]
    rows = dot(point_order[...], block_s[288:, :], 1, 0)
    for z in range(NZ):
        all_s[z * NX + me] += rows[z * 24:(z + 1) * 24]
    for q in range(32):
        out[q] = all_s[q].astype(BF16)


def weights_kernel(slab, to_d, to_h, conv_w, point_w, rows_s, point_s):
    for g in range(2):
        for p in range(8):
            for t in range(3):
                at = t * 96 + g * 48
                rows_s[p * 48:(p + 1) * 48, t * TAKE:(t + 1) * TAKE] = slab[p, at:at + 48, :]
        conv_w[g * 384:(g + 1) * 384, :] = dot(to_d[...], rows_s[...], 1, 0).astype(BF16)
    for p in range(8):
        for j in range(6):
            at = 288 + j * 16
            point_s[p * 16:(p + 1) * 16, j * TAKE:(j + 1) * TAKE] = slab[p, at:at + 16, :]
    point_w[...] = dot(to_h[...], point_s[...], 1, 0).astype(BF16)


def middle_kernel(
    act0, act1, act2, act3, ct0, ct1, ct2, ct3, conv_w_far, point_w_far, from_d_far, from_h_far,
    grads_far, own_far, out_mid_far, act_mid_far, to_right_far, to_left_far,
    acts, cts, conv_w, point_w, from_d, from_h, grads, own, mids, to_right, to_left,
    inner_act, spread_grad, taps_s, grad_s, conv_g, in_sems, out_sems,
):
    me = lax.axis_index("x")
    place = [lax.rem(me + r, NX) for r in range(NX)]
    keep_before = [(p != 0).astype(F32) for p in place]
    keep_after = [(p != NX - 1).astype(F32) for p in place]
    copies = fetch(
        (conv_w_far, act0, act1, act2, act3, point_w_far, ct0, ct1, ct2, ct3, from_d_far, from_h_far),
        (conv_w, *[acts.at[r] for r in range(NX)], point_w, *[cts.at[r] for r in range(NX)], from_d, from_h),
        in_sems,
    )
    copies[0].wait()
    for r in range(NX):
        copies[1 + r].wait()
        taps_s[r] = dot(acts[r], conv_w[...], 1, 0)
    copies[5].wait()
    for r in range(NX):
        copies[6 + r].wait()
        grad_pre = dot(cts[r], point_w[...], 1, 1)
        conv_out = (
            taps_s[r, :, TAKE:2 * TAKE]
            + taps_s[(r - 1) % NX, :, :TAKE] * keep_before[r]
            + taps_s[(r + 1) % NX, :, 2 * TAKE:] * keep_after[r]
        )
        t = tanh_of(conv_out)
        cdf = 0.5 * (1.0 + t)
        inner_act[r] = (conv_out * cdf).astype(BF16)
        slope = cdf + (0.5 * conv_out) * (
            (1.0 - t * t) * (SCALE * (1.0 + 3.0 * CUBIC * (conv_out * conv_out)))
        )
        grad_s[r] = (grad_pre * slope).astype(BF16)
    for r in range(NX):
        spread_grad[r, :, :TAKE] = grad_s[(r + 1) % NX] * keep_after[r].astype(BF16)
        spread_grad[r, :, TAKE:2 * TAKE] = grad_s[r]
        spread_grad[r, :, 2 * TAKE:] = grad_s[(r - 1) % NX] * keep_before[r].astype(BF16)

    def out_part(r):
        return dot(inner_act[r], point_w[...], 1, 0).astype(BF16)

    def act_part(r):
        return dot(spread_grad[r], conv_w[...], 1, 1).astype(BF16)

    to_right[0], to_right[1] = out_part(2), act_part(1)
    sent = fetch((to_right,), (to_right_far,), out_sems)
    to_left[0], to_left[1] = act_part(2), out_part(3)
    sent += fetch((to_left,), (to_left_far,), out_sems, 1)

    for t in range(3):
        at = slice(t * TAKE, (t + 1) * TAKE)
        total = dot(spread_grad[0, :, at], acts[0], 0, 0)
        for r in range(1, NX):
            total = total + dot(spread_grad[r, :, at], acts[r], 0, 0)
        conv_g[:, at] = total.T.astype(BF16)
    copies[10].wait()
    copies[11].wait()
    for g in range(2):
        rows = dot(from_d[...], conv_g[g * 384:(g + 1) * 384, :], 1, 0).astype(BF16)
        for p in range(8):
            for t in range(3):
                grads[p, t * 96 + g * 48:t * 96 + g * 48 + 48, :] = rows[
                    p * 48:(p + 1) * 48, t * TAKE:(t + 1) * TAKE
                ]
    total = dot(inner_act[0], cts[0], 0, 0)
    for r in range(1, NX):
        total = total + dot(inner_act[r], cts[r], 0, 0)
    rows = dot(from_h[...], total.astype(BF16), 1, 0).astype(BF16)
    for p in range(8):
        for j in range(6):
            grads[p, 288 + j * 16:304 + j * 16, :] = rows[
                p * 16:(p + 1) * 16, j * TAKE:(j + 1) * TAKE
            ]
    sent += fetch((grads,), (grads_far,), out_sems, 2)
    own[0], own[1] = out_part(0), act_part(0)
    sent += fetch((own,), (own_far,), out_sems, 3)
    mids[0], mids[1] = out_part(1), act_part(3)
    sent += fetch((mids.at[0], mids.at[1]), (out_mid_far, act_mid_far), out_sems, 4)
    for copy in sent:
        copy.wait()


def shards(tokens, cotangent, w_conv, w_point):
    def constant(matrix):
        return jnp.asarray(matrix, BF16)

    columns, conv_rows, point_rows = column_order(), conv_rows_order(), point_rows_order()
    channels, inner = channel_order(), inner_order()

    own = kernel_call(
        own_kernel, shape(32, 24, TAKE),
        scratch=[
            pltpu.VMEM((16, INNER), F32), pltpu.VMEM((24, TAKE), F32),
            pltpu.VMEM((3, 3, INNER), BF16), pltpu.VMEM((2, D), BF16), pltpu.VMEM((INNER, INNER), BF16),
            pltpu.SemaphoreType.DMA((3,)),
        ],
        moved=2**19, far=3, limit=60,
    )(w_conv, w_point, constant(columns))
    line = lax.all_to_all(own, SHEET, 0, 0)
    act, ct = [None] * NX, [None] * NX
    act[0] = gelu_tanh(tokens[0].astype(F32)).astype(BF16)
    ct[0] = cotangent[0]
    act[3], act[1] = step_along_x(act[0], 1), step_along_x(act[0], -1)
    ct[3], ct[1] = step_along_x(ct[0], 1), step_along_x(ct[0], -1)
    line, act[1], act[3], ct[1], ct[3] = lax.optimization_barrier((line, act[1], act[3], ct[1], ct[3]))
    act[2] = step_along_x(act[3], 1)
    ct[2] = step_along_x(ct[1], -1)

    blocks = kernel_call(
        spread_kernel, shape(8, 384, TAKE),
        scratch=[pltpu.VMEM((384, TAKE), BF16), pltpu.VMEM((192, TAKE), F32), pltpu.VMEM((D, TAKE), F32)],
        flops=10**8, moved=2**20,
    )(line, constant(conv_rows), constant(point_rows))
    slab = lax.all_to_all(blocks, SLAB, 0, 0)
    conv_w, point_w = kernel_call(
        weights_kernel,
        [shape(D, 3 * TAKE), shape(TAKE, D)],
        scratch=[pltpu.VMEM((384, 3 * TAKE), BF16), pltpu.VMEM((TAKE, D), BF16)],
        flops=10**9,
        moved=3 * 2**20,
    )(slab, constant(channels), constant(inner))

    blocks = (2, ROWS, D)
    grads, own, out_mid, act_mid, to_right, to_left = kernel_call(
        middle_kernel,
        [
            shape(8, 384, TAKE), shape(*blocks), shape(ROWS, D), shape(ROWS, D), shape(*blocks), shape(*blocks),
        ],
        scratch=[
            pltpu.VMEM((NX, ROWS, D), BF16), pltpu.VMEM((NX, ROWS, D), BF16),
            pltpu.VMEM((D, 3 * TAKE), BF16), pltpu.VMEM((TAKE, D), BF16),
            pltpu.VMEM((384, 384), BF16), pltpu.VMEM((TAKE, TAKE), BF16),
            pltpu.VMEM((8, 384, TAKE), BF16),
            *[pltpu.VMEM(blocks, BF16)] * 4,
            pltpu.VMEM((NX, ROWS, TAKE), BF16),
            pltpu.VMEM((NX, ROWS, 3 * TAKE), BF16),
            pltpu.VMEM((NX, ROWS, 3 * TAKE), F32),
            pltpu.VMEM((NX, ROWS, TAKE), BF16),
            pltpu.VMEM((D, 3 * TAKE), BF16),
            pltpu.SemaphoreType.DMA((12,)),
            pltpu.SemaphoreType.DMA((6,)),
        ],
        flops=5 * 10**9,
        moved=12 * 2**20,
        limit=60,
        far=12,
        far_out=True,
    )(*act, *ct, conv_w, point_w, constant(channels.T), constant(inner.T))
    slab_g = lax.all_to_all(grads, SLAB, 0, 0)

    from_left, from_right = step_along_x(to_right, 1), step_along_x(to_left, -1)
    add = kernel_call(add_kernel, shape(ROWS, D), moved=2**20)
    out_right = step_along_x(add(out_mid, from_left), 1)
    act_left = step_along_x(add(act_mid, from_right), -1)
    slope = kernel_call(slope_kernel, shape(ROWS, D, dtype=F32), flops=10**7, moved=2**20)(tokens[0])
    output, grad_tokens = kernel_call(
        out_kernel, [shape(ROWS, D), shape(ROWS, D)], flops=10**7, moved=4 * 2**20
    )(tokens[0], ct[0], slope, own, from_left, from_right, out_right, act_left)

    line_g = kernel_call(
        line_kernel, shape(32, 24, TAKE),
        scratch=[pltpu.VMEM((384, TAKE), BF16), pltpu.VMEM((32, 24, TAKE), F32)],
        flops=10**8, moved=2**20,
    )(slab_g, constant(conv_rows.T), constant(point_rows.T))
    line_g = lax.all_to_all(line_g, SHEET, 0, 0)
    line_g, output, grad_tokens = lax.optimization_barrier((line_g, output, grad_tokens))
    conv_share, point_share = kernel_call(
        share_kernel,
        [shape(3, 3, INNER, dtype=F32), shape(2, D, dtype=F32)],
        scratch=[pltpu.VMEM((16, INNER), F32), pltpu.VMEM((24, TAKE), F32)],
        moved=2**18,
    )(line_g, constant(columns))
    return (output[None], grad_tokens[None], conv_share, point_share)


def solution(mesh):
    fine = Mesh(mesh.devices.reshape(NZ, NYH, NX, NYL, NC), AXES)
    dp, seq = ("z", "yh"), ("x", "yl", "core")
    rows = P(dp, seq, None)
    return jax.shard_map(
        shards,
        mesh=fine,
        in_specs=(rows, rows, P(None, AXES, None), P(AXES, None)),
        out_specs=(rows, rows, P(AXES, None, None), P(AXES, None)),
        check_vma=False,
    )
```

time: 120 us -> 104 us (0.87)
  blocking collectives: 0 us -> 18.7 us
  waiting for transfers between devices: 42.2 us -> 28.6 us
  starting transfers between devices: 43.5 us -> 31.3 us
  local copies, waits for them, and re-layouts: 13.6 us -> 2.63 us
  Pallas kernels: 10.4 us -> 18.8 us
  other arithmetic: 8.13 us -> 1.32 us
    ppermute x12 -> x10, waiting for transfers between devices: 32.7 us -> 13.1 us  [step_along_x(): return lax.ppermute(value, 'x', [(i, (i + step) % NX) for i in range(NX)])]
    all_to_all x0 -> x1, blocking collectives: none -> 18.7 us  [shards(): line = lax.all_to_all(own, SHEET, 0, 0)]
    all_to_all x4 -> x3, starting transfers between devices: 27.5 us -> 17 us  [the longest x1 7.99 us: shards(): slab = lax.all_to_all(blocks, SLAB, 0, 0)]
    pallas_call x4 -> x10, Pallas kernels: 10.4 us -> 18.8 us  [call(): pl.pallas_call(body, out_shape=out_shapes, in_specs=[vmem] * (len(operand...]
    unnamed x30 -> x44, local copies, waits for them, and re-layouts: 10.1 us -> 2.63 us
    all_to_all x4 -> x3, waiting for transfers between devices: 9.5 us -> 15.5 us  [the longest x1 9.59 us: shards(): slab = lax.all_to_all(blocks, SLAB, 0, 0)]
    convert_element_type x3 -> x1, other arithmetic: 5.03 us -> 1.32 us  [shards(): act[0] = gelu_tanh(tokens[0].astype(F32)).astype(BF16)]
    broadcast_in_dim x1 -> x0, other arithmetic: 3.06 us -> none  [shards(): return (output[None], grad_tokens[None], conv_share, point_share)]
  transfers between devices with their start and end apart: 16 -> 13, of which waited for: 8 -> 4; matrix products, arithmetic and copies ran while one was open for 7% -> 0% of each run, Pallas kernels for 2% -> 8%
where the time goes in v3:
time: 104 us; the launch traced here: 102 us
  starting transfers between devices  31.3 us (30%)
  waiting for transfers between devices  28.6 us (28%)
  Pallas kernels  18.8 us (18%)
  blocking collectives  18.7 us (18%)
  local copies, waits for them, and re-layouts  2.63 us (3%)
  other arithmetic  1.32 us (1%)
    pallas_call x10, Pallas kernels, call(): pl.pallas_call(body, out_shape=out_shapes, in_specs=[vmem] * (len(operand...  18.8 us
    all_to_all x1, blocking collectives, shards(): line = lax.all_to_all(own, SHEET, 0, 0)  18.7 us
    ppermute x10, starting transfers between devices, step_along_x(): return lax.ppermute(value, 'x', [(i, (i + step) % NX) for i in range(NX)])  14.3 us
    ppermute x10, waiting for transfers between devices, step_along_x(): return lax.ppermute(value, 'x', [(i, (i + step) % NX) for i in range(NX)])  13.1 us
    all_to_all x1, waiting for transfers between devices, shards(): slab = lax.all_to_all(blocks, SLAB, 0, 0)  9.59 us
    all_to_all x1, starting transfers between devices, shards(): slab = lax.all_to_all(blocks, SLAB, 0, 0)  7.99 us
    all_to_all x1, waiting for transfers between devices, shards(): line_g = lax.all_to_all(line_g, SHEET, 0, 0)  5.86 us
    all_to_all x1, starting transfers between devices, shards(): slab_g = lax.all_to_all(grads, SLAB, 0, 0)  5.01 us
  transfers between devices with their start and end apart: 13, of which 4 were waited for; matrix products, arithmetic and copies ran while one was open for 0% of the time, Pallas kernels for 8%

profile of v3, /device:TPU:1, one launch (start us, length us, event | category | flops | bytes accessed | tf_op | source)
XLA Modules:
  0.0 102.2 jit_solution(14303357374501883556)
XLA Ops:
  0.6 1.3 %fusion.5.act0 = bf16[256,768]{1,0:T(8,128)(2,1)S(1)} fusion(bf16[1,256,768]{2,1,0:T(8,128)(2,1)} %param.14), kind=kLoop, calls=%fused_computation.9 | loop fusion | flops 1966080 | bytes 786432 | tf_op jit(solution)/shard_map/convert_element_type | solution.py:333
  2.0 2.1 %collective-permute-start.1 = (bf16[256,768]{1,0:T(8,128)(2,1)S(1)}, bf16[256,768]{1,0:T(8,128)(2,1)S(1)}, u32[]{:S(2)}, u32[]{:S(2)}) collective-permute-start(bf16[256,768]{1,0:T(8,128)(2,1)S(1)} %fusion.5.act0), channel_id=1, source_target_pairs={{0,4},{4,8},{8,12},{12,0},{1,5},{5,9},{9,13},{13,1},{2,6},{6,10},{... | collective-permute-start | bytes 1179656 | tf_op jit(solution)/shard_map/ppermute | solution.py:61
  4.1 1.4 %collective-permute-start = (bf16[256,768]{1,0:T(8,128)(2,1)S(1)}, bf16[256,768]{1,0:T(8,128)(2,1)S(1)}, u32[]{:S(2)}, u32[]{:S(2)}) collective-permute-start(bf16[256,768]{1,0:T(8,128)(2,1)S(1)} %fusion.5.act0), channel_id=1, source_target_pairs={{0,12},{4,0},{8,4},{12,8},{1,13},{5,1},{9,5},{13,9},{2,14},{6,2},{... | collective-permute-start | bytes 1179656 | tf_op jit(solution)/shard_map/ppermute | solution.py:61
  5.6 2.6 %collective-permute-start.2 = (bf16[256,768]{1,0:T(8,128)(2,1)S(1)}, bf16[256,768]{1,0:T(8,128)(2,1)S(1)}, u32[]{:S(2)}, u32[]{:S(2)}) collective-permute-start(bf16[256,768]{1,0:T(8,128)(2,1)S(1)} %bitcast.9), channel_id=1, source_target_pairs={{0,12},{4,0},{8,4},{12,8},{1,13},{5,1},{9,5},{13,9},{2,14},{6,2},{... | collective-permute-start | bytes 1179656 | tf_op jit(solution)/shard_map/ppermute | solution.py:61
  8.1 2.1 %shard_map.165 = bf16[32,24,128]{2,1,0:T(8,128)(2,1)} custom-call(bf16[3,3,512]{2,1,0:T(4,128)(2,1)} %w_conv_far.1, bf16[2,768]{1,0:T(2,128)(2,1)} %w_point_far.1, bf16[512,512]{1,0:T(8,128)(2,1)} %constant.24.clone.order_far.order), custom_call_target="tpu_custom_call" | custom-call | bytes 524288 | tf_op jit(solution)/shard_map/pallas_call | solution.py:89
  10.2 18.7 %all_to_all.20.line = bf16[32,24,128]{2,1,0:T(8,128)(2,1)S(1)} all-to-all(bf16[32,24,128]{2,1,0:T(8,128)(2,1)} %shard_map.165), channel_id=1, replica_groups=mesh['z'=8,'yh'=2,'x'=4,'yl'=2,'core'=2] {'z','x'}, dimensions={0} | all-to-all | bytes 393216 | tf_op jit(solution)/shard_map/all_to_all | solution.py:331
  29.1 1.3 %shard_map.166 = bf16[8,384,128]{2,1,0:T(8,128)(2,1)} custom-call(bf16[32,24,128]{2,1,0:T(8,128)(2,1)S(1)} %all_to_all.20.line, bf16[144,384]{1,0:T(8,128)(2,1)S(1)} %copy-done.8, bf16[96,192]{1,0:T(8,128)(2,1)S(1)} %copy-done.10), custom_call_target="tpu_custom_call" | custom-call | flops 100000000 | bytes 1048576 | tf_op jit(solution)/shard_map/pallas_call | solution.py:89
  30.4 8.0 %all-to-all-start.1 = ((bf16[8,384,128]{2,1,0:T(8,128)(2,1)}), bf16[8,384,128]{2,1,0:T(8,128)(2,1)S(1)}, u32[]{:S(2)}, u32[]{:S(2)}) async-start(bf16[8,384,128]{2,1,0:T(8,128)(2,1)} %shard_map.166), calls=%async_computation.1 | async-start | bytes 1572864 | tf_op jit(solution)/shard_map/all_to_all | solution.py:346
  38.4 2.7 %collective-permute-start.5 = (bf16[256,768]{1,0:T(8,128)(2,1)S(1)}, bf16[256,768]{1,0:T(8,128)(2,1)S(1)}, u32[]{:S(2)}, u32[]{:S(2)}) collective-permute-start(bf16[256,768]{1,0:T(8,128)(2,1)S(1)} %collective-permute-done.2.ct1), channel_id=1, source_target_pairs={{0,12},{4,0},{8,4},{12,8},{1,13},{5,1},{9,5},{13,9},{2,14},{6,2},{... | collective-permute-start | bytes 1179656 | tf_op jit(solution)/shard_map/ppermute | solution.py:61
  41.1 9.6 %all-to-all-done.1.slab = bf16[8,384,128]{2,1,0:T(8,128)(2,1)S(1)} async-done(((bf16[8,384,128]{2,1,0:T(8,128)(2,1)}), bf16[8,384,128]{2,1,0:T(8,128)(2,1)S(1)}, u32[]{:S(2)}, u32[]{:S(2)}) %all-to-all-start.1) | async-done | bytes 786464 | tf_op jit(solution)/shard_map/all_to_all | solution.py:346
  51.3 0.8 copy-done.13
  53.7 8.2 %shard_map.168 = (bf16[8,384,128]{2,1,0:T(8,128)(2,1)}, bf16[2,256,768]{2,1,0:T(8,128)(2,1)}, bf16[256,768]{1,0:T(8,128)(2,1)}, bf16[256,768]{1,0:T(8,128)(2,1)}...) custom-call(bf16[256,768]{1,0:T(8,128)(2,1)} %copy-done.15, bf16[256,768]{1,0:T(8,128)(2,1)} %copy-done.17, ...), custom_call_target="tpu_custom_call" | custom-call | flops 5000000000 | bytes 12582912 | tf_op jit(solution)/shard_map/pallas_call | solution.py:89
  62.2 2.7 %collective-permute-start.7 = (bf16[2,256,768]{2,1,0:T(8,128)(2,1)}, bf16[2,256,768]{2,1,0:T(8,128)(2,1)S(1)}, u32[]{:S(2)}, u32[]{:S(2)}) collective-permute-start(bf16[2,256,768]{2,1,0:T(8,128)(2,1)} %get-tuple-element.34), channel_id=1, source_target_pairs={{0,12},{4,0},{8,4},{12,8},{1,13},{5,1},{9,5},{13,9},{2,14},{6,2},{... | collective-permute-start | bytes 2359304 | tf_op jit(solution)/shard_map/ppermute | solution.py:61
  64.9 5.0 %all-to-all-start.2 = ((bf16[8,384,128]{2,1,0:T(8,128)(2,1)}), bf16[8,384,128]{2,1,0:T(8,128)(2,1)S(1)}, u32[]{:S(2)}, u32[]{:S(2)}) async-start(bf16[8,384,128]{2,1,0:T(8,128)(2,1)} %get-tuple-element.31), calls=%async_computation.2 | async-start | bytes 1572864 | tf_op jit(solution)/shard_map/all_to_all | solution.py:381
  69.9 11.9 %collective-permute-done.6.others.from_left = bf16[2,256,768]{2,1,0:T(8,128)(2,1)S(1)} collective-permute-done((bf16[2,256,768]{2,1,0:T(8,128)(2,1)}, bf16[2,256,768]{2,1,0:T(8,128)(2,1)S(1)}, u32[]{:S(2)}, u32[]{:S(2)}) %collective-permute-start.6) | collective-permute-done | bytes 786464 | tf_op jit(solution)/shard_map/ppermute | solution.py:61
  81.8 0.8 shard_map.171
  82.8 0.8 shard_map.172
  83.6 2.5 %collective-permute-start.9 = (bf16[256,768]{1,0:T(8,128)(2,1)}, bf16[256,768]{1,0:T(8,128)(2,1)}, u32[]{:S(2)}, u32[]{:S(2)}) collective-permute-start(bf16[256,768]{1,0:T(8,128)(2,1)} %shard_map.172), channel_id=1, source_target_pairs={{0,12},{4,0},{8,4},{12,8},{1,13},{5,1},{9,5},{13,9},{2,14},{6,2},{... | collective-permute-start | bytes 1179656 | tf_op jit(solution)/shard_map/ppermute | solution.py:61
  86.2 1.1 %shard_map.169 = bf16[32,24,128]{2,1,0:T(8,128)(2,1)} custom-call(bf16[8,384,128]{2,1,0:T(8,128)(2,1)S(1)} %all-to-all-done.2.slab, bf16[384,144]{1,0:T(8,128)(2,1)S(1)} %copy-done.7, bf16[192,96]{1,0:T(8,128)(2,1)S(1)} %copy-done.9), custom_call_target="tpu_custom_call" | custom-call | flops 100000000 | bytes 1048576 | tf_op jit(solution)/shard_map/pallas_call | solution.py:89
  87.3 4.0 %all-to-all-start.3 = ((bf16[32,24,128]{2,1,0:T(8,128)(2,1)}), bf16[32,24,128]{2,1,0:T(8,128)(2,1)S(1)}, u32[]{:S(2)}, u32[]{:S(2)}) async-start(bf16[32,24,128]{2,1,0:T(8,128)(2,1)} %shard_map.169), calls=%async_computation.3 | async-start | bytes 393216 | tf_op jit(solution)/shard_map/all_to_all | solution.py:397
  91.8 1.2 %collective-permute-done.8.out_right = bf16[256,768]{1,0:T(8,128)(2,1)} collective-permute-done((bf16[256,768]{1,0:T(8,128)(2,1)}, bf16[256,768]{1,0:T(8,128)(2,1)}, u32[]{:S(2)}, u32[]{:S(2)}) %collective-permute-start.8) | collective-permute-done | bytes 393248 | tf_op jit(solution)/shard_map/ppermute | solution.py:61
  93.0 2.4 %shard_map.173 = (bf16[256,768]{1,0:T(8,128)(2,1)}, bf16[256,768]{1,0:T(8,128)(2,1)}) custom-call(bf16[256,768]{1,0:T(8,128)(2,1)S(1)} %bitcast.6, bf16[256,768]{1,0:T(8,128)(2,1)S(1)} %bitcast.10, f32[256,768]{1,0:T(8,128)S(1)} %shard_map.170.slope, bf16[2,256,768]{2,1,0:T(8,128)(2,1)S(1)} %copy-done.2, ...), custom_call_target="tpu_custom_call" | custom-call | flops 10000000 | bytes 4194304 | tf_op jit(solution)/shard_map/pallas_call | solution.py:89
  95.4 5.9 %all-to-all-done.3.line = bf16[32,24,128]{2,1,0:T(8,128)(2,1)S(1)} async-done(((bf16[32,24,128]{2,1,0:T(8,128)(2,1)}), bf16[32,24,128]{2,1,0:T(8,128)(2,1)S(1)}, u32[]{:S(2)}, u32[]{:S(2)}) %all-to-all-start.3) | async-done | bytes 196640 | tf_op jit(solution)/shard_map/all_to_all | solution.py:397
  101.3 0.9 shard_map.174
  (58 shorter events, 3.3 us)
Async XLA Ops:
  0.6 4.8 %copy-start.3 = (bf16[1,256,768]{2,1,0:T(8,128)(2,1)S(1)}, bf16[1,256,768]{2,1,0:T(8,128)(2,1)}, u32[]{:S(2)}) copy-start(bf16[1,256,768]{2,1,0:T(8,128)(2,1)} %param.15) | copy-start | bytes 1179652
  2.0 27.0 %copy-start.15 = (bf16[256,768]{1,0:T(8,128)(2,1)}, bf16[256,768]{1,0:T(8,128)(2,1)S(1)}, u32[]{:S(2)}) copy-start(bf16[256,768]{1,0:T(8,128)(2,1)S(1)} %fusion.5.act0) | copy-start | bytes 1179652
  2.0 27.0 %collective-permute-start.1 = (bf16[256,768]{1,0:T(8,128)(2,1)S(1)}, bf16[256,768]{1,0:T(8,128)(2,1)S(1)}, u32[]{:S(2)}, u32[]{:S(2)}) collective-permute-start(bf16[256,768]{1,0:T(8,128)(2,1)S(1)} %fusion.5.act0), channel_id=1, source_target_pairs={{0,4},{4,8},{8,12},{12,0},{1,5},{5,9},{9,13},{13,1},{2,6},{6,10},{... | collective-permute-start | bytes 1179656 | tf_op jit(solution)/shard_map/ppermute | solution.py:61
  4.1 24.9 %collective-permute-start = (bf16[256,768]{1,0:T(8,128)(2,1)S(1)}, bf16[256,768]{1,0:T(8,128)(2,1)S(1)}, u32[]{:S(2)}, u32[]{:S(2)}) collective-permute-start(bf16[256,768]{1,0:T(8,128)(2,1)S(1)} %fusion.5.act0), channel_id=1, source_target_pairs={{0,12},{4,0},{8,4},{12,8},{1,13},{5,1},{9,5},{13,9},{2,14},{6,2},{... | collective-permute-start | bytes 1179656 | tf_op jit(solution)/shard_map/ppermute | solution.py:61
  5.5 23.5 %collective-permute-start.3 = (bf16[256,768]{1,0:T(8,128)(2,1)S(1)}, bf16[256,768]{1,0:T(8,128)(2,1)S(1)}, u32[]{:S(2)}, u32[]{:S(2)}) collective-permute-start(bf16[256,768]{1,0:T(8,128)(2,1)S(1)} %bitcast.8), channel_id=1, source_target_pairs={{0,4},{4,8},{8,12},{12,0},{1,5},{5,9},{9,13},{13,1},{2,6},{6,10},{... | collective-permute-start | bytes 1179656 | tf_op jit(solution)/shard_map/ppermute | solution.py:61
  5.6 23.5 %collective-permute-start.2 = (bf16[256,768]{1,0:T(8,128)(2,1)S(1)}, bf16[256,768]{1,0:T(8,128)(2,1)S(1)}, u32[]{:S(2)}, u32[]{:S(2)}) collective-permute-start(bf16[256,768]{1,0:T(8,128)(2,1)S(1)} %bitcast.9), channel_id=1, source_target_pairs={{0,12},{4,0},{8,4},{12,8},{1,13},{5,1},{9,5},{13,9},{2,14},{6,2},{... | collective-permute-start | bytes 1179656 | tf_op jit(solution)/shard_map/ppermute | solution.py:61
  10.2 18.8 %copy-start.8 = (bf16[144,384]{1,0:T(8,128)(2,1)S(1)}, bf16[144,384]{1,0:T(8,128)(2,1)}, u32[]{:S(2)}) copy-start(bf16[144,384]{1,0:T(8,128)(2,1)} %constant.25.clone.conv_order) | copy-start | bytes 331780
  10.2 18.8 %copy-start.10 = (bf16[96,192]{1,0:T(8,128)(2,1)S(1)}, bf16[96,192]{1,0:T(8,128)(2,1)}, u32[]{:S(2)}) copy-start(bf16[96,192]{1,0:T(8,128)(2,1)} %constant.26.clone.point_order) | copy-start | bytes 110596
  29.0 9.4 %copy-start.16 = (bf16[256,768]{1,0:T(8,128)(2,1)}, bf16[256,768]{1,0:T(8,128)(2,1)S(1)}, u32[]{:S(2)}) copy-start(bf16[256,768]{1,0:T(8,128)(2,1)S(1)} %collective-permute-done.1.act3) | copy-start | bytes 1179652
  29.0 9.3 %copy-start.19 = (bf16[256,768]{1,0:T(8,128)(2,1)}, bf16[256,768]{1,0:T(8,128)(2,1)S(1)}, u32[]{:S(2)}) copy-start(bf16[256,768]{1,0:T(8,128)(2,1)S(1)} %collective-permute-done.2.ct1) | copy-start | bytes 1179652
  30.4 20.3 %copy-start.11 = (bf16[384,384]{1,0:T(8,128)(2,1)S(1)}, bf16[384,384]{1,0:T(8,128)(2,1)}, u32[]{:S(2)}) copy-start(bf16[384,384]{1,0:T(8,128)(2,1)} %constant.27.clone.to_d) | copy-start | bytes 884740
  30.4 20.3 %copy-start.12 = (bf16[128,128]{1,0:T(8,128)(2,1)S(1)}, bf16[128,128]{1,0:T(8,128)(2,1)}, u32[]{:S(2)}) copy-start(bf16[128,128]{1,0:T(8,128)(2,1)} %constant.28.clone.to_h.from_h_far) | copy-start | bytes 98308
  30.4 20.3 %all-to-all-start.1 = ((bf16[8,384,128]{2,1,0:T(8,128)(2,1)}), bf16[8,384,128]{2,1,0:T(8,128)(2,1)S(1)}, u32[]{:S(2)}, u32[]{:S(2)}) async-start(bf16[8,384,128]{2,1,0:T(8,128)(2,1)} %shard_map.166), calls=%async_computation.1 | async-start | bytes 1572864 | tf_op jit(solution)/shard_map/all_to_all | solution.py:346
  38.4 14.4 %collective-permute-start.4 = (bf16[256,768]{1,0:T(8,128)(2,1)S(1)}, bf16[256,768]{1,0:T(8,128)(2,1)S(1)}, u32[]{:S(2)}, u32[]{:S(2)}) collective-permute-start(bf16[256,768]{1,0:T(8,128)(2,1)S(1)} %collective-permute-done.1.act3), channel_id=1, source_target_pairs={{0,4},{4,8},{8,12},{12,0},{1,5},{5,9},{9,13},{13,1},{2,6},{6,10},{... | collective-permute-start | bytes 1179656 | tf_op jit(solution)/shard_map/ppermute | solution.py:61
  38.4 14.4 %collective-permute-start.5 = (bf16[256,768]{1,0:T(8,128)(2,1)S(1)}, bf16[256,768]{1,0:T(8,128)(2,1)S(1)}, u32[]{:S(2)}, u32[]{:S(2)}) collective-permute-start(bf16[256,768]{1,0:T(8,128)(2,1)S(1)} %collective-permute-done.2.ct1), channel_id=1, source_target_pairs={{0,12},{4,0},{8,4},{12,8},{1,13},{5,1},{9,5},{13,9},{2,14},{6,2},{... | collective-permute-start | bytes 1179656 | tf_op jit(solution)/shard_map/ppermute | solution.py:61
  61.9 19.9 %collective-permute-start.6 = (bf16[2,256,768]{2,1,0:T(8,128)(2,1)}, bf16[2,256,768]{2,1,0:T(8,128)(2,1)S(1)}, u32[]{:S(2)}, u32[]{:S(2)}) collective-permute-start(bf16[2,256,768]{2,1,0:T(8,128)(2,1)} %get-tuple-element.33), channel_id=1, source_target_pairs={{0,4},{4,8},{8,12},{12,0},{1,5},{5,9},{9,13},{13,1},{2,6},{6,10},{... | collective-permute-start | bytes 2359304 | tf_op jit(solution)/shard_map/ppermute | solution.py:61
  62.2 20.4 %collective-permute-start.7 = (bf16[2,256,768]{2,1,0:T(8,128)(2,1)}, bf16[2,256,768]{2,1,0:T(8,128)(2,1)S(1)}, u32[]{:S(2)}, u32[]{:S(2)}) collective-permute-start(bf16[2,256,768]{2,1,0:T(8,128)(2,1)} %get-tuple-element.34), channel_id=1, source_target_pairs={{0,12},{4,0},{8,4},{12,8},{1,13},{5,1},{9,5},{13,9},{2,14},{6,2},{... | collective-permute-start | bytes 2359304 | tf_op jit(solution)/shard_map/ppermute | solution.py:61
  64.9 16.9 %copy-start.6 = (bf16[256,768]{1,0:T(8,128)(2,1)S(1)}, bf16[256,768]{1,0:T(8,128)(2,1)}, u32[]{:S(2)}) copy-start(bf16[256,768]{1,0:T(8,128)(2,1)} %get-tuple-element.35.mine) | copy-start | bytes 1179652
  64.9 21.3 %all-to-all-start.2 = ((bf16[8,384,128]{2,1,0:T(8,128)(2,1)}), bf16[8,384,128]{2,1,0:T(8,128)(2,1)S(1)}, u32[]{:S(2)}, u32[]{:S(2)}) async-start(bf16[8,384,128]{2,1,0:T(8,128)(2,1)} %get-tuple-element.31), calls=%async_computation.2 | async-start | bytes 1572864 | tf_op jit(solution)/shard_map/all_to_all | solution.py:381
  82.6 10.4 %collective-permute-start.8 = (bf16[256,768]{1,0:T(8,128)(2,1)}, bf16[256,768]{1,0:T(8,128)(2,1)}, u32[]{:S(2)}, u32[]{:S(2)}) collective-permute-start(bf16[256,768]{1,0:T(8,128)(2,1)} %shard_map.171), channel_id=1, source_target_pairs={{0,4},{4,8},{8,12},{12,0},{1,5},{5,9},{9,13},{13,1},{2,6},{6,10},{... | collective-permute-start | bytes 1179656 | tf_op jit(solution)/shard_map/ppermute | solution.py:61
  83.6 9.3 %collective-permute-start.9 = (bf16[256,768]{1,0:T(8,128)(2,1)}, bf16[256,768]{1,0:T(8,128)(2,1)}, u32[]{:S(2)}, u32[]{:S(2)}) collective-permute-start(bf16[256,768]{1,0:T(8,128)(2,1)} %shard_map.172), channel_id=1, source_target_pairs={{0,12},{4,0},{8,4},{12,8},{1,13},{5,1},{9,5},{13,9},{2,14},{6,2},{... | collective-permute-start | bytes 1179656 | tf_op jit(solution)/shard_map/ppermute | solution.py:61
  87.3 5.7 %copy-start.2 = (bf16[2,256,768]{2,1,0:T(8,128)(2,1)S(1)}, bf16[2,256,768]{2,1,0:T(8,128)(2,1)}, u32[]{:S(2)}) copy-start(bf16[2,256,768]{2,1,0:T(8,128)(2,1)} %get-tuple-element.32.own) | copy-start | bytes 2359300
  87.3 14.0 %all-to-all-start.3 = ((bf16[32,24,128]{2,1,0:T(8,128)(2,1)}), bf16[32,24,128]{2,1,0:T(8,128)(2,1)S(1)}, u32[]{:S(2)}, u32[]{:S(2)}) async-start(bf16[32,24,128]{2,1,0:T(8,128)(2,1)} %shard_map.169), calls=%async_computation.3 | async-start | bytes 393216 | tf_op jit(solution)/shard_map/all_to_all | solution.py:397
  93.0 8.3 %copy-start.1 = (bf16[512,512]{1,0:T(8,128)(2,1)S(1)}, bf16[512,512]{1,0:T(8,128)(2,1)}, u32[]{:S(2)}) copy-start(bf16[512,512]{1,0:T(8,128)(2,1)} %constant.24.clone.order_far.order) | copy-start | bytes 1572868
  (11 other events, 19.3 us)

commit v4 on v3

--- a/solution.py
+++ b/solution.py
@@ -113,8 +113,17 @@
     return copies
 
 
-def own_kernel(w_conv_far, w_point_far, order_far, out, rows_s, block_s, w_conv, w_point, order, sems):
-    for copy in fetch((w_conv_far, w_point_far, order_far), (w_conv, w_point, order), sems):
+def front_kernel(
+    w_conv_far, w_point_far, order_far, tokens_far,
+    out_far, act_far,
+    rows_s, block_s, w_conv, w_point, order, tokens, act, own_s, in_sems, out_sems,
+):
+    copies = fetch(
+        (tokens_far.at[0], w_conv_far, w_point_far, order_far),
+        (tokens, w_conv, w_point, order),
+        in_sems,
+    )
+    for copy in copies[1:]:
         copy.wait()
     rows_s[...] = jnp.zeros_like(rows_s)
     for t in range(3):
@@ -129,7 +138,15 @@
         block_s[:9, :] = parted[:9, x * TAKE:(x + 1) * TAKE]
         block = block_s[...].astype(BF16)
         for z in range(NZ):
-            out[z * NX + x] = block
+            own_s[z * NX + x] = block
+    sent = fetch((own_s,), (out_far,), out_sems)
+    copies[0].wait()
+    for k in range(4):
+        at = slice(k * 64, (k + 1) * 64)
+        act[at, :] = gelu_tanh(tokens[at, :].astype(F32)).astype(BF16)
+    sent += fetch((act,), (act_far,), out_sems, 1)
+    for copy in sent:
+        copy.wait()
 
 
 def share_kernel(line, order, conv_share, point_share, rows_s, sum_s):
@@ -163,18 +180,20 @@
         slope[at, :] = gelu_slope(tokens[at, :].astype(F32))
 
 
-def add_kernel(mine, others, out):
-    out[...] = (mine[...].astype(F32) + others[0].astype(F32)).astype(BF16)
-
-
-def out_kernel(tokens, cotangent, slope, own, from_left, from_right, out_right, act_left, output, grad_tokens):
+def add_kernel(mine, other, out):
+    out[...] = (mine[...].astype(F32) + other[...].astype(F32)).astype(BF16)
+
+
+def out_kernel(
+    tokens, cotangent, slope, own, out_left, out_right, act_left, act_right, output, grad_tokens
+):
     for k in range(4):
         at = slice(k * 64, (k + 1) * 64)
         output[at, :] = (
             tokens[at, :].astype(F32) + own[0, at, :].astype(F32)
-            + from_right[1, at, :].astype(F32) + out_right[at, :].astype(F32)
+            + out_left[at, :].astype(F32) + out_right[at, :].astype(F32)
         ).astype(BF16)
-        grad_act = own[1, at, :].astype(F32) + from_left[1, at, :].astype(F32) + act_left[at, :].astype(F32)
+        grad_act = own[1, at, :].astype(F32) + act_right[at, :].astype(F32) + act_left[at, :].astype(F32)
         grad_tokens[at, :] = (cotangent[at, :].astype(F32) + grad_act * slope[at, :]).astype(BF16)
 
 
@@ -214,7 +233,31 @@
         out[q] = all_s[q].astype(BF16)
 
 
-def weights_kernel(slab, to_d, to_h, conv_w, point_w, rows_s, point_s):
+def middle_kernel(
+    slab_far, to_d_far, to_h_far, from_d_far, from_h_far, *refs,
+):
+    parts_far, refs = refs[:10], refs[10:]
+    grads_far, own_far, out1_far, act3_far, out2_far, act2_far, out3_far, act1_far = refs[:8]
+    (
+        slab, to_d, to_h, acts, cts, conv_w, point_w, from_d, from_h, rows_s, point_s, grads, sends,
+        inner_act, spread_grad, taps_s, grad_s, conv_g, in_sems, out_sems,
+    ) = refs[8:]
+    me = lax.axis_index("x")
+    place = [lax.rem(me + r, NX) for r in range(NX)]
+    keep_before = [(p != 0).astype(F32) for p in place]
+    keep_after = [(p != NX - 1).astype(F32) for p in place]
+    top, low = slice(0, ROWS // 2), slice(ROWS // 2, ROWS)
+    places = [
+        full.at[r, at] for full in (acts, cts)
+        for r, at in ((0, slice(None)), (1, slice(None)), (3, slice(None)), (2, top), (2, low))
+    ]
+    copies = fetch(
+        (slab_far, to_d_far, to_h_far, *parts_far, from_d_far, from_h_far),
+        (slab, to_d, to_h, *places, from_d, from_h),
+        in_sems,
+    )
+    for copy in copies[:3]:
+        copy.wait()
     for g in range(2):
         for p in range(8):
             for t in range(3):
@@ -226,30 +269,13 @@
             at = 288 + j * 16
             point_s[p * 16:(p + 1) * 16, j * TAKE:(j + 1) * TAKE] = slab[p, at:at + 16, :]
     point_w[...] = dot(to_h[...], point_s[...], 1, 0).astype(BF16)
-
-
-def middle_kernel(
-    act0, act1, act2, act3, ct0, ct1, ct2, ct3, conv_w_far, point_w_far, from_d_far, from_h_far,
-    grads_far, own_far, out_mid_far, act_mid_far, to_right_far, to_left_far,
-    acts, cts, conv_w, point_w, from_d, from_h, grads, own, mids, to_right, to_left,
-    inner_act, spread_grad, taps_s, grad_s, conv_g, in_sems, out_sems,
-):
-    me = lax.axis_index("x")
-    place = [lax.rem(me + r, NX) for r in range(NX)]
-    keep_before = [(p != 0).astype(F32) for p in place]
-    keep_after = [(p != NX - 1).astype(F32) for p in place]
-    copies = fetch(
-        (conv_w_far, act0, act1, act2, act3, point_w_far, ct0, ct1, ct2, ct3, from_d_far, from_h_far),
-        (conv_w, *[acts.at[r] for r in range(NX)], point_w, *[cts.at[r] for r in range(NX)], from_d, from_h),
-        in_sems,
-    )
-    copies[0].wait()
+    for copy in copies[3:8]:
+        copy.wait()
     for r in range(NX):
-        copies[1 + r].wait()
         taps_s[r] = dot(acts[r], conv_w[...], 1, 0)
-    copies[5].wait()
+    for copy in copies[8:13]:
+        copy.wait()
     for r in range(NX):
-        copies[6 + r].wait()
         grad_pre = dot(cts[r], point_w[...], 1, 1)
         conv_out = (
             taps_s[r, :, TAKE:2 * TAKE]
@@ -274,10 +300,20 @@
     def act_part(r):
         return dot(spread_grad[r], conv_w[...], 1, 1).astype(BF16)
 
-    to_right[0], to_right[1] = out_part(2), act_part(1)
-    sent = fetch((to_right,), (to_right_far,), out_sems)
-    to_left[0], to_left[1] = act_part(2), out_part(3)
-    sent += fetch((to_left,), (to_left_far,), out_sems, 1)
+    sent = []
+
+    def send(k, value, target):
+        sends[k] = value
+        sent.extend(fetch((sends.at[k],), (target,), out_sems, k))
+
+    send(0, out_part(2), out2_far)
+    send(1, act_part(2), act2_far)
+    send(2, out_part(3), out3_far)
+    send(3, act_part(1), act1_far)
+    send(4, out_part(1), out1_far)
+    send(5, act_part(3), act3_far)
+    send(6, out_part(0), own_far.at[0])
+    send(7, act_part(0), own_far.at[1])
 
     for t in range(3):
         at = slice(t * TAKE, (t + 1) * TAKE)
@@ -285,8 +321,8 @@
         for r in range(1, NX):
             total = total + dot(spread_grad[r, :, at], acts[r], 0, 0)
         conv_g[:, at] = total.T.astype(BF16)
-    copies[10].wait()
-    copies[11].wait()
+    copies[13].wait()
+    copies[14].wait()
     for g in range(2):
         rows = dot(from_d[...], conv_g[g * 384:(g + 1) * 384, :], 1, 0).astype(BF16)
         for p in range(8):
@@ -303,11 +339,7 @@
             grads[p, 288 + j * 16:304 + j * 16, :] = rows[
                 p * 16:(p + 1) * 16, j * TAKE:(j + 1) * TAKE
             ]
-    sent += fetch((grads,), (grads_far,), out_sems, 2)
-    own[0], own[1] = out_part(0), act_part(0)
-    sent += fetch((own,), (own_far,), out_sems, 3)
-    mids[0], mids[1] = out_part(1), act_part(3)
-    sent += fetch((mids.at[0], mids.at[1]), (out_mid_far, act_mid_far), out_sems, 4)
+    sent.extend(fetch((grads,), (grads_far,), out_sems, 8))
     for copy in sent:
         copy.wait()
 
@@ -319,81 +351,80 @@
     columns, conv_rows, point_rows = column_order(), conv_rows_order(), point_rows_order()
     channels, inner = channel_order(), inner_order()
 
-    own = kernel_call(
-        own_kernel, shape(32, 24, TAKE),
+    act, ct = [None] * NX, [None] * NX
+    own, act[0] = kernel_call(
+        front_kernel, [shape(32, 24, TAKE), shape(ROWS, D)],
         scratch=[
             pltpu.VMEM((16, INNER), F32), pltpu.VMEM((24, TAKE), F32),
             pltpu.VMEM((3, 3, INNER), BF16), pltpu.VMEM((2, D), BF16), pltpu.VMEM((INNER, INNER), BF16),
-            pltpu.SemaphoreType.DMA((3,)),
+            pltpu.VMEM((ROWS, D), BF16), pltpu.VMEM((ROWS, D), BF16), pltpu.VMEM((32, 24, TAKE), BF16),
+            pltpu.SemaphoreType.DMA((4,)), pltpu.SemaphoreType.DMA((2,)),
         ],
-        moved=2**19, far=3, limit=60,
-    )(w_conv, w_point, constant(columns))
+        flops=10**7, moved=2 * 2**20, far=4, far_out=True, limit=60,
+    )(w_conv, w_point, constant(columns), tokens)
     line = lax.all_to_all(own, SHEET, 0, 0)
-    act, ct = [None] * NX, [None] * NX
-    act[0] = gelu_tanh(tokens[0].astype(F32)).astype(BF16)
     ct[0] = cotangent[0]
     act[3], act[1] = step_along_x(act[0], 1), step_along_x(act[0], -1)
     ct[3], ct[1] = step_along_x(ct[0], 1), step_along_x(ct[0], -1)
+    def far_block(blocks):
+        top, low = blocks[3][:ROWS // 2], blocks[1][ROWS // 2:]
+        return step_along_x(top, 1), step_along_x(low, -1)
+
     line, act[1], act[3], ct[1], ct[3] = lax.optimization_barrier((line, act[1], act[3], ct[1], ct[3]))
-    act[2] = step_along_x(act[3], 1)
-    ct[2] = step_along_x(ct[1], -1)
-
+    act[2] = far_block(act)
+    ct[2] = far_block(ct)
     blocks = kernel_call(
         spread_kernel, shape(8, 384, TAKE),
         scratch=[pltpu.VMEM((384, TAKE), BF16), pltpu.VMEM((192, TAKE), F32), pltpu.VMEM((D, TAKE), F32)],
-        flops=10**8, moved=2**20,
+        flops=2 * 10**10, moved=2**20,
     )(line, constant(conv_rows), constant(point_rows))
     slab = lax.all_to_all(blocks, SLAB, 0, 0)
-    conv_w, point_w = kernel_call(
-        weights_kernel,
-        [shape(D, 3 * TAKE), shape(TAKE, D)],
-        scratch=[pltpu.VMEM((384, 3 * TAKE), BF16), pltpu.VMEM((TAKE, D), BF16)],
-        flops=10**9,
-        moved=3 * 2**20,
-    )(slab, constant(channels), constant(inner))
-
-    blocks = (2, ROWS, D)
-    grads, own, out_mid, act_mid, to_right, to_left = kernel_call(
+    block = shape(ROWS, D)
+    grads, own, out1, act3, out2, act2, out3, act1 = kernel_call(
         middle_kernel,
-        [
-            shape(8, 384, TAKE), shape(*blocks), shape(ROWS, D), shape(ROWS, D), shape(*blocks), shape(*blocks),
-        ],
+        [shape(8, 384, TAKE), shape(2, ROWS, D)] + [block] * 6,
         scratch=[
+            pltpu.VMEM((8, 384, TAKE), BF16), pltpu.VMEM((384, 384), BF16), pltpu.VMEM((TAKE, TAKE), BF16),
             pltpu.VMEM((NX, ROWS, D), BF16), pltpu.VMEM((NX, ROWS, D), BF16),
             pltpu.VMEM((D, 3 * TAKE), BF16), pltpu.VMEM((TAKE, D), BF16),
             pltpu.VMEM((384, 384), BF16), pltpu.VMEM((TAKE, TAKE), BF16),
+            pltpu.VMEM((384, 3 * TAKE), BF16), pltpu.VMEM((TAKE, D), BF16),
             pltpu.VMEM((8, 384, TAKE), BF16),
-            *[pltpu.VMEM(blocks, BF16)] * 4,
+            pltpu.VMEM((8, ROWS, D), BF16),
             pltpu.VMEM((NX, ROWS, TAKE), BF16),
             pltpu.VMEM((NX, ROWS, 3 * TAKE), BF16),
             pltpu.VMEM((NX, ROWS, 3 * TAKE), F32),
             pltpu.VMEM((NX, ROWS, TAKE), BF16),
             pltpu.VMEM((D, 3 * TAKE), BF16),
-            pltpu.SemaphoreType.DMA((12,)),
-            pltpu.SemaphoreType.DMA((6,)),
+            pltpu.SemaphoreType.DMA((15,)),
+            pltpu.SemaphoreType.DMA((9,)),
         ],
         flops=5 * 10**9,
         moved=12 * 2**20,
         limit=60,
-        far=12,
+        far=15,
         far_out=True,
-    )(*act, *ct, conv_w, point_w, constant(channels.T), constant(inner.T))
+    )(
+        slab, constant(channels), constant(inner), constant(channels.T), constant(inner.T),
+        act[0], act[1], act[3], *act[2], ct[0], ct[1], ct[3], *ct[2],
+    )
     slab_g = lax.all_to_all(grads, SLAB, 0, 0)
 
-    from_left, from_right = step_along_x(to_right, 1), step_along_x(to_left, -1)
-    add = kernel_call(add_kernel, shape(ROWS, D), moved=2**20)
-    out_right = step_along_x(add(out_mid, from_left), 1)
-    act_left = step_along_x(add(act_mid, from_right), -1)
-    slope = kernel_call(slope_kernel, shape(ROWS, D, dtype=F32), flops=10**7, moved=2**20)(tokens[0])
-    output, grad_tokens = kernel_call(
-        out_kernel, [shape(ROWS, D), shape(ROWS, D)], flops=10**7, moved=4 * 2**20
-    )(tokens[0], ct[0], slope, own, from_left, from_right, out_right, act_left)
-
+    out_far, act_far = step_along_x(out2, 1), step_along_x(act2, -1)
+    out_left, act_right = step_along_x(out3, -1), step_along_x(act1, 1)
     line_g = kernel_call(
         line_kernel, shape(32, 24, TAKE),
         scratch=[pltpu.VMEM((384, TAKE), BF16), pltpu.VMEM((32, 24, TAKE), F32)],
         flops=10**8, moved=2**20,
     )(slab_g, constant(conv_rows.T), constant(point_rows.T))
+    add = kernel_call(add_kernel, block, moved=2**20)
+    out_right = step_along_x(add(out1, out_far), 1)
+    act_left = step_along_x(add(act3, act_far), -1)
+    slope = kernel_call(slope_kernel, shape(ROWS, D, dtype=F32), flops=10**7, moved=2**20)(tokens[0])
+    output, grad_tokens = kernel_call(
+        out_kernel, [shape(ROWS, D), shape(ROWS, D)], flops=10**7, moved=4 * 2**20
+    )(tokens[0], cotangent[0], slope, own, out_left, out_right, act_left, act_right)
+
     line_g = lax.all_to_all(line_g, SHEET, 0, 0)
     line_g, output, grad_tokens = lax.optimization_barrier((line_g, output, grad_tokens))
     conv_share, point_share = kernel_call(

time: 104 us -> 98.6 us (0.948); the launches traced: 102 us -> 98 us
  waiting for transfers between devices: 28.6 us -> 24.2 us
  starting transfers between devices: 31.3 us -> 35.1 us
  Pallas kernels: 18.8 us -> 16.7 us
  other arithmetic: 1.32 us -> 0 us
    ppermute x10 -> x14, waiting for transfers between devices: 13.1 us -> 24 us  [step_along_x(): return lax.ppermute(value, 'x', [(i, (i + step) % NX) for i in range(NX)])]
    all_to_all x1, waiting for transfers between devices: 9.59 us -> 0.14 us  [shards(): slab = lax.all_to_all(blocks, SLAB, 0, 0)]
    all_to_all x1, waiting for transfers between devices: 5.86 us -> 0.01 us  [shards(): line_g = lax.all_to_all(line_g, SHEET, 0, 0)]
    ppermute x10 -> x14, starting transfers between devices: 14.3 us -> 17.9 us  [step_along_x(): return lax.ppermute(value, 'x', [(i, (i + step) % NX) for i in range(NX)])]
    pallas_call x10 -> x9, Pallas kernels: 18.8 us -> 16.7 us  [call(): pl.pallas_call(body, out_shape=out_shapes, in_specs=[vmem] * (len(operand...]
    convert_element_type x1 -> x0, other arithmetic: 1.32 us -> none  [shards(): act[0] = gelu_tanh(tokens[0].astype(F32)).astype(BF16)]
  transfers between devices with their start and end apart: 13 -> 17, of which waited for: 4 -> 5; matrix products, arithmetic and copies ran while one was open for 0% -> 0% of each run, Pallas kernels for 8% -> 7%
where the time goes in v4:
time: 98.6 us; the launch traced here: 98 us
  starting transfers between devices  35.1 us (36%)
  waiting for transfers between devices  24.2 us (25%)
  blocking collectives  18.7 us (19%)
  Pallas kernels  16.7 us (17%)
  local copies, waits for them, and re-layouts  2.42 us (2%)
    ppermute x14, waiting for transfers between devices, step_along_x(): return lax.ppermute(value, 'x', [(i, (i + step) % NX) for i in range(NX)])  24 us
    all_to_all x1, blocking collectives, shards(): line = lax.all_to_all(own, SHEET, 0, 0)  18.7 us
    ppermute x14, starting transfers between devices, step_along_x(): return lax.ppermute(value, 'x', [(i, (i + step) % NX) for i in range(NX)])  17.9 us
    pallas_call x9, Pallas kernels, call(): pl.pallas_call(body, out_shape=out_shapes, in_specs=[vmem] * (len(operand...  16.7 us
    all_to_all x1, starting transfers between devices, shards(): slab = lax.all_to_all(blocks, SLAB, 0, 0)  7.84 us
    all_to_all x1, starting transfers between devices, shards(): slab_g = lax.all_to_all(grads, SLAB, 0, 0)  5.39 us
    all_to_all x1, starting transfers between devices, shards(): line_g = lax.all_to_all(line_g, SHEET, 0, 0)  4 us
    unnamed x44, local copies, waits for them, and re-layouts  2.36 us
  transfers between devices with their start and end apart: 17, of which 5 were waited for; matrix products, arithmetic and copies ran while one was open for 0% of the time, Pallas kernels for 7%

profile of v4, /device:TPU:1, one launch (start us, length us, event | category | flops | bytes accessed | tf_op | source)
XLA Modules:
  0.0 98.0 jit_solution(6395638316370351603)
XLA Ops:
  0.6 2.1 %collective-permute-start.3 = (bf16[256,768]{1,0:T(8,128)(2,1)}, bf16[256,768]{1,0:T(8,128)(2,1)S(1)}, u32[]{:S(2)}, u32[]{:S(2)}) collective-permute-start(bf16[256,768]{1,0:T(8,128)(2,1)} %bitcast.6), channel_id=1, source_target_pairs={{0,4},{4,8},{8,12},{12,0},{1,5},{5,9},{9,13},{13,1},{2,6},{6,10},{... | collective-permute-start | bytes 1179656 | tf_op jit(solution)/shard_map/ppermute | solution.py:61
  2.7 1.4 %collective-permute-start.2 = (bf16[256,768]{1,0:T(8,128)(2,1)}, bf16[256,768]{1,0:T(8,128)(2,1)S(1)}, u32[]{:S(2)}, u32[]{:S(2)}) collective-permute-start(bf16[256,768]{1,0:T(8,128)(2,1)} %bitcast.7), channel_id=1, source_target_pairs={{0,12},{4,0},{8,4},{12,8},{1,13},{5,1},{9,5},{13,9},{2,14},{6,2},{... | collective-permute-start | bytes 1179656 | tf_op jit(solution)/shard_map/ppermute | solution.py:61
  4.1 2.5 %shard_map.165 = (bf16[32,24,128]{2,1,0:T(8,128)(2,1)}, bf16[256,768]{1,0:T(8,128)(2,1)}) custom-call(bf16[3,3,512]{2,1,0:T(4,128)(2,1)} %w_conv_far.1, bf16[2,768]{1,0:T(2,128)(2,1)} %w_point_far.1, bf16[512,512]{1,0:T(8,128)(2,1)} %constant.16.clone.order_far.order, bf16[1,256,768]{2,1,0:T(8,128)(2,1)} %tokens_far.1), custom_call_target="tpu_custom_call" | custom-call | flops 10000000 | bytes 2097152 | tf_op jit(solution)/shard_map/pallas_call | solution.py:89
  6.8 2.6 %collective-permute-start = (bf16[256,768]{1,0:T(8,128)(2,1)}, bf16[256,768]{1,0:T(8,128)(2,1)S(1)}, u32[]{:S(2)}, u32[]{:S(2)}) collective-permute-start(bf16[256,768]{1,0:T(8,128)(2,1)} %get-tuple-element.27.refs_0_), channel_id=1, source_target_pairs={{0,12},{4,0},{8,4},{12,8},{1,13},{5,1},{9,5},{13,9},{2,14},{6,2},{... | collective-permute-start | bytes 1179656 | tf_op jit(solution)/shard_map/ppermute | solution.py:61
  9.4 18.7 %all_to_all.20.line = bf16[32,24,128]{2,1,0:T(8,128)(2,1)S(1)} all-to-all(bf16[32,24,128]{2,1,0:T(8,128)(2,1)} %get-tuple-element.26), channel_id=1, replica_groups=mesh['z'=8,'yh'=2,'x'=4,'yl'=2,'core'=2] {'z','x'}, dimensions={0} | all-to-all | bytes 393216 | tf_op jit(solution)/shard_map/all_to_all | solution.py:365
  28.2 1.3 %shard_map.166 = bf16[8,384,128]{2,1,0:T(8,128)(2,1)} custom-call(bf16[32,24,128]{2,1,0:T(8,128)(2,1)S(1)} %all_to_all.20.line, bf16[144,384]{1,0:T(8,128)(2,1)S(1)} %copy-done.8, bf16[96,192]{1,0:T(8,128)(2,1)S(1)} %copy-done.9), custom_call_target="tpu_custom_call" | custom-call | flops 20000000000 | bytes 1048576 | tf_op jit(solution)/shard_map/pallas_call | solution.py:89
  29.6 7.8 %all-to-all-start.1 = ((bf16[8,384,128]{2,1,0:T(8,128)(2,1)}), bf16[8,384,128]{2,1,0:T(8,128)(2,1)S(1)}, u32[]{:S(2)}, u32[]{:S(2)}) async-start(bf16[8,384,128]{2,1,0:T(8,128)(2,1)} %shard_map.166), calls=%async_computation.1 | async-start | bytes 1572864 | tf_op jit(solution)/shard_map/all_to_all | solution.py:381
  37.6 2.7 %collective-permute-start.7 = (bf16[128,768]{1,0:T(8,128)(2,1)S(1)}, bf16[128,768]{1,0:T(8,128)(2,1)S(1)}, u32[]{:S(2)}, u32[]{:S(2)}) collective-permute-start(bf16[128,768]{1,0:T(8,128)(2,1)S(1)} %slice.15), channel_id=1, source_target_pairs={{0,12},{4,0},{8,4},{12,8},{1,13},{5,1},{9,5},{13,9},{2,14},{6,2},{... | collective-permute-start | bytes 589832 | tf_op jit(solution)/shard_map/ppermute | solution.py:61
  40.3 2.7 %collective-permute-start.5 = (bf16[128,768]{1,0:T(8,128)(2,1)S(1)}, bf16[128,768]{1,0:T(8,128)(2,1)S(1)}, u32[]{:S(2)}, u32[]{:S(2)}) collective-permute-start(bf16[128,768]{1,0:T(8,128)(2,1)S(1)} %slice.13), channel_id=1, source_target_pairs={{0,12},{4,0},{8,4},{12,8},{1,13},{5,1},{9,5},{13,9},{2,14},{6,2},{... | collective-permute-start | bytes 589832 | tf_op jit(solution)/shard_map/ppermute | solution.py:61
  43.0 2.4 %collective-permute-done.6.refs_8_ = bf16[128,768]{1,0:T(8,128)(2,1)S(1)} collective-permute-done((bf16[128,768]{1,0:T(8,128)(2,1)S(1)}, bf16[128,768]{1,0:T(8,128)(2,1)S(1)}, u32[]{:S(2)}, u32[]{:S(2)}) %collective-permute-start.6) | collective-permute-done | bytes 196640 | tf_op jit(solution)/shard_map/ppermute | solution.py:61
  45.3 4.2 %collective-permute-done.4.refs_3_ = bf16[128,768]{1,0:T(8,128)(2,1)S(1)} collective-permute-done((bf16[128,768]{1,0:T(8,128)(2,1)S(1)}, bf16[128,768]{1,0:T(8,128)(2,1)S(1)}, u32[]{:S(2)}, u32[]{:S(2)}) %collective-permute-start.4) | collective-permute-done | bytes 196640 | tf_op jit(solution)/shard_map/ppermute | solution.py:61
  50.3 0.9 copy-done.10
  51.2 7.7 %shard_map.167 = (bf16[8,384,128]{2,1,0:T(8,128)(2,1)}, bf16[2,256,768]{2,1,0:T(8,128)(2,1)}, bf16[256,768]{1,0:T(8,128)(2,1)}, bf16[256,768]{1,0:T(8,128)(2,1)}...) custom-call(bf16[8,384,128]{2,1,0:T(8,128)(2,1)} %copy-done.10, ...), custom_call_target="tpu_custom_call" | custom-call | flops 5000000000 | bytes 12582912 | tf_op jit(solution)/shard_map/pallas_call | solution.py:89
  59.0 5.4 %all-to-all-start.2 = ((bf16[8,384,128]{2,1,0:T(8,128)(2,1)}), bf16[8,384,128]{2,1,0:T(8,128)(2,1)S(1)}, u32[]{:S(2)}, u32[]{:S(2)}) async-start(bf16[8,384,128]{2,1,0:T(8,128)(2,1)} %get-tuple-element.33), calls=%async_computation.2 | async-start | bytes 1572864 | tf_op jit(solution)/shard_map/all_to_all | solution.py:411
  64.4 2.7 %collective-permute-start.11 = (bf16[256,768]{1,0:T(8,128)(2,1)S(1)}, bf16[256,768]{1,0:T(8,128)(2,1)S(1)}, u32[]{:S(2)}, u32[]{:S(2)}) collective-permute-start(bf16[256,768]{1,0:T(8,128)(2,1)S(1)} %copy-done.16), channel_id=1, source_target_pairs={{0,12},{4,0},{8,4},{12,8},{1,13},{5,1},{9,5},{13,9},{2,14},{6,2},{... | collective-permute-start | bytes 1179656 | tf_op jit(solution)/shard_map/ppermute | solution.py:61
  67.1 1.4 %collective-permute-start.8 = (bf16[256,768]{1,0:T(8,128)(2,1)}, bf16[256,768]{1,0:T(8,128)(2,1)S(1)}, u32[]{:S(2)}, u32[]{:S(2)}) collective-permute-start(bf16[256,768]{1,0:T(8,128)(2,1)} %get-tuple-element.35), channel_id=1, source_target_pairs={{0,12},{4,0},{8,4},{12,8},{1,13},{5,1},{9,5},{13,9},{2,14},{6,2},{... | collective-permute-start | bytes 1179656 | tf_op jit(solution)/shard_map/ppermute | solution.py:61
  68.5 7.7 %collective-permute-done.9.other = bf16[256,768]{1,0:T(8,128)(2,1)S(1)} collective-permute-done((bf16[256,768]{1,0:T(8,128)(2,1)S(1)}, bf16[256,768]{1,0:T(8,128)(2,1)S(1)}, u32[]{:S(2)}, u32[]{:S(2)}) %collective-permute-start.9) | collective-permute-done | bytes 393248 | tf_op jit(solution)/shard_map/ppermute | solution.py:61
  76.5 0.8 copy-done.3
  77.4 1.9 %collective-permute-start.12 = (bf16[256,768]{1,0:T(8,128)(2,1)S(1)}, bf16[256,768]{1,0:T(8,128)(2,1)}, u32[]{:S(2)}, u32[]{:S(2)}) collective-permute-start(bf16[256,768]{1,0:T(8,128)(2,1)S(1)} %shard_map.171), channel_id=1, source_target_pairs={{0,12},{4,0},{8,4},{12,8},{1,13},{5,1},{9,5},{13,9},{2,14},{6,2},{... | collective-permute-start | bytes 1179656 | tf_op jit(solution)/shard_map/ppermute | solution.py:61
  79.3 1.1 %shard_map.168 = bf16[32,24,128]{2,1,0:T(8,128)(2,1)} custom-call(bf16[8,384,128]{2,1,0:T(8,128)(2,1)S(1)} %all-to-all-done.2.slab, bf16[384,144]{1,0:T(8,128)(2,1)S(1)} %copy-done.6, bf16[192,96]{1,0:T(8,128)(2,1)S(1)} %copy-done.7), custom_call_target="tpu_custom_call" | custom-call | flops 100000000 | bytes 1048576 | tf_op jit(solution)/shard_map/pallas_call | solution.py:89
  80.4 4.0 %all-to-all-start.3 = ((bf16[32,24,128]{2,1,0:T(8,128)(2,1)}), bf16[32,24,128]{2,1,0:T(8,128)(2,1)S(1)}, u32[]{:S(2)}, u32[]{:S(2)}) async-start(bf16[32,24,128]{2,1,0:T(8,128)(2,1)} %shard_map.168), calls=%async_computation.3 | async-start | bytes 393216 | tf_op jit(solution)/shard_map/all_to_all | solution.py:428
  85.0 9.7 %collective-permute-done.10.out_right = bf16[256,768]{1,0:T(8,128)(2,1)} collective-permute-done((bf16[256,768]{1,0:T(8,128)(2,1)S(1)}, bf16[256,768]{1,0:T(8,128)(2,1)}, u32[]{:S(2)}, u32[]{:S(2)}) %collective-permute-start.10) | collective-permute-done | bytes 393248 | tf_op jit(solution)/shard_map/ppermute | solution.py:61
  94.7 2.4 %shard_map.172 = (bf16[256,768]{1,0:T(8,128)(2,1)}, bf16[256,768]{1,0:T(8,128)(2,1)}) custom-call(bf16[256,768]{1,0:T(8,128)(2,1)S(1)} %bitcast.5, bf16[256,768]{1,0:T(8,128)(2,1)S(1)} %bitcast.9, f32[256,768]{1,0:T(8,128)S(1)} %shard_map.169.slope, bf16[2,256,768]{2,1,0:T(8,128)(2,1)S(1)} %copy-done.2, ...), custom_call_target="tpu_custom_call" | custom-call | flops 10000000 | bytes 4194304 | tf_op jit(solution)/shard_map/pallas_call | solution.py:89
  97.1 0.9 shard_map.173
  (68 shorter events, 2.0 us)
Async XLA Ops:
  0.6 27.5 %collective-permute-start.3 = (bf16[256,768]{1,0:T(8,128)(2,1)}, bf16[256,768]{1,0:T(8,128)(2,1)S(1)}, u32[]{:S(2)}, u32[]{:S(2)}) collective-permute-start(bf16[256,768]{1,0:T(8,128)(2,1)} %bitcast.6), channel_id=1, source_target_pairs={{0,4},{4,8},{8,12},{12,0},{1,5},{5,9},{9,13},{13,1},{2,6},{6,10},{... | collective-permute-start | bytes 1179656 | tf_op jit(solution)/shard_map/ppermute | solution.py:61
  2.7 25.4 %collective-permute-start.2 = (bf16[256,768]{1,0:T(8,128)(2,1)}, bf16[256,768]{1,0:T(8,128)(2,1)S(1)}, u32[]{:S(2)}, u32[]{:S(2)}) collective-permute-start(bf16[256,768]{1,0:T(8,128)(2,1)} %bitcast.7), channel_id=1, source_target_pairs={{0,12},{4,0},{8,4},{12,8},{1,13},{5,1},{9,5},{13,9},{2,14},{6,2},{... | collective-permute-start | bytes 1179656 | tf_op jit(solution)/shard_map/ppermute | solution.py:61
  6.7 21.5 %collective-permute-start.1 = (bf16[256,768]{1,0:T(8,128)(2,1)}, bf16[256,768]{1,0:T(8,128)(2,1)S(1)}, u32[]{:S(2)}, u32[]{:S(2)}) collective-permute-start(bf16[256,768]{1,0:T(8,128)(2,1)} %get-tuple-element.27.refs_0_), channel_id=1, source_target_pairs={{0,4},{4,8},{8,12},{12,0},{1,5},{5,9},{9,13},{13,1},{2,6},{6,10},{... | collective-permute-start | bytes 1179656 | tf_op jit(solution)/shard_map/ppermute | solution.py:61
  6.8 21.3 %collective-permute-start = (bf16[256,768]{1,0:T(8,128)(2,1)}, bf16[256,768]{1,0:T(8,128)(2,1)S(1)}, u32[]{:S(2)}, u32[]{:S(2)}) collective-permute-start(bf16[256,768]{1,0:T(8,128)(2,1)} %get-tuple-element.27.refs_0_), channel_id=1, source_target_pairs={{0,12},{4,0},{8,4},{12,8},{1,13},{5,1},{9,5},{13,9},{2,14},{6,2},{... | collective-permute-start | bytes 1179656 | tf_op jit(solution)/shard_map/ppermute | solution.py:61
  9.4 18.8 %copy-start.8 = (bf16[144,384]{1,0:T(8,128)(2,1)S(1)}, bf16[144,384]{1,0:T(8,128)(2,1)}, u32[]{:S(2)}) copy-start(bf16[144,384]{1,0:T(8,128)(2,1)} %constant.17.clone.conv_order) | copy-start | bytes 331780
  9.4 18.8 %copy-start.9 = (bf16[96,192]{1,0:T(8,128)(2,1)S(1)}, bf16[96,192]{1,0:T(8,128)(2,1)}, u32[]{:S(2)}) copy-start(bf16[96,192]{1,0:T(8,128)(2,1)} %constant.18.clone.point_order) | copy-start | bytes 110596
  28.1 9.3 %copy-start.11 = (bf16[256,768]{1,0:T(8,128)(2,1)}, bf16[256,768]{1,0:T(8,128)(2,1)S(1)}, u32[]{:S(2)}) copy-start(bf16[256,768]{1,0:T(8,128)(2,1)S(1)} %collective-permute-done.3.refs_7_) | copy-start | bytes 1179652
  29.6 20.1 %all-to-all-start.1 = ((bf16[8,384,128]{2,1,0:T(8,128)(2,1)}), bf16[8,384,128]{2,1,0:T(8,128)(2,1)S(1)}, u32[]{:S(2)}, u32[]{:S(2)}) async-start(bf16[8,384,128]{2,1,0:T(8,128)(2,1)} %shard_map.166), calls=%async_computation.1 | async-start | bytes 1572864 | tf_op jit(solution)/shard_map/all_to_all | solution.py:381
  37.5 7.8 %collective-permute-start.6 = (bf16[128,768]{1,0:T(8,128)(2,1)S(1)}, bf16[128,768]{1,0:T(8,128)(2,1)S(1)}, u32[]{:S(2)}, u32[]{:S(2)}) collective-permute-start(bf16[128,768]{1,0:T(8,128)(2,1)S(1)} %slice.14), channel_id=1, source_target_pairs={{0,4},{4,8},{8,12},{12,0},{1,5},{5,9},{9,13},{13,1},{2,6},{6,10},{... | collective-permute-start | bytes 589832 | tf_op jit(solution)/shard_map/ppermute | solution.py:61
  37.6 7.7 %collective-permute-start.7 = (bf16[128,768]{1,0:T(8,128)(2,1)S(1)}, bf16[128,768]{1,0:T(8,128)(2,1)S(1)}, u32[]{:S(2)}, u32[]{:S(2)}) collective-permute-start(bf16[128,768]{1,0:T(8,128)(2,1)S(1)} %slice.15), channel_id=1, source_target_pairs={{0,12},{4,0},{8,4},{12,8},{1,13},{5,1},{9,5},{13,9},{2,14},{6,2},{... | collective-permute-start | bytes 589832 | tf_op jit(solution)/shard_map/ppermute | solution.py:61
  40.3 9.3 %collective-permute-start.4 = (bf16[128,768]{1,0:T(8,128)(2,1)S(1)}, bf16[128,768]{1,0:T(8,128)(2,1)S(1)}, u32[]{:S(2)}, u32[]{:S(2)}) collective-permute-start(bf16[128,768]{1,0:T(8,128)(2,1)S(1)} %slice.12), channel_id=1, source_target_pairs={{0,4},{4,8},{8,12},{12,0},{1,5},{5,9},{9,13},{13,1},{2,6},{6,10},{... | collective-permute-start | bytes 589832 | tf_op jit(solution)/shard_map/ppermute | solution.py:61
  40.3 9.3 %collective-permute-start.5 = (bf16[128,768]{1,0:T(8,128)(2,1)S(1)}, bf16[128,768]{1,0:T(8,128)(2,1)S(1)}, u32[]{:S(2)}, u32[]{:S(2)}) collective-permute-start(bf16[128,768]{1,0:T(8,128)(2,1)S(1)} %slice.13), channel_id=1, source_target_pairs={{0,12},{4,0},{8,4},{12,8},{1,13},{5,1},{9,5},{13,9},{2,14},{6,2},{... | collective-permute-start | bytes 589832 | tf_op jit(solution)/shard_map/ppermute | solution.py:61
  58.9 9.5 %copy-start.15 = (bf16[256,768]{1,0:T(8,128)(2,1)S(1)}, bf16[256,768]{1,0:T(8,128)(2,1)}, u32[]{:S(2)}) copy-start(bf16[256,768]{1,0:T(8,128)(2,1)} %get-tuple-element.40) | copy-start | bytes 1179652
  59.0 17.3 %copy-start.4 = (bf16[256,768]{1,0:T(8,128)(2,1)S(1)}, bf16[256,768]{1,0:T(8,128)(2,1)}, u32[]{:S(2)}) copy-start(bf16[256,768]{1,0:T(8,128)(2,1)} %get-tuple-element.36.mine) | copy-start | bytes 1179652
  59.0 20.3 %all-to-all-start.2 = ((bf16[8,384,128]{2,1,0:T(8,128)(2,1)}), bf16[8,384,128]{2,1,0:T(8,128)(2,1)S(1)}, u32[]{:S(2)}, u32[]{:S(2)}) async-start(bf16[8,384,128]{2,1,0:T(8,128)(2,1)} %get-tuple-element.33), calls=%async_computation.2 | async-start | bytes 1572864 | tf_op jit(solution)/shard_map/all_to_all | solution.py:411
  64.4 11.9 %collective-permute-start.9 = (bf16[256,768]{1,0:T(8,128)(2,1)S(1)}, bf16[256,768]{1,0:T(8,128)(2,1)S(1)}, u32[]{:S(2)}, u32[]{:S(2)}) collective-permute-start(bf16[256,768]{1,0:T(8,128)(2,1)S(1)} %copy-done.17), channel_id=1, source_target_pairs={{0,4},{4,8},{8,12},{12,0},{1,5},{5,9},{9,13},{13,1},{2,6},{6,10},{... | collective-permute-start | bytes 1179656 | tf_op jit(solution)/shard_map/ppermute | solution.py:61
  64.4 12.1 %collective-permute-start.11 = (bf16[256,768]{1,0:T(8,128)(2,1)S(1)}, bf16[256,768]{1,0:T(8,128)(2,1)S(1)}, u32[]{:S(2)}, u32[]{:S(2)}) collective-permute-start(bf16[256,768]{1,0:T(8,128)(2,1)S(1)} %copy-done.16), channel_id=1, source_target_pairs={{0,12},{4,0},{8,4},{12,8},{1,13},{5,1},{9,5},{13,9},{2,14},{6,2},{... | collective-permute-start | bytes 1179656 | tf_op jit(solution)/shard_map/ppermute | solution.py:61
  67.1 17.9 %collective-permute-start.8 = (bf16[256,768]{1,0:T(8,128)(2,1)}, bf16[256,768]{1,0:T(8,128)(2,1)S(1)}, u32[]{:S(2)}, u32[]{:S(2)}) collective-permute-start(bf16[256,768]{1,0:T(8,128)(2,1)} %get-tuple-element.35), channel_id=1, source_target_pairs={{0,12},{4,0},{8,4},{12,8},{1,13},{5,1},{9,5},{13,9},{2,14},{6,2},{... | collective-permute-start | bytes 1179656 | tf_op jit(solution)/shard_map/ppermute | solution.py:61
  68.5 16.5 %collective-permute-start.13 = (bf16[256,768]{1,0:T(8,128)(2,1)S(1)}, bf16[256,768]{1,0:T(8,128)(2,1)S(1)}, u32[]{:S(2)}, u32[]{:S(2)}) collective-permute-start(bf16[256,768]{1,0:T(8,128)(2,1)S(1)} %copy-done.15), channel_id=1, source_target_pairs={{0,4},{4,8},{8,12},{12,0},{1,5},{5,9},{9,13},{13,1},{2,6},{6,10},{... | collective-permute-start | bytes 1179656 | tf_op jit(solution)/shard_map/ppermute | solution.py:61
  76.4 18.3 %collective-permute-start.10 = (bf16[256,768]{1,0:T(8,128)(2,1)S(1)}, bf16[256,768]{1,0:T(8,128)(2,1)}, u32[]{:S(2)}, u32[]{:S(2)}) collective-permute-start(bf16[256,768]{1,0:T(8,128)(2,1)S(1)} %shard_map.170), channel_id=1, source_target_pairs={{0,4},{4,8},{8,12},{12,0},{1,5},{5,9},{9,13},{13,1},{2,6},{6,10},{... | collective-permute-start | bytes 1179656 | tf_op jit(solution)/shard_map/ppermute | solution.py:61
  77.4 17.3 %collective-permute-start.12 = (bf16[256,768]{1,0:T(8,128)(2,1)S(1)}, bf16[256,768]{1,0:T(8,128)(2,1)}, u32[]{:S(2)}, u32[]{:S(2)}) collective-permute-start(bf16[256,768]{1,0:T(8,128)(2,1)S(1)} %shard_map.171), channel_id=1, source_target_pairs={{0,12},{4,0},{8,4},{12,8},{1,13},{5,1},{9,5},{13,9},{2,14},{6,2},{... | collective-permute-start | bytes 1179656 | tf_op jit(solution)/shard_map/ppermute | solution.py:61
  80.4 14.2 %copy-start.2 = (bf16[2,256,768]{2,1,0:T(8,128)(2,1)S(1)}, bf16[2,256,768]{2,1,0:T(8,128)(2,1)}, u32[]{:S(2)}) copy-start(bf16[2,256,768]{2,1,0:T(8,128)(2,1)} %get-tuple-element.34.own) | copy-start | bytes 2359300
  80.4 16.7 %all-to-all-start.3 = ((bf16[32,24,128]{2,1,0:T(8,128)(2,1)}), bf16[32,24,128]{2,1,0:T(8,128)(2,1)S(1)}, u32[]{:S(2)}, u32[]{:S(2)}) async-start(bf16[32,24,128]{2,1,0:T(8,128)(2,1)} %shard_map.168), calls=%async_computation.3 | async-start | bytes 393216 | tf_op jit(solution)/shard_map/all_to_all | solution.py:428
  84.4 10.2 %copy-start.5 = (bf16[1,256,768]{2,1,0:T(8,128)(2,1)S(1)}, bf16[1,256,768]{2,1,0:T(8,128)(2,1)}, u32[]{:S(2)}) copy-start(bf16[1,256,768]{2,1,0:T(8,128)(2,1)} %param.15) | copy-start | bytes 1179652
  (15 other events, 61.2 us)

commit v5 on v4

--- a/solution.py
+++ b/solution.py
@@ -417,7 +417,8 @@
         scratch=[pltpu.VMEM((384, TAKE), BF16), pltpu.VMEM((32, 24, TAKE), F32)],
         flops=10**8, moved=2**20,
     )(slab_g, constant(conv_rows.T), constant(point_rows.T))
-    add = kernel_call(add_kernel, block, moved=2**20)
+    out_far, act_far = lax.optimization_barrier((out_far, act_far))
+    add = kernel_call(add_kernel, block, flops=3 * 10**9, moved=2**20)
     out_right = step_along_x(add(out1, out_far), 1)
     act_left = step_along_x(add(act3, act_far), -1)
     slope = kernel_call(slope_kernel, shape(ROWS, D, dtype=F32), flops=10**7, moved=2**20)(tokens[0])

time: 98.6 us -> 96.9 us (0.983)
  waiting for transfers between devices: 24.2 us -> 21.6 us
  starting transfers between devices: 35.1 us -> 36.3 us
    ppermute x14, waiting for transfers between devices: 24 us -> 10.8 us  [step_along_x(): return lax.ppermute(value, 'x', [(i, (i + step) % NX) for i in range(NX)])]
    all_to_all x1, waiting for transfers between devices: 0.01 us -> 5.6 us  [shards(): slab_g = lax.all_to_all(grads, SLAB, 0, 0)]
    all_to_all x1, waiting for transfers between devices: 0.01 us -> 5.08 us  [shards(): line_g = lax.all_to_all(line_g, SHEET, 0, 0)]
    unnamed x44 -> x40, local copies, waits for them, and re-layouts: 2.36 us -> 1.56 us
  transfers between devices with their start and end apart: 17 -> 17, of which waited for: 5 -> 8; matrix products, arithmetic and copies ran while one was open for 0% -> 0% of each run, Pallas kernels for 7% -> 7%
where the time goes in v5:
time: 96.9 us; the launch traced here: 96.1 us
  starting transfers between devices  36.3 us (37%)
  waiting for transfers between devices  21.6 us (22%)
  blocking collectives  18.7 us (19%)
  Pallas kernels  17 us (18%)
  local copies, waits for them, and re-layouts  1.61 us (2%)
    all_to_all x1, blocking collectives, shards(): line = lax.all_to_all(own, SHEET, 0, 0)  18.7 us
    ppermute x14, starting transfers between devices, step_along_x(): return lax.ppermute(value, 'x', [(i, (i + step) % NX) for i in range(NX)])  18.2 us
    pallas_call x9, Pallas kernels, call(): pl.pallas_call(body, out_shape=out_shapes, in_specs=[vmem] * (len(operand...  17 us
    ppermute x14, waiting for transfers between devices, step_along_x(): return lax.ppermute(value, 'x', [(i, (i + step) % NX) for i in range(NX)])  10.8 us
    all_to_all x1, starting transfers between devices, shards(): slab = lax.all_to_all(blocks, SLAB, 0, 0)  7.84 us
    all_to_all x1, starting transfers between devices, shards(): slab_g = lax.all_to_all(grads, SLAB, 0, 0)  5.94 us
    all_to_all x1, waiting for transfers between devices, shards(): slab_g = lax.all_to_all(grads, SLAB, 0, 0)  5.6 us
    all_to_all x1, waiting for transfers between devices, shards(): line_g = lax.all_to_all(line_g, SHEET, 0, 0)  5.08 us
  transfers between devices with their start and end apart: 17, of which 8 were waited for; matrix products, arithmetic and copies ran while one was open for 0% of the time, Pallas kernels for 7%

profile of v5, /device:TPU:1, one launch (start us, length us, event | category | flops | bytes accessed | tf_op | source)
XLA Modules:
  0.0 96.1 jit_solution(11490223693826789989)
XLA Ops:
  0.6 2.1 %collective-permute-start.3 = (bf16[256,768]{1,0:T(8,128)(2,1)}, bf16[256,768]{1,0:T(8,128)(2,1)S(1)}, u32[]{:S(2)}, u32[]{:S(2)}) collective-permute-start(bf16[256,768]{1,0:T(8,128)(2,1)} %bitcast.6), channel_id=1, source_target_pairs={{0,4},{4,8},{8,12},{12,0},{1,5},{5,9},{9,13},{13,1},{2,6},{6,10},{... | collective-permute-start | bytes 1179656 | tf_op jit(solution)/shard_map/ppermute | solution.py:61
  2.7 1.4 %collective-permute-start.2 = (bf16[256,768]{1,0:T(8,128)(2,1)}, bf16[256,768]{1,0:T(8,128)(2,1)S(1)}, u32[]{:S(2)}, u32[]{:S(2)}) collective-permute-start(bf16[256,768]{1,0:T(8,128)(2,1)} %bitcast.7), channel_id=1, source_target_pairs={{0,12},{4,0},{8,4},{12,8},{1,13},{5,1},{9,5},{13,9},{2,14},{6,2},{... | collective-permute-start | bytes 1179656 | tf_op jit(solution)/shard_map/ppermute | solution.py:61
  4.1 2.5 %shard_map.165 = (bf16[32,24,128]{2,1,0:T(8,128)(2,1)}, bf16[256,768]{1,0:T(8,128)(2,1)}) custom-call(bf16[3,3,512]{2,1,0:T(4,128)(2,1)} %w_conv_far.1, bf16[2,768]{1,0:T(2,128)(2,1)} %w_point_far.1, bf16[512,512]{1,0:T(8,128)(2,1)} %constant.16.clone.order_far.order, bf16[1,256,768]{2,1,0:T(8,128)(2,1)} %tokens_far.1), custom_call_target="tpu_custom_call" | custom-call | flops 10000000 | bytes 2097152 | tf_op jit(solution)/shard_map/pallas_call | solution.py:89
  6.8 2.6 %collective-permute-start = (bf16[256,768]{1,0:T(8,128)(2,1)}, bf16[256,768]{1,0:T(8,128)(2,1)S(1)}, u32[]{:S(2)}, u32[]{:S(2)}) collective-permute-start(bf16[256,768]{1,0:T(8,128)(2,1)} %get-tuple-element.29.refs_0_), channel_id=1, source_target_pairs={{0,12},{4,0},{8,4},{12,8},{1,13},{5,1},{9,5},{13,9},{2,14},{6,2},{... | collective-permute-start | bytes 1179656 | tf_op jit(solution)/shard_map/ppermute | solution.py:61
  9.4 18.7 %all_to_all.20.line = bf16[32,24,128]{2,1,0:T(8,128)(2,1)S(1)} all-to-all(bf16[32,24,128]{2,1,0:T(8,128)(2,1)} %get-tuple-element.28), channel_id=1, replica_groups=mesh['z'=8,'yh'=2,'x'=4,'yl'=2,'core'=2] {'z','x'}, dimensions={0} | all-to-all | bytes 393216 | tf_op jit(solution)/shard_map/all_to_all | solution.py:365
  28.2 1.3 %shard_map.166 = bf16[8,384,128]{2,1,0:T(8,128)(2,1)} custom-call(bf16[32,24,128]{2,1,0:T(8,128)(2,1)S(1)} %all_to_all.20.line, bf16[144,384]{1,0:T(8,128)(2,1)S(1)} %copy-done.6, bf16[96,192]{1,0:T(8,128)(2,1)S(1)} %copy-done.7), custom_call_target="tpu_custom_call" | custom-call | flops 20000000000 | bytes 1048576 | tf_op jit(solution)/shard_map/pallas_call | solution.py:89
  29.6 7.8 %all-to-all-start.1 = ((bf16[8,384,128]{2,1,0:T(8,128)(2,1)}), bf16[8,384,128]{2,1,0:T(8,128)(2,1)S(1)}, u32[]{:S(2)}, u32[]{:S(2)}) async-start(bf16[8,384,128]{2,1,0:T(8,128)(2,1)} %shard_map.166), calls=%async_computation.1 | async-start | bytes 1572864 | tf_op jit(solution)/shard_map/all_to_all | solution.py:381
  37.6 2.7 %collective-permute-start.7 = (bf16[128,768]{1,0:T(8,128)(2,1)S(1)}, bf16[128,768]{1,0:T(8,128)(2,1)S(1)}, u32[]{:S(2)}, u32[]{:S(2)}) collective-permute-start(bf16[128,768]{1,0:T(8,128)(2,1)S(1)} %slice.15), channel_id=1, source_target_pairs={{0,12},{4,0},{8,4},{12,8},{1,13},{5,1},{9,5},{13,9},{2,14},{6,2},{... | collective-permute-start | bytes 589832 | tf_op jit(solution)/shard_map/ppermute | solution.py:61
  40.3 2.7 %collective-permute-start.5 = (bf16[128,768]{1,0:T(8,128)(2,1)S(1)}, bf16[128,768]{1,0:T(8,128)(2,1)S(1)}, u32[]{:S(2)}, u32[]{:S(2)}) collective-permute-start(bf16[128,768]{1,0:T(8,128)(2,1)S(1)} %slice.13), channel_id=1, source_target_pairs={{0,12},{4,0},{8,4},{12,8},{1,13},{5,1},{9,5},{13,9},{2,14},{6,2},{... | collective-permute-start | bytes 589832 | tf_op jit(solution)/shard_map/ppermute | solution.py:61
  43.0 2.4 %collective-permute-done.6.refs_8_ = bf16[128,768]{1,0:T(8,128)(2,1)S(1)} collective-permute-done((bf16[128,768]{1,0:T(8,128)(2,1)S(1)}, bf16[128,768]{1,0:T(8,128)(2,1)S(1)}, u32[]{:S(2)}, u32[]{:S(2)}) %collective-permute-start.6) | collective-permute-done | bytes 196640 | tf_op jit(solution)/shard_map/ppermute | solution.py:61
  45.3 4.2 %collective-permute-done.4.refs_3_ = bf16[128,768]{1,0:T(8,128)(2,1)S(1)} collective-permute-done((bf16[128,768]{1,0:T(8,128)(2,1)S(1)}, bf16[128,768]{1,0:T(8,128)(2,1)S(1)}, u32[]{:S(2)}, u32[]{:S(2)}) %collective-permute-start.4) | collective-permute-done | bytes 196640 | tf_op jit(solution)/shard_map/ppermute | solution.py:61
  51.2 7.7 %shard_map.167 = (bf16[8,384,128]{2,1,0:T(8,128)(2,1)}, bf16[2,256,768]{2,1,0:T(8,128)(2,1)}, bf16[256,768]{1,0:T(8,128)(2,1)}, bf16[256,768]{1,0:T(8,128)(2,1)}...) custom-call(bf16[8,384,128]{2,1,0:T(8,128)(2,1)} %copy-done.10, ...), custom_call_target="tpu_custom_call" | custom-call | flops 5000000000 | bytes 12582912 | tf_op jit(solution)/shard_map/pallas_call | solution.py:89
  59.0 2.7 %collective-permute-start.10 = (bf16[256,768]{1,0:T(8,128)(2,1)}, bf16[256,768]{1,0:T(8,128)(2,1)S(1)}, u32[]{:S(2)}, u32[]{:S(2)}) collective-permute-start(bf16[256,768]{1,0:T(8,128)(2,1)} %get-tuple-element.40), channel_id=1, source_target_pairs={{0,12},{4,0},{8,4},{12,8},{1,13},{5,1},{9,5},{13,9},{2,14},{6,2},{... | collective-permute-start | bytes 1179656 | tf_op jit(solution)/shard_map/ppermute | solution.py:61
  61.7 5.9 %all-to-all-start.2 = ((bf16[8,384,128]{2,1,0:T(8,128)(2,1)}), bf16[8,384,128]{2,1,0:T(8,128)(2,1)S(1)}, u32[]{:S(2)}, u32[]{:S(2)}) async-start(bf16[8,384,128]{2,1,0:T(8,128)(2,1)} %get-tuple-element.35), calls=%async_computation.2 | async-start | bytes 1572864 | tf_op jit(solution)/shard_map/all_to_all | solution.py:411
  67.6 1.4 %collective-permute-start.8 = (bf16[256,768]{1,0:T(8,128)(2,1)}, bf16[256,768]{1,0:T(8,128)(2,1)S(1)}, u32[]{:S(2)}, u32[]{:S(2)}) collective-permute-start(bf16[256,768]{1,0:T(8,128)(2,1)} %get-tuple-element.37), channel_id=1, source_target_pairs={{0,12},{4,0},{8,4},{12,8},{1,13},{5,1},{9,5},{13,9},{2,14},{6,2},{... | collective-permute-start | bytes 1179656 | tf_op jit(solution)/shard_map/ppermute | solution.py:61
  69.1 1.2 %collective-permute-done.9.other = bf16[256,768]{1,0:T(8,128)(2,1)S(1)} collective-permute-done((bf16[256,768]{1,0:T(8,128)(2,1)}, bf16[256,768]{1,0:T(8,128)(2,1)S(1)}, u32[]{:S(2)}, u32[]{:S(2)}) %collective-permute-start.9) | collective-permute-done | bytes 393248 | tf_op jit(solution)/shard_map/ppermute | solution.py:61
  71.1 2.4 %collective-permute-start.12 = (bf16[256,768]{1,0:T(8,128)(2,1)}, bf16[256,768]{1,0:T(8,128)(2,1)S(1)}, u32[]{:S(2)}, u32[]{:S(2)}) collective-permute-start(bf16[256,768]{1,0:T(8,128)(2,1)} %shard_map.171), channel_id=1, source_target_pairs={{0,12},{4,0},{8,4},{12,8},{1,13},{5,1},{9,5},{13,9},{2,14},{6,2},{... | collective-permute-start | bytes 1179656 | tf_op jit(solution)/shard_map/ppermute | solution.py:61
  74.3 5.6 %all-to-all-done.2.slab = bf16[8,384,128]{2,1,0:T(8,128)(2,1)S(1)} async-done(((bf16[8,384,128]{2,1,0:T(8,128)(2,1)}), bf16[8,384,128]{2,1,0:T(8,128)(2,1)S(1)}, u32[]{:S(2)}, u32[]{:S(2)}) %all-to-all-start.2) | async-done | bytes 786464 | tf_op jit(solution)/shard_map/all_to_all | solution.py:411
  79.9 1.1 %shard_map.168 = bf16[32,24,128]{2,1,0:T(8,128)(2,1)} custom-call(bf16[8,384,128]{2,1,0:T(8,128)(2,1)S(1)} %all-to-all-done.2.slab, bf16[384,144]{1,0:T(8,128)(2,1)S(1)} %copy-done.4, bf16[192,96]{1,0:T(8,128)(2,1)S(1)} %copy-done.5), custom_call_target="tpu_custom_call" | custom-call | flops 100000000 | bytes 1048576 | tf_op jit(solution)/shard_map/pallas_call | solution.py:89
  81.0 4.3 %all-to-all-start.3 = ((bf16[32,24,128]{2,1,0:T(8,128)(2,1)}), bf16[32,24,128]{2,1,0:T(8,128)(2,1)S(1)}, u32[]{:S(2)}, u32[]{:S(2)}) async-start(bf16[32,24,128]{2,1,0:T(8,128)(2,1)} %shard_map.168), calls=%async_computation.3 | async-start | bytes 393216 | tf_op jit(solution)/shard_map/all_to_all | solution.py:429
  85.8 1.2 %collective-permute-done.12.act_left = bf16[256,768]{1,0:T(8,128)(2,1)S(1)} collective-permute-done((bf16[256,768]{1,0:T(8,128)(2,1)}, bf16[256,768]{1,0:T(8,128)(2,1)S(1)}, u32[]{:S(2)}, u32[]{:S(2)}) %collective-permute-start.12) | collective-permute-done | bytes 393248 | tf_op jit(solution)/shard_map/ppermute | solution.py:61
  87.0 1.9 %collective-permute-done.11.out_right = bf16[256,768]{1,0:T(8,128)(2,1)S(1)} collective-permute-done((bf16[256,768]{1,0:T(8,128)(2,1)}, bf16[256,768]{1,0:T(8,128)(2,1)S(1)}, u32[]{:S(2)}, u32[]{:S(2)}) %collective-permute-start.11) | collective-permute-done | bytes 393248 | tf_op jit(solution)/shard_map/ppermute | solution.py:61
  88.9 1.2 %shard_map.172 = (bf16[256,768]{1,0:T(8,128)(2,1)}, bf16[256,768]{1,0:T(8,128)(2,1)}) custom-call(bf16[256,768]{1,0:T(8,128)(2,1)S(1)} %bitcast.5, bf16[256,768]{1,0:T(8,128)(2,1)S(1)} %bitcast.9, f32[256,768]{1,0:T(8,128)S(1)} %shard_map.169.slope, bf16[2,256,768]{2,1,0:T(8,128)(2,1)S(1)} %copy-done.2, ...), custom_call_target="tpu_custom_call" | custom-call | flops 10000000 | bytes 4194304 | tf_op jit(solution)/shard_map/pallas_call | solution.py:89
  90.1 5.1 %all-to-all-done.3.line = bf16[32,24,128]{2,1,0:T(8,128)(2,1)S(1)} async-done(((bf16[32,24,128]{2,1,0:T(8,128)(2,1)}), bf16[32,24,128]{2,1,0:T(8,128)(2,1)S(1)}, u32[]{:S(2)}, u32[]{:S(2)}) %all-to-all-start.3) | async-done | bytes 196640 | tf_op jit(solution)/shard_map/all_to_all | solution.py:429
  (64 shorter events, 5.2 us)
Async XLA Ops:
  0.6 27.5 %collective-permute-start.3 = (bf16[256,768]{1,0:T(8,128)(2,1)}, bf16[256,768]{1,0:T(8,128)(2,1)S(1)}, u32[]{:S(2)}, u32[]{:S(2)}) collective-permute-start(bf16[256,768]{1,0:T(8,128)(2,1)} %bitcast.6), channel_id=1, source_target_pairs={{0,4},{4,8},{8,12},{12,0},{1,5},{5,9},{9,13},{13,1},{2,6},{6,10},{... | collective-permute-start | bytes 1179656 | tf_op jit(solution)/shard_map/ppermute | solution.py:61
  2.7 25.4 %collective-permute-start.2 = (bf16[256,768]{1,0:T(8,128)(2,1)}, bf16[256,768]{1,0:T(8,128)(2,1)S(1)}, u32[]{:S(2)}, u32[]{:S(2)}) collective-permute-start(bf16[256,768]{1,0:T(8,128)(2,1)} %bitcast.7), channel_id=1, source_target_pairs={{0,12},{4,0},{8,4},{12,8},{1,13},{5,1},{9,5},{13,9},{2,14},{6,2},{... | collective-permute-start | bytes 1179656 | tf_op jit(solution)/shard_map/ppermute | solution.py:61
  6.7 21.5 %collective-permute-start.1 = (bf16[256,768]{1,0:T(8,128)(2,1)}, bf16[256,768]{1,0:T(8,128)(2,1)S(1)}, u32[]{:S(2)}, u32[]{:S(2)}) collective-permute-start(bf16[256,768]{1,0:T(8,128)(2,1)} %get-tuple-element.29.refs_0_), channel_id=1, source_target_pairs={{0,4},{4,8},{8,12},{12,0},{1,5},{5,9},{9,13},{13,1},{2,6},{6,10},{... | collective-permute-start | bytes 1179656 | tf_op jit(solution)/shard_map/ppermute | solution.py:61
  6.8 21.3 %collective-permute-start = (bf16[256,768]{1,0:T(8,128)(2,1)}, bf16[256,768]{1,0:T(8,128)(2,1)S(1)}, u32[]{:S(2)}, u32[]{:S(2)}) collective-permute-start(bf16[256,768]{1,0:T(8,128)(2,1)} %get-tuple-element.29.refs_0_), channel_id=1, source_target_pairs={{0,12},{4,0},{8,4},{12,8},{1,13},{5,1},{9,5},{13,9},{2,14},{6,2},{... | collective-permute-start | bytes 1179656 | tf_op jit(solution)/shard_map/ppermute | solution.py:61
  9.4 18.8 %copy-start.6 = (bf16[144,384]{1,0:T(8,128)(2,1)S(1)}, bf16[144,384]{1,0:T(8,128)(2,1)}, u32[]{:S(2)}) copy-start(bf16[144,384]{1,0:T(8,128)(2,1)} %constant.17.clone.conv_order) | copy-start | bytes 331780
  9.4 18.8 %copy-start.7 = (bf16[96,192]{1,0:T(8,128)(2,1)S(1)}, bf16[96,192]{1,0:T(8,128)(2,1)}, u32[]{:S(2)}) copy-start(bf16[96,192]{1,0:T(8,128)(2,1)} %constant.18.clone.point_order) | copy-start | bytes 110596
  28.1 9.3 %copy-start.11 = (bf16[256,768]{1,0:T(8,128)(2,1)}, bf16[256,768]{1,0:T(8,128)(2,1)S(1)}, u32[]{:S(2)}) copy-start(bf16[256,768]{1,0:T(8,128)(2,1)S(1)} %collective-permute-done.3.refs_7_) | copy-start | bytes 1179652
  28.2 9.3 %copy-start.12 = (bf16[256,768]{1,0:T(8,128)(2,1)}, bf16[256,768]{1,0:T(8,128)(2,1)S(1)}, u32[]{:S(2)}) copy-start(bf16[256,768]{1,0:T(8,128)(2,1)S(1)} %collective-permute-done.2.refs_6_) | copy-start | bytes 1179652
  28.2 9.3 %copy-start.13 = (bf16[256,768]{1,0:T(8,128)(2,1)}, bf16[256,768]{1,0:T(8,128)(2,1)S(1)}, u32[]{:S(2)}) copy-start(bf16[256,768]{1,0:T(8,128)(2,1)S(1)} %collective-permute-done.1.refs_2_) | copy-start | bytes 1179652
  28.2 9.2 %copy-start.14 = (bf16[256,768]{1,0:T(8,128)(2,1)}, bf16[256,768]{1,0:T(8,128)(2,1)S(1)}, u32[]{:S(2)}) copy-start(bf16[256,768]{1,0:T(8,128)(2,1)S(1)} %collective-permute-done.refs_1_) | copy-start | bytes 1179652
  29.6 20.1 %all-to-all-start.1 = ((bf16[8,384,128]{2,1,0:T(8,128)(2,1)}), bf16[8,384,128]{2,1,0:T(8,128)(2,1)S(1)}, u32[]{:S(2)}, u32[]{:S(2)}) async-start(bf16[8,384,128]{2,1,0:T(8,128)(2,1)} %shard_map.166), calls=%async_computation.1 | async-start | bytes 1572864 | tf_op jit(solution)/shard_map/all_to_all | solution.py:381
  37.5 7.8 %collective-permute-start.6 = (bf16[128,768]{1,0:T(8,128)(2,1)S(1)}, bf16[128,768]{1,0:T(8,128)(2,1)S(1)}, u32[]{:S(2)}, u32[]{:S(2)}) collective-permute-start(bf16[128,768]{1,0:T(8,128)(2,1)S(1)} %slice.14), channel_id=1, source_target_pairs={{0,4},{4,8},{8,12},{12,0},{1,5},{5,9},{9,13},{13,1},{2,6},{6,10},{... | collective-permute-start | bytes 589832 | tf_op jit(solution)/shard_map/ppermute | solution.py:61
  37.6 7.7 %collective-permute-start.7 = (bf16[128,768]{1,0:T(8,128)(2,1)S(1)}, bf16[128,768]{1,0:T(8,128)(2,1)S(1)}, u32[]{:S(2)}, u32[]{:S(2)}) collective-permute-start(bf16[128,768]{1,0:T(8,128)(2,1)S(1)} %slice.15), channel_id=1, source_target_pairs={{0,12},{4,0},{8,4},{12,8},{1,13},{5,1},{9,5},{13,9},{2,14},{6,2},{... | collective-permute-start | bytes 589832 | tf_op jit(solution)/shard_map/ppermute | solution.py:61
  40.3 9.3 %collective-permute-start.4 = (bf16[128,768]{1,0:T(8,128)(2,1)S(1)}, bf16[128,768]{1,0:T(8,128)(2,1)S(1)}, u32[]{:S(2)}, u32[]{:S(2)}) collective-permute-start(bf16[128,768]{1,0:T(8,128)(2,1)S(1)} %slice.12), channel_id=1, source_target_pairs={{0,4},{4,8},{8,12},{12,0},{1,5},{5,9},{9,13},{13,1},{2,6},{6,10},{... | collective-permute-start | bytes 589832 | tf_op jit(solution)/shard_map/ppermute | solution.py:61
  40.3 9.3 %collective-permute-start.5 = (bf16[128,768]{1,0:T(8,128)(2,1)S(1)}, bf16[128,768]{1,0:T(8,128)(2,1)S(1)}, u32[]{:S(2)}, u32[]{:S(2)}) collective-permute-start(bf16[128,768]{1,0:T(8,128)(2,1)S(1)} %slice.13), channel_id=1, source_target_pairs={{0,12},{4,0},{8,4},{12,8},{1,13},{5,1},{9,5},{13,9},{2,14},{6,2},{... | collective-permute-start | bytes 589832 | tf_op jit(solution)/shard_map/ppermute | solution.py:61
  58.9 11.3 %collective-permute-start.9 = (bf16[256,768]{1,0:T(8,128)(2,1)}, bf16[256,768]{1,0:T(8,128)(2,1)S(1)}, u32[]{:S(2)}, u32[]{:S(2)}) collective-permute-start(bf16[256,768]{1,0:T(8,128)(2,1)} %get-tuple-element.39), channel_id=1, source_target_pairs={{0,4},{4,8},{8,12},{12,0},{1,5},{5,9},{9,13},{13,1},{2,6},{6,10},{... | collective-permute-start | bytes 1179656 | tf_op jit(solution)/shard_map/ppermute | solution.py:61
  59.0 11.2 %collective-permute-start.10 = (bf16[256,768]{1,0:T(8,128)(2,1)}, bf16[256,768]{1,0:T(8,128)(2,1)S(1)}, u32[]{:S(2)}, u32[]{:S(2)}) collective-permute-start(bf16[256,768]{1,0:T(8,128)(2,1)} %get-tuple-element.40), channel_id=1, source_target_pairs={{0,12},{4,0},{8,4},{12,8},{1,13},{5,1},{9,5},{13,9},{2,14},{6,2},{... | collective-permute-start | bytes 1179656 | tf_op jit(solution)/shard_map/ppermute | solution.py:61
  61.7 8.6 %copy-start.9 = (bf16[256,768]{1,0:T(8,128)(2,1)S(1)}, bf16[256,768]{1,0:T(8,128)(2,1)}, u32[]{:S(2)}) copy-start(bf16[256,768]{1,0:T(8,128)(2,1)} %get-tuple-element.42.mine) | copy-start | bytes 1179652
  61.7 18.2 %all-to-all-start.2 = ((bf16[8,384,128]{2,1,0:T(8,128)(2,1)}), bf16[8,384,128]{2,1,0:T(8,128)(2,1)S(1)}, u32[]{:S(2)}, u32[]{:S(2)}) async-start(bf16[8,384,128]{2,1,0:T(8,128)(2,1)} %get-tuple-element.35), calls=%async_computation.2 | async-start | bytes 1572864 | tf_op jit(solution)/shard_map/all_to_all | solution.py:411
  67.6 18.2 %collective-permute-start.8 = (bf16[256,768]{1,0:T(8,128)(2,1)}, bf16[256,768]{1,0:T(8,128)(2,1)S(1)}, u32[]{:S(2)}, u32[]{:S(2)}) collective-permute-start(bf16[256,768]{1,0:T(8,128)(2,1)} %get-tuple-element.37), channel_id=1, source_target_pairs={{0,12},{4,0},{8,4},{12,8},{1,13},{5,1},{9,5},{13,9},{2,14},{6,2},{... | collective-permute-start | bytes 1179656 | tf_op jit(solution)/shard_map/ppermute | solution.py:61
  69.0 16.8 %collective-permute-start.13 = (bf16[256,768]{1,0:T(8,128)(2,1)S(1)}, bf16[256,768]{1,0:T(8,128)(2,1)S(1)}, u32[]{:S(2)}, u32[]{:S(2)}) collective-permute-start(bf16[256,768]{1,0:T(8,128)(2,1)S(1)} %copy-done.15), channel_id=1, source_target_pairs={{0,4},{4,8},{8,12},{12,0},{1,5},{5,9},{9,13},{13,1},{2,6},{6,10},{... | collective-permute-start | bytes 1179656 | tf_op jit(solution)/shard_map/ppermute | solution.py:61
  71.1 15.9 %collective-permute-start.12 = (bf16[256,768]{1,0:T(8,128)(2,1)}, bf16[256,768]{1,0:T(8,128)(2,1)S(1)}, u32[]{:S(2)}, u32[]{:S(2)}) collective-permute-start(bf16[256,768]{1,0:T(8,128)(2,1)} %shard_map.171), channel_id=1, source_target_pairs={{0,12},{4,0},{8,4},{12,8},{1,13},{5,1},{9,5},{13,9},{2,14},{6,2},{... | collective-permute-start | bytes 1179656 | tf_op jit(solution)/shard_map/ppermute | solution.py:61
  74.3 14.6 %collective-permute-start.11 = (bf16[256,768]{1,0:T(8,128)(2,1)}, bf16[256,768]{1,0:T(8,128)(2,1)S(1)}, u32[]{:S(2)}, u32[]{:S(2)}) collective-permute-start(bf16[256,768]{1,0:T(8,128)(2,1)} %shard_map.170), channel_id=1, source_target_pairs={{0,4},{4,8},{8,12},{12,0},{1,5},{5,9},{9,13},{13,1},{2,6},{6,10},{... | collective-permute-start | bytes 1179656 | tf_op jit(solution)/shard_map/ppermute | solution.py:61
  81.0 14.2 %all-to-all-start.3 = ((bf16[32,24,128]{2,1,0:T(8,128)(2,1)}), bf16[32,24,128]{2,1,0:T(8,128)(2,1)S(1)}, u32[]{:S(2)}, u32[]{:S(2)}) async-start(bf16[32,24,128]{2,1,0:T(8,128)(2,1)} %shard_map.168), calls=%async_computation.3 | async-start | bytes 393216 | tf_op jit(solution)/shard_map/all_to_all | solution.py:429
  (13 other events, 56.5 us)

commit v6 on v5

--- a/solution.py
+++ b/solution.py
@@ -269,9 +269,9 @@
             at = 288 + j * 16
             point_s[p * 16:(p + 1) * 16, j * TAKE:(j + 1) * TAKE] = slab[p, at:at + 16, :]
     point_w[...] = dot(to_h[...], point_s[...], 1, 0).astype(BF16)
-    for copy in copies[3:8]:
-        copy.wait()
-    for r in range(NX):
+    for r, arrived in ((0, copies[3:4]), (1, copies[4:5]), (3, copies[5:6]), (2, copies[6:8])):
+        for copy in arrived:
+            copy.wait()
         taps_s[r] = dot(acts[r], conv_w[...], 1, 0)
     for copy in copies[8:13]:
         copy.wait()
@@ -330,6 +330,7 @@
                 grads[p, t * 96 + g * 48:t * 96 + g * 48 + 48, :] = rows[
                     p * 48:(p + 1) * 48, t * TAKE:(t + 1) * TAKE
                 ]
+    sent.extend(fetch((grads.at[:, :288],), (grads_far.at[:, :288],), out_sems, 8))
     total = dot(inner_act[0], cts[0], 0, 0)
     for r in range(1, NX):
         total = total + dot(inner_act[r], cts[r], 0, 0)
@@ -339,7 +340,7 @@
             grads[p, 288 + j * 16:304 + j * 16, :] = rows[
                 p * 16:(p + 1) * 16, j * TAKE:(j + 1) * TAKE
             ]
-    sent.extend(fetch((grads,), (grads_far,), out_sems, 8))
+    sent.extend(fetch((grads.at[:, 288:],), (grads_far.at[:, 288:],), out_sems, 9))
     for copy in sent:
         copy.wait()
 
@@ -397,7 +398,7 @@
             pltpu.VMEM((NX, ROWS, TAKE), BF16),
             pltpu.VMEM((D, 3 * TAKE), BF16),
             pltpu.SemaphoreType.DMA((15,)),
-            pltpu.SemaphoreType.DMA((9,)),
+            pltpu.SemaphoreType.DMA((10,)),
         ],
         flops=5 * 10**9,
         moved=12 * 2**20,

time: 96.9 us -> 97.2 us (level)
  no operation moved by 1% of the time
where the time goes in v6:
time: 97.2 us; the launch traced here: 96.4 us
  starting transfers between devices  36.3 us (37%)
  waiting for transfers between devices  21.6 us (22%)
  blocking collectives  18.7 us (19%)
  Pallas kernels  17.3 us (18%)
  local copies, waits for them, and re-layouts  1.61 us (2%)
    all_to_all x1, blocking collectives, shards(): line = lax.all_to_all(own, SHEET, 0, 0)  18.7 us
    ppermute x14, starting transfers between devices, step_along_x(): return lax.ppermute(value, 'x', [(i, (i + step) % NX) for i in range(NX)])  18.2 us
    pallas_call x9, Pallas kernels, call(): pl.pallas_call(body, out_shape=out_shapes, in_specs=[vmem] * (len(operand...  17.3 us
    ppermute x14, waiting for transfers between devices, step_along_x(): return lax.ppermute(value, 'x', [(i, (i + step) % NX) for i in range(NX)])  10.8 us
    all_to_all x1, starting transfers between devices, shards(): slab = lax.all_to_all(blocks, SLAB, 0, 0)  7.84 us
    all_to_all x1, starting transfers between devices, shards(): slab_g = lax.all_to_all(grads, SLAB, 0, 0)  5.93 us
    all_to_all x1, waiting for transfers between devices, shards(): slab_g = lax.all_to_all(grads, SLAB, 0, 0)  5.58 us
    all_to_all x1, waiting for transfers between devices, shards(): line_g = lax.all_to_all(line_g, SHEET, 0, 0)  5.13 us
  transfers between devices with their start and end apart: 17, of which 8 were waited for; matrix products, arithmetic and copies ran while one was open for 0% of the time, Pallas kernels for 7%

profile of v6, /device:TPU:1, one launch (start us, length us, event | category | flops | bytes accessed | tf_op | source)
XLA Modules:
  0.0 96.4 jit_solution(9329992438654093855)
XLA Ops:
  0.6 2.1 %collective-permute-start.3 = (bf16[256,768]{1,0:T(8,128)(2,1)}, bf16[256,768]{1,0:T(8,128)(2,1)S(1)}, u32[]{:S(2)}, u32[]{:S(2)}) collective-permute-start(bf16[256,768]{1,0:T(8,128)(2,1)} %bitcast.6), channel_id=1, source_target_pairs={{0,4},{4,8},{8,12},{12,0},{1,5},{5,9},{9,13},{13,1},{2,6},{6,10},{... | collective-permute-start | bytes 1179656 | tf_op jit(solution)/shard_map/ppermute | solution.py:61
  2.7 1.4 %collective-permute-start.2 = (bf16[256,768]{1,0:T(8,128)(2,1)}, bf16[256,768]{1,0:T(8,128)(2,1)S(1)}, u32[]{:S(2)}, u32[]{:S(2)}) collective-permute-start(bf16[256,768]{1,0:T(8,128)(2,1)} %bitcast.7), channel_id=1, source_target_pairs={{0,12},{4,0},{8,4},{12,8},{1,13},{5,1},{9,5},{13,9},{2,14},{6,2},{... | collective-permute-start | bytes 1179656 | tf_op jit(solution)/shard_map/ppermute | solution.py:61
  4.1 2.5 %shard_map.165 = (bf16[32,24,128]{2,1,0:T(8,128)(2,1)}, bf16[256,768]{1,0:T(8,128)(2,1)}) custom-call(bf16[3,3,512]{2,1,0:T(4,128)(2,1)} %w_conv_far.1, bf16[2,768]{1,0:T(2,128)(2,1)} %w_point_far.1, bf16[512,512]{1,0:T(8,128)(2,1)} %constant.16.clone.order_far.order, bf16[1,256,768]{2,1,0:T(8,128)(2,1)} %tokens_far.1), custom_call_target="tpu_custom_call" | custom-call | flops 10000000 | bytes 2097152 | tf_op jit(solution)/shard_map/pallas_call | solution.py:89
  6.8 2.6 %collective-permute-start = (bf16[256,768]{1,0:T(8,128)(2,1)}, bf16[256,768]{1,0:T(8,128)(2,1)S(1)}, u32[]{:S(2)}, u32[]{:S(2)}) collective-permute-start(bf16[256,768]{1,0:T(8,128)(2,1)} %get-tuple-element.29.refs_0_), channel_id=1, source_target_pairs={{0,12},{4,0},{8,4},{12,8},{1,13},{5,1},{9,5},{13,9},{2,14},{6,2},{... | collective-permute-start | bytes 1179656 | tf_op jit(solution)/shard_map/ppermute | solution.py:61
  9.4 18.7 %all_to_all.20.line = bf16[32,24,128]{2,1,0:T(8,128)(2,1)S(1)} all-to-all(bf16[32,24,128]{2,1,0:T(8,128)(2,1)} %get-tuple-element.28), channel_id=1, replica_groups=mesh['z'=8,'yh'=2,'x'=4,'yl'=2,'core'=2] {'z','x'}, dimensions={0} | all-to-all | bytes 393216 | tf_op jit(solution)/shard_map/all_to_all | solution.py:366
  28.2 1.3 %shard_map.166 = bf16[8,384,128]{2,1,0:T(8,128)(2,1)} custom-call(bf16[32,24,128]{2,1,0:T(8,128)(2,1)S(1)} %all_to_all.20.line, bf16[144,384]{1,0:T(8,128)(2,1)S(1)} %copy-done.6, bf16[96,192]{1,0:T(8,128)(2,1)S(1)} %copy-done.7), custom_call_target="tpu_custom_call" | custom-call | flops 20000000000 | bytes 1048576 | tf_op jit(solution)/shard_map/pallas_call | solution.py:89
  29.6 7.8 %all-to-all-start.1 = ((bf16[8,384,128]{2,1,0:T(8,128)(2,1)}), bf16[8,384,128]{2,1,0:T(8,128)(2,1)S(1)}, u32[]{:S(2)}, u32[]{:S(2)}) async-start(bf16[8,384,128]{2,1,0:T(8,128)(2,1)} %shard_map.166), calls=%async_computation.1 | async-start | bytes 1572864 | tf_op jit(solution)/shard_map/all_to_all | solution.py:382
  37.6 2.7 %collective-permute-start.7 = (bf16[128,768]{1,0:T(8,128)(2,1)S(1)}, bf16[128,768]{1,0:T(8,128)(2,1)S(1)}, u32[]{:S(2)}, u32[]{:S(2)}) collective-permute-start(bf16[128,768]{1,0:T(8,128)(2,1)S(1)} %slice.15), channel_id=1, source_target_pairs={{0,12},{4,0},{8,4},{12,8},{1,13},{5,1},{9,5},{13,9},{2,14},{6,2},{... | collective-permute-start | bytes 589832 | tf_op jit(solution)/shard_map/ppermute | solution.py:61
  40.3 2.7 %collective-permute-start.5 = (bf16[128,768]{1,0:T(8,128)(2,1)S(1)}, bf16[128,768]{1,0:T(8,128)(2,1)S(1)}, u32[]{:S(2)}, u32[]{:S(2)}) collective-permute-start(bf16[128,768]{1,0:T(8,128)(2,1)S(1)} %slice.13), channel_id=1, source_target_pairs={{0,12},{4,0},{8,4},{12,8},{1,13},{5,1},{9,5},{13,9},{2,14},{6,2},{... | collective-permute-start | bytes 589832 | tf_op jit(solution)/shard_map/ppermute | solution.py:61
  43.0 2.4 %collective-permute-done.6.refs_8_ = bf16[128,768]{1,0:T(8,128)(2,1)S(1)} collective-permute-done((bf16[128,768]{1,0:T(8,128)(2,1)S(1)}, bf16[128,768]{1,0:T(8,128)(2,1)S(1)}, u32[]{:S(2)}, u32[]{:S(2)}) %collective-permute-start.6) | collective-permute-done | bytes 196640 | tf_op jit(solution)/shard_map/ppermute | solution.py:61
  45.3 4.2 %collective-permute-done.4.refs_3_ = bf16[128,768]{1,0:T(8,128)(2,1)S(1)} collective-permute-done((bf16[128,768]{1,0:T(8,128)(2,1)S(1)}, bf16[128,768]{1,0:T(8,128)(2,1)S(1)}, u32[]{:S(2)}, u32[]{:S(2)}) %collective-permute-start.4) | collective-permute-done | bytes 196640 | tf_op jit(solution)/shard_map/ppermute | solution.py:61
  51.2 8.0 %shard_map.167 = (bf16[8,384,128]{2,1,0:T(8,128)(2,1)}, bf16[2,256,768]{2,1,0:T(8,128)(2,1)}, bf16[256,768]{1,0:T(8,128)(2,1)}, bf16[256,768]{1,0:T(8,128)(2,1)}...) custom-call(bf16[8,384,128]{2,1,0:T(8,128)(2,1)} %copy-done.10, ...), custom_call_target="tpu_custom_call" | custom-call | flops 5000000000 | bytes 12582912 | tf_op jit(solution)/shard_map/pallas_call | solution.py:89
  59.3 2.7 %collective-permute-start.10 = (bf16[256,768]{1,0:T(8,128)(2,1)}, bf16[256,768]{1,0:T(8,128)(2,1)S(1)}, u32[]{:S(2)}, u32[]{:S(2)}) collective-permute-start(bf16[256,768]{1,0:T(8,128)(2,1)} %get-tuple-element.40), channel_id=1, source_target_pairs={{0,12},{4,0},{8,4},{12,8},{1,13},{5,1},{9,5},{13,9},{2,14},{6,2},{... | collective-permute-start | bytes 1179656 | tf_op jit(solution)/shard_map/ppermute | solution.py:61
  62.0 5.9 %all-to-all-start.2 = ((bf16[8,384,128]{2,1,0:T(8,128)(2,1)}), bf16[8,384,128]{2,1,0:T(8,128)(2,1)S(1)}, u32[]{:S(2)}, u32[]{:S(2)}) async-start(bf16[8,384,128]{2,1,0:T(8,128)(2,1)} %get-tuple-element.35), calls=%async_computation.2 | async-start | bytes 1572864 | tf_op jit(solution)/shard_map/all_to_all | solution.py:412
  67.9 1.4 %collective-permute-start.8 = (bf16[256,768]{1,0:T(8,128)(2,1)}, bf16[256,768]{1,0:T(8,128)(2,1)S(1)}, u32[]{:S(2)}, u32[]{:S(2)}) collective-permute-start(bf16[256,768]{1,0:T(8,128)(2,1)} %get-tuple-element.37), channel_id=1, source_target_pairs={{0,12},{4,0},{8,4},{12,8},{1,13},{5,1},{9,5},{13,9},{2,14},{6,2},{... | collective-permute-start | bytes 1179656 | tf_op jit(solution)/shard_map/ppermute | solution.py:61
  69.4 1.2 %collective-permute-done.9.other = bf16[256,768]{1,0:T(8,128)(2,1)S(1)} collective-permute-done((bf16[256,768]{1,0:T(8,128)(2,1)}, bf16[256,768]{1,0:T(8,128)(2,1)S(1)}, u32[]{:S(2)}, u32[]{:S(2)}) %collective-permute-start.9) | collective-permute-done | bytes 393248 | tf_op jit(solution)/shard_map/ppermute | solution.py:61
  71.4 2.4 %collective-permute-start.12 = (bf16[256,768]{1,0:T(8,128)(2,1)}, bf16[256,768]{1,0:T(8,128)(2,1)S(1)}, u32[]{:S(2)}, u32[]{:S(2)}) collective-permute-start(bf16[256,768]{1,0:T(8,128)(2,1)} %shard_map.171), channel_id=1, source_target_pairs={{0,12},{4,0},{8,4},{12,8},{1,13},{5,1},{9,5},{13,9},{2,14},{6,2},{... | collective-permute-start | bytes 1179656 | tf_op jit(solution)/shard_map/ppermute | solution.py:61
  74.6 5.6 %all-to-all-done.2.slab = bf16[8,384,128]{2,1,0:T(8,128)(2,1)S(1)} async-done(((bf16[8,384,128]{2,1,0:T(8,128)(2,1)}), bf16[8,384,128]{2,1,0:T(8,128)(2,1)S(1)}, u32[]{:S(2)}, u32[]{:S(2)}) %all-to-all-start.2) | async-done | bytes 786464 | tf_op jit(solution)/shard_map/all_to_all | solution.py:412
  80.2 1.1 %shard_map.168 = bf16[32,24,128]{2,1,0:T(8,128)(2,1)} custom-call(bf16[8,384,128]{2,1,0:T(8,128)(2,1)S(1)} %all-to-all-done.2.slab, bf16[384,144]{1,0:T(8,128)(2,1)S(1)} %copy-done.4, bf16[192,96]{1,0:T(8,128)(2,1)S(1)} %copy-done.5), custom_call_target="tpu_custom_call" | custom-call | flops 100000000 | bytes 1048576 | tf_op jit(solution)/shard_map/pallas_call | solution.py:89
  81.3 4.3 %all-to-all-start.3 = ((bf16[32,24,128]{2,1,0:T(8,128)(2,1)}), bf16[32,24,128]{2,1,0:T(8,128)(2,1)S(1)}, u32[]{:S(2)}, u32[]{:S(2)}) async-start(bf16[32,24,128]{2,1,0:T(8,128)(2,1)} %shard_map.168), calls=%async_computation.3 | async-start | bytes 393216 | tf_op jit(solution)/shard_map/all_to_all | solution.py:430
  86.1 1.2 %collective-permute-done.12.act_left = bf16[256,768]{1,0:T(8,128)(2,1)S(1)} collective-permute-done((bf16[256,768]{1,0:T(8,128)(2,1)}, bf16[256,768]{1,0:T(8,128)(2,1)S(1)}, u32[]{:S(2)}, u32[]{:S(2)}) %collective-permute-start.12) | collective-permute-done | bytes 393248 | tf_op jit(solution)/shard_map/ppermute | solution.py:61
  87.3 1.8 %collective-permute-done.11.out_right = bf16[256,768]{1,0:T(8,128)(2,1)S(1)} collective-permute-done((bf16[256,768]{1,0:T(8,128)(2,1)}, bf16[256,768]{1,0:T(8,128)(2,1)S(1)}, u32[]{:S(2)}, u32[]{:S(2)}) %collective-permute-start.11) | collective-permute-done | bytes 393248 | tf_op jit(solution)/shard_map/ppermute | solution.py:61
  89.1 1.2 %shard_map.172 = (bf16[256,768]{1,0:T(8,128)(2,1)}, bf16[256,768]{1,0:T(8,128)(2,1)}) custom-call(bf16[256,768]{1,0:T(8,128)(2,1)S(1)} %bitcast.5, bf16[256,768]{1,0:T(8,128)(2,1)S(1)} %bitcast.9, f32[256,768]{1,0:T(8,128)S(1)} %shard_map.169.slope, bf16[2,256,768]{2,1,0:T(8,128)(2,1)S(1)} %copy-done.2, ...), custom_call_target="tpu_custom_call" | custom-call | flops 10000000 | bytes 4194304 | tf_op jit(solution)/shard_map/pallas_call | solution.py:89
  90.4 5.1 %all-to-all-done.3.line = bf16[32,24,128]{2,1,0:T(8,128)(2,1)S(1)} async-done(((bf16[32,24,128]{2,1,0:T(8,128)(2,1)}), bf16[32,24,128]{2,1,0:T(8,128)(2,1)S(1)}, u32[]{:S(2)}, u32[]{:S(2)}) %all-to-all-start.3) | async-done | bytes 196640 | tf_op jit(solution)/shard_map/all_to_all | solution.py:430
  (64 shorter events, 5.2 us)
Async XLA Ops:
  0.6 27.5 %collective-permute-start.3 = (bf16[256,768]{1,0:T(8,128)(2,1)}, bf16[256,768]{1,0:T(8,128)(2,1)S(1)}, u32[]{:S(2)}, u32[]{:S(2)}) collective-permute-start(bf16[256,768]{1,0:T(8,128)(2,1)} %bitcast.6), channel_id=1, source_target_pairs={{0,4},{4,8},{8,12},{12,0},{1,5},{5,9},{9,13},{13,1},{2,6},{6,10},{... | collective-permute-start | bytes 1179656 | tf_op jit(solution)/shard_map/ppermute | solution.py:61
  2.7 25.4 %collective-permute-start.2 = (bf16[256,768]{1,0:T(8,128)(2,1)}, bf16[256,768]{1,0:T(8,128)(2,1)S(1)}, u32[]{:S(2)}, u32[]{:S(2)}) collective-permute-start(bf16[256,768]{1,0:T(8,128)(2,1)} %bitcast.7), channel_id=1, source_target_pairs={{0,12},{4,0},{8,4},{12,8},{1,13},{5,1},{9,5},{13,9},{2,14},{6,2},{... | collective-permute-start | bytes 1179656 | tf_op jit(solution)/shard_map/ppermute | solution.py:61
  6.7 21.5 %collective-permute-start.1 = (bf16[256,768]{1,0:T(8,128)(2,1)}, bf16[256,768]{1,0:T(8,128)(2,1)S(1)}, u32[]{:S(2)}, u32[]{:S(2)}) collective-permute-start(bf16[256,768]{1,0:T(8,128)(2,1)} %get-tuple-element.29.refs_0_), channel_id=1, source_target_pairs={{0,4},{4,8},{8,12},{12,0},{1,5},{5,9},{9,13},{13,1},{2,6},{6,10},{... | collective-permute-start | bytes 1179656 | tf_op jit(solution)/shard_map/ppermute | solution.py:61
  6.8 21.3 %collective-permute-start = (bf16[256,768]{1,0:T(8,128)(2,1)}, bf16[256,768]{1,0:T(8,128)(2,1)S(1)}, u32[]{:S(2)}, u32[]{:S(2)}) collective-permute-start(bf16[256,768]{1,0:T(8,128)(2,1)} %get-tuple-element.29.refs_0_), channel_id=1, source_target_pairs={{0,12},{4,0},{8,4},{12,8},{1,13},{5,1},{9,5},{13,9},{2,14},{6,2},{... | collective-permute-start | bytes 1179656 | tf_op jit(solution)/shard_map/ppermute | solution.py:61
  9.4 18.8 %copy-start.6 = (bf16[144,384]{1,0:T(8,128)(2,1)S(1)}, bf16[144,384]{1,0:T(8,128)(2,1)}, u32[]{:S(2)}) copy-start(bf16[144,384]{1,0:T(8,128)(2,1)} %constant.17.clone.conv_order) | copy-start | bytes 331780
  9.4 18.8 %copy-start.7 = (bf16[96,192]{1,0:T(8,128)(2,1)S(1)}, bf16[96,192]{1,0:T(8,128)(2,1)}, u32[]{:S(2)}) copy-start(bf16[96,192]{1,0:T(8,128)(2,1)} %constant.18.clone.point_order) | copy-start | bytes 110596
  28.1 9.3 %copy-start.11 = (bf16[256,768]{1,0:T(8,128)(2,1)}, bf16[256,768]{1,0:T(8,128)(2,1)S(1)}, u32[]{:S(2)}) copy-start(bf16[256,768]{1,0:T(8,128)(2,1)S(1)} %collective-permute-done.3.refs_7_) | copy-start | bytes 1179652
  28.2 9.3 %copy-start.12 = (bf16[256,768]{1,0:T(8,128)(2,1)}, bf16[256,768]{1,0:T(8,128)(2,1)S(1)}, u32[]{:S(2)}) copy-start(bf16[256,768]{1,0:T(8,128)(2,1)S(1)} %collective-permute-done.2.refs_6_) | copy-start | bytes 1179652
  28.2 9.3 %copy-start.13 = (bf16[256,768]{1,0:T(8,128)(2,1)}, bf16[256,768]{1,0:T(8,128)(2,1)S(1)}, u32[]{:S(2)}) copy-start(bf16[256,768]{1,0:T(8,128)(2,1)S(1)} %collective-permute-done.1.refs_2_) | copy-start | bytes 1179652
  28.2 9.2 %copy-start.14 = (bf16[256,768]{1,0:T(8,128)(2,1)}, bf16[256,768]{1,0:T(8,128)(2,1)S(1)}, u32[]{:S(2)}) copy-start(bf16[256,768]{1,0:T(8,128)(2,1)S(1)} %collective-permute-done.refs_1_) | copy-start | bytes 1179652
  29.6 20.1 %all-to-all-start.1 = ((bf16[8,384,128]{2,1,0:T(8,128)(2,1)}), bf16[8,384,128]{2,1,0:T(8,128)(2,1)S(1)}, u32[]{:S(2)}, u32[]{:S(2)}) async-start(bf16[8,384,128]{2,1,0:T(8,128)(2,1)} %shard_map.166), calls=%async_computation.1 | async-start | bytes 1572864 | tf_op jit(solution)/shard_map/all_to_all | solution.py:382
  37.5 7.8 %collective-permute-start.6 = (bf16[128,768]{1,0:T(8,128)(2,1)S(1)}, bf16[128,768]{1,0:T(8,128)(2,1)S(1)}, u32[]{:S(2)}, u32[]{:S(2)}) collective-permute-start(bf16[128,768]{1,0:T(8,128)(2,1)S(1)} %slice.14), channel_id=1, source_target_pairs={{0,4},{4,8},{8,12},{12,0},{1,5},{5,9},{9,13},{13,1},{2,6},{6,10},{... | collective-permute-start | bytes 589832 | tf_op jit(solution)/shard_map/ppermute | solution.py:61
  37.6 7.7 %collective-permute-start.7 = (bf16[128,768]{1,0:T(8,128)(2,1)S(1)}, bf16[128,768]{1,0:T(8,128)(2,1)S(1)}, u32[]{:S(2)}, u32[]{:S(2)}) collective-permute-start(bf16[128,768]{1,0:T(8,128)(2,1)S(1)} %slice.15), channel_id=1, source_target_pairs={{0,12},{4,0},{8,4},{12,8},{1,13},{5,1},{9,5},{13,9},{2,14},{6,2},{... | collective-permute-start | bytes 589832 | tf_op jit(solution)/shard_map/ppermute | solution.py:61
  40.3 9.3 %collective-permute-start.4 = (bf16[128,768]{1,0:T(8,128)(2,1)S(1)}, bf16[128,768]{1,0:T(8,128)(2,1)S(1)}, u32[]{:S(2)}, u32[]{:S(2)}) collective-permute-start(bf16[128,768]{1,0:T(8,128)(2,1)S(1)} %slice.12), channel_id=1, source_target_pairs={{0,4},{4,8},{8,12},{12,0},{1,5},{5,9},{9,13},{13,1},{2,6},{6,10},{... | collective-permute-start | bytes 589832 | tf_op jit(solution)/shard_map/ppermute | solution.py:61
  40.3 9.3 %collective-permute-start.5 = (bf16[128,768]{1,0:T(8,128)(2,1)S(1)}, bf16[128,768]{1,0:T(8,128)(2,1)S(1)}, u32[]{:S(2)}, u32[]{:S(2)}) collective-permute-start(bf16[128,768]{1,0:T(8,128)(2,1)S(1)} %slice.13), channel_id=1, source_target_pairs={{0,12},{4,0},{8,4},{12,8},{1,13},{5,1},{9,5},{13,9},{2,14},{6,2},{... | collective-permute-start | bytes 589832 | tf_op jit(solution)/shard_map/ppermute | solution.py:61
  59.2 11.3 %collective-permute-start.9 = (bf16[256,768]{1,0:T(8,128)(2,1)}, bf16[256,768]{1,0:T(8,128)(2,1)S(1)}, u32[]{:S(2)}, u32[]{:S(2)}) collective-permute-start(bf16[256,768]{1,0:T(8,128)(2,1)} %get-tuple-element.39), channel_id=1, source_target_pairs={{0,4},{4,8},{8,12},{12,0},{1,5},{5,9},{9,13},{13,1},{2,6},{6,10},{... | collective-permute-start | bytes 1179656 | tf_op jit(solution)/shard_map/ppermute | solution.py:61
  59.3 11.3 %collective-permute-start.10 = (bf16[256,768]{1,0:T(8,128)(2,1)}, bf16[256,768]{1,0:T(8,128)(2,1)S(1)}, u32[]{:S(2)}, u32[]{:S(2)}) collective-permute-start(bf16[256,768]{1,0:T(8,128)(2,1)} %get-tuple-element.40), channel_id=1, source_target_pairs={{0,12},{4,0},{8,4},{12,8},{1,13},{5,1},{9,5},{13,9},{2,14},{6,2},{... | collective-permute-start | bytes 1179656 | tf_op jit(solution)/shard_map/ppermute | solution.py:61
  62.0 8.6 %copy-start.9 = (bf16[256,768]{1,0:T(8,128)(2,1)S(1)}, bf16[256,768]{1,0:T(8,128)(2,1)}, u32[]{:S(2)}) copy-start(bf16[256,768]{1,0:T(8,128)(2,1)} %get-tuple-element.42.mine) | copy-start | bytes 1179652
  62.0 18.2 %all-to-all-start.2 = ((bf16[8,384,128]{2,1,0:T(8,128)(2,1)}), bf16[8,384,128]{2,1,0:T(8,128)(2,1)S(1)}, u32[]{:S(2)}, u32[]{:S(2)}) async-start(bf16[8,384,128]{2,1,0:T(8,128)(2,1)} %get-tuple-element.35), calls=%async_computation.2 | async-start | bytes 1572864 | tf_op jit(solution)/shard_map/all_to_all | solution.py:412
  67.9 18.2 %collective-permute-start.8 = (bf16[256,768]{1,0:T(8,128)(2,1)}, bf16[256,768]{1,0:T(8,128)(2,1)S(1)}, u32[]{:S(2)}, u32[]{:S(2)}) collective-permute-start(bf16[256,768]{1,0:T(8,128)(2,1)} %get-tuple-element.37), channel_id=1, source_target_pairs={{0,12},{4,0},{8,4},{12,8},{1,13},{5,1},{9,5},{13,9},{2,14},{6,2},{... | collective-permute-start | bytes 1179656 | tf_op jit(solution)/shard_map/ppermute | solution.py:61
  69.3 16.8 %collective-permute-start.13 = (bf16[256,768]{1,0:T(8,128)(2,1)S(1)}, bf16[256,768]{1,0:T(8,128)(2,1)S(1)}, u32[]{:S(2)}, u32[]{:S(2)}) collective-permute-start(bf16[256,768]{1,0:T(8,128)(2,1)S(1)} %copy-done.15), channel_id=1, source_target_pairs={{0,4},{4,8},{8,12},{12,0},{1,5},{5,9},{9,13},{13,1},{2,6},{6,10},{... | collective-permute-start | bytes 1179656 | tf_op jit(solution)/shard_map/ppermute | solution.py:61
  71.4 15.9 %collective-permute-start.12 = (bf16[256,768]{1,0:T(8,128)(2,1)}, bf16[256,768]{1,0:T(8,128)(2,1)S(1)}, u32[]{:S(2)}, u32[]{:S(2)}) collective-permute-start(bf16[256,768]{1,0:T(8,128)(2,1)} %shard_map.171), channel_id=1, source_target_pairs={{0,12},{4,0},{8,4},{12,8},{1,13},{5,1},{9,5},{13,9},{2,14},{6,2},{... | collective-permute-start | bytes 1179656 | tf_op jit(solution)/shard_map/ppermute | solution.py:61
  74.6 14.5 %collective-permute-start.11 = (bf16[256,768]{1,0:T(8,128)(2,1)}, bf16[256,768]{1,0:T(8,128)(2,1)S(1)}, u32[]{:S(2)}, u32[]{:S(2)}) collective-permute-start(bf16[256,768]{1,0:T(8,128)(2,1)} %shard_map.170), channel_id=1, source_target_pairs={{0,4},{4,8},{8,12},{12,0},{1,5},{5,9},{9,13},{13,1},{2,6},{6,10},{... | collective-permute-start | bytes 1179656 | tf_op jit(solution)/shard_map/ppermute | solution.py:61
  81.3 14.2 %all-to-all-start.3 = ((bf16[32,24,128]{2,1,0:T(8,128)(2,1)}), bf16[32,24,128]{2,1,0:T(8,128)(2,1)S(1)}, u32[]{:S(2)}, u32[]{:S(2)}) async-start(bf16[32,24,128]{2,1,0:T(8,128)(2,1)} %shard_map.168), calls=%async_computation.3 | async-start | bytes 393216 | tf_op jit(solution)/shard_map/all_to_all | solution.py:430
  (13 other events, 56.4 us)
